TPU v7x, 128 devices: a whole 4x4x4 slice. The times are simulated.
128 devices in a mesh: req: 4 (over y), exp: 32 (over z, x, core).
Axes of the slice: x: 4, y: 4, z: 4, core: 2. Of those that a mesh axis runs over, the one named last changes fastest.
Arguments:
- cand_emb: bfloat16 [32768, 1024], P(('req', 'exp')), may hold values from -6 to 6
- cand_request: int32 [32768], P(('req', 'exp')), may hold values from 0 to 1
- hist_blocks: int32 [256], P(('req', 'exp')), may hold values from 1 to 4
- cache_kv: bfloat16 [1024, 128, 2048], P(('req', 'exp')), may hold values from -20 to 20
- block_map: int32 [1024], P(('req', 'exp')), may hold values from 0 to 3, as said below
- w_query_update: bfloat16 [1024, 2048], replicated, may hold values from -0.1875 to 0.1875
- rel_bias: float32 [8, 4], replicated, may hold values from -4 to 4
- norm_gain: float32 [1024], replicated, may hold values from 0.5 to 1.5
- w_gate: bfloat16 [1024, 192], replicated, may hold values from -0.1875 to 0.1875
- expert_ids: int32 [32768, 2], P(('req', 'exp')), may hold values from 0 to 31, all different within a row; in each aligned block of 256 rows (0 to 255, 256 to 511, ...) at most 32 rows name the same one
- w_up: bfloat16 [32, 1024, 4096], P('exp'), may hold values from -0.1875 to 0.1875
- w_down: bfloat16 [32, 4096, 1024], P('exp'), may hold values from -0.09375 to 0.09375
- w_tower: bfloat16 [1024, 6], replicated, may hold values from -0.1875 to 0.1875
Outputs:
- task_scores: float32 [32768, 6], P(('req', 'exp'))
Inputs may be any that keep to these rules, and one draw needn't show every extreme that they name: `block_map`: for each request, every block number from 0 to 3 is held by exactly one slot, and each owner holds 1 of them. `expert_ids`: among the candidates of one device no expert is chosen more than 32 times.
All inputs are finite; a program needn't handle non-finite values.
Results may differ from a plain program's by a relative error of at most 0.015.
Values may be sent and summed in bfloat16 or wider, within the bound.
No kernel may reach another device: no remote copies, remote signals or barrier semaphores. Data moves between devices by JAX's collectives and lax.ppermute only.
A program may use at most 128 MiB of HBM per device.

v0:
```python
import math

import jax
import jax.numpy as jnp
from jax import lax
from jax.sharding import PartitionSpec as P

EPSILON = 1e-05


def attend(queries, keys_values, key_group, key_block, cand_group, group_blocks, rel_bias):
    row_count, feature = queries.shape
    head_count = rel_bias.shape[0]
    head_dim = feature // head_count
    key_part = keys_values[:, :feature].reshape(-1, head_count, head_dim)
    value_part = keys_values[:, feature:].reshape(-1, head_count, head_dim)
    query_heads = queries.reshape(row_count, head_count, head_dim)
    scores = jnp.einsum("chd,nhd->hcn", query_heads, key_part, preferred_element_type=jnp.float32)
    block_hot = (
        key_block[:, None] == jnp.arange(rel_bias.shape[1], dtype=jnp.int32)[None, :]
    ).astype(jnp.float32)
    block_bias = jnp.sum(rel_bias[:, None, :] * block_hot[None, :, :], axis=2)
    scores = scores * (1.0 / math.sqrt(head_dim)) + block_bias[:, None, :]
    group_hot = cand_group[:, None] == jnp.arange(group_blocks.shape[0], dtype=jnp.int32)[None, :]
    group_len = jnp.sum(jnp.where(group_hot, group_blocks[None, :], 0), axis=1)
    allowed = (cand_group[:, None] == key_group[None, :]) & (
        key_block[None, :] < group_len[:, None]
    )
    weights = jnp.where(allowed[None], jax.nn.silu(scores), 0.0).astype(jnp.bfloat16)
    attended = jnp.einsum("hcn,nhd->chd", weights, value_part, preferred_element_type=jnp.float32)
    return attended.reshape(row_count, feature)


def local(
    cand_emb,
    cand_request,
    hist_blocks,
    cache_kv,
    block_map,
    w_query_update,
    rel_bias,
    norm_gain,
    w_gate,
    expert_ids,
    w_up,
    w_down,
    w_tower,
):
    row_count, feature = cand_emb.shape
    req_size = lax.axis_size("req")
    slot_count = cache_kv.shape[0]
    block_len = cache_kv.shape[1]
    group_slots = slot_count // req_size
    req_local = hist_blocks.shape[0]
    per_group = group_slots // req_local
    projected = jnp.dot(cand_emb, w_query_update, preferred_element_type=jnp.float32)
    queries = projected[:, :feature].astype(jnp.bfloat16)
    update = jax.nn.silu(projected[:, feature:])
    moved_kv, moved_ids = (
        lax.all_to_all(
            cache_kv.reshape(req_size, group_slots, block_len, 2 * feature),
            "req",
            split_axis=0,
            concat_axis=0,
            tiled=True,
        ),
        lax.all_to_all(
            block_map.astype(jnp.bfloat16).reshape(req_size, group_slots),
            "req",
            split_axis=0,
            concat_axis=0,
            tiled=True,
        ),
    )
    owner_slots = jnp.arange(group_slots, dtype=jnp.int32)
    key_group = jnp.repeat(owner_slots // per_group % req_local, block_len)
    attended = jnp.zeros((row_count, feature), jnp.float32)
    for owner in range(req_size):
        key_block = jnp.repeat(moved_ids[owner].astype(jnp.int32), block_len)
        partial_value = attend(
            queries,
            moved_kv[owner].reshape(group_slots * block_len, 2 * feature),
            key_group,
            key_block,
            cand_request,
            hist_blocks,
            rel_bias,
        )
        rounded = lax.optimization_barrier(partial_value.astype(jnp.bfloat16))
        attended = attended + rounded.astype(jnp.float32)
    inv_rms = lax.rsqrt(jnp.mean(attended * attended, axis=1, keepdims=True) + EPSILON)
    mixed_rows = (cand_emb.astype(jnp.float32) + norm_gain * attended * inv_rms * update).astype(
        jnp.bfloat16
    )
    task_count = w_tower.shape[1]
    expert_count = w_gate.shape[1] // task_count
    top_count = expert_ids.shape[1]
    capacity = 2 * row_count * top_count // expert_count
    logits = jnp.dot(mixed_rows, w_gate, preferred_element_type=jnp.float32).reshape(
        row_count, task_count, expert_count
    )
    expert_range = jnp.arange(expert_count, dtype=jnp.int32)
    chosen = (expert_ids[:, :, None] == expert_range[None, None, :]).astype(jnp.float32)
    picked = jnp.sum(logits[:, :, None, :] * chosen[:, None, :, :], axis=3)
    squashed = jax.nn.sigmoid(picked)
    gates = squashed / jnp.sum(squashed, axis=2, keepdims=True)
    flat_ids = expert_ids.reshape(-1)
    route_hot = (flat_ids[:, None] == expert_range[None, :]).astype(jnp.int32)
    position = jnp.sum(jnp.cumsum(route_hot, axis=0) * route_hot, axis=1) - 1
    slot_of = flat_ids * capacity + position
    source = (
        jnp.zeros((expert_count * capacity,), jnp.int32)
        .at[slot_of]
        .set(jnp.arange(flat_ids.shape[0], dtype=jnp.int32) + 1)
    )
    filled = source > 0
    outgoing = jnp.where(
        filled[:, None],
        mixed_rows[jnp.maximum(source - 1, 0) // top_count],
        jnp.zeros((), jnp.bfloat16),
    ).reshape(expert_count, capacity, feature)
    up_matrix = w_up[0]
    down_matrix = w_down[0]
    arrived = lax.all_to_all(outgoing, "exp", split_axis=0, concat_axis=0, tiled=True)
    source_count = arrived.shape[0]
    item_count = arrived.shape[1]
    flat_rows = arrived.reshape(source_count * item_count, feature)
    hidden = jax.nn.silu(jnp.dot(flat_rows, up_matrix, preferred_element_type=jnp.float32)).astype(
        jnp.bfloat16
    )
    produced = jnp.dot(hidden, down_matrix, preferred_element_type=jnp.float32).astype(jnp.bfloat16)
    came_back = lax.all_to_all(
        produced.reshape(source_count, item_count, feature),
        "exp",
        split_axis=0,
        concat_axis=0,
        tiled=True,
    )
    flat_back = came_back.reshape(expert_count * capacity, came_back.shape[2])
    per_route = flat_back[slot_of]
    per_route = jnp.dot(per_route, w_tower, preferred_element_type=jnp.float32)
    per_route = per_route.reshape(row_count, top_count, task_count)
    return jnp.sum(gates * jnp.transpose(per_route, (0, 2, 1)), axis=2)


def solution(mesh):
    placed = (
        P(("req", "exp"), None),
        P(("req", "exp")),
        P(("req", "exp")),
        P(("req", "exp"), None, None),
        P(("req", "exp")),
        P(),
        P(),
        P(),
        P(),
        P(("req", "exp"), None),
        P("exp", None, None),
        P("exp", None, None),
        P(),
    )
    return jax.shard_map(
        local, mesh=mesh, in_specs=placed, out_specs=P(("req", "exp"), None), check_vma=False
    )
```

profile of v0, /device:TPU:1, one launch (start us, length us, event | category | flops | bytes accessed | tf_op | source)
XLA Modules:
  0.0 204.0 jit_solution(10045929903647714881)
XLA Ops:
  0.0 0.7 convert_element_type.141
  0.7 0.7 all_to_all.20
  1.4 5.0 %all-to-all-start = ((bf16[4,1,2]{2,1,0:T(2,128)(2,1)}), bf16[4,1,2]{2,1,0:T(2,128)(2,1)S(1)}, u32[]{:S(2)}, u32[]{:S(2)}) async-start(bf16[4,1,2]{2,1,0:T(2,128)(2,1)} %all_to_all.20), calls=%async_computation | async-start | bytes 4096 | tf_op jit(solution)/shard_map/all_to_all | solution.py:67
  6.4 0.8 copy.88
  7.2 0.1 eq.221
  7.4 0.1 eq.217
  7.5 0.7 broadcast_multiply_fusion
  8.2 11.1 %copy.74 = bf16[4,2,128,2048]{2,1,3,0:T(2,128)(2,1)} copy(bf16[4,2,128,2048]{3,2,1,0:T(8,128)(2,1)} %bitcast.162) | data formatting | bytes 8388608 | tf_op jit(solution)/shard_map/reshape | solution.py:61
  19.3 1.2 reduce-window.6
  20.5 0.2 slice_reduce_fusion
  20.8 0.1 fusion.63
  20.9 0.1 copy.87
  21.0 0.1 mul.168
  21.2 0.5 copy-done.6
  21.7 2.4 %scatter_custom_fusion = s32[1024]{0:T(1024)S(1)} fusion(s32[512]{0:T(512)S(1)} %bitcast.187, s32[512]{0:T(512)S(1)} %iota_add_fusion, s32[]{:T(128)} %constant.68.clone.1), kind=kCustom, calls=%fused_computation.105 | custom fusion | bytes 4100 | tf_op jit(solution)/shard_map/scatter | solution.py:114
  24.2 0.0 copy-start.8
  24.2 0.0 copy-start.11
  24.2 0.0 copy-start.2
  24.2 5.2 %all-to-all-start.1 = ((bf16[4,2,128,2048]{2,1,3,0:T(2,128)(2,1)}), bf16[4,2,128,2048]{2,1,3,0:T(2,128)(2,1)}, u32[]{:S(2)}, u32[]{:S(2)}) async-start(bf16[4,2,128,2048]{2,1,3,0:T(2,128)(2,1)} %copy.74), calls=%async_computation.1 | async-start | bytes 8388608 | tf_op jit(solution)/shard_map/all_to_all | solution.py:60
  29.4 0.1 broadcast_in_dim.148
  29.5 0.1 fusion.72
  29.6 0.1 broadcast_bitcast_fusion.4
  29.7 0.0 copy-start.10
  29.7 4.8 %fusion.99 = f32[256,2048]{1,0:T(8,128)} fusion(bf16[256,1024]{1,0:T(8,128)(2,1)S(1)} %copy-done.2, bf16[1024,2048]{1,0:T(8,128)(2,1)} %param.18), kind=kOutput, calls=%fused_computation.144 | convolution fusion | flops 1073741824 | bytes 6815744 | tf_op jit(solution)/shard_map/dot_general | solution.py:56
  34.6 0.1 broadcast_bitcast_fusion
  34.6 0.1 broadcast_bitcast_fusion.2
  34.7 0.7 multiply_reduce_fusion.5
  35.4 1.0 compare_and_fusion.3
  36.4 41.0 %all-to-all-done.1 = bf16[4,2,128,2048]{2,1,3,0:T(2,128)(2,1)} async-done(((bf16[4,2,128,2048]{2,1,3,0:T(2,128)(2,1)}), bf16[4,2,128,2048]{2,1,3,0:T(2,128)(2,1)}, u32[]{:S(2)}, u32[]{:S(2)}) %all-to-all-start.1) | async-done | bytes 4194336 | tf_op jit(solution)/shard_map/all_to_all | solution.py:60
  77.4 5.2 %fusion.93 = (bf16[1,2,128,2048]{2,1,3,0:T(2,128)(2,1)S(1)}, bf16[1,2,128,2048]{2,1,3,0:T(2,128)(2,1)S(1)}, bf16[1,2,128,2048]{2,1,3,0:T(2,128)(2,1)}, bf16[1,2,128,2048]{2,1,3,0:T(2,128)(2,1)S(1)}) fusion(bf16[4,2,128,2048]{2,1,3,0:T(2,128)(2,1)} %all-to-all-done.1), kind=kLoop, calls=%fused_computation.138 | loop fusion | bytes 8388608 | tf_op jit(solution)/shard_map/slice | solution.py:82
  82.6 0.1 copy.139
  82.7 0.9 fusion.94
  83.6 2.4 %fusion.21 = bf16[8,256,128]{1,2,0:T(8,128)(2,1)S(1)} fusion(bf16[256,8,128]{0,2,1:T(8,128)(2,1)} %bitcast.182, bf16[256,8,128]{0,2,1:T(8,128)(2,1)S(1)} %bitcast.181, f32[8,256]{1,0:T(8,128)} %get-tuple-element.5, pred[256,256]{1,0:T(8,128)(4,1)} %get-tuple-element.21, f32[256,2048]{1,0:T(8,128)} %fusion.99), kind=kOutput, calls=%fused_computation.22 | convolution fusion | flops 272891904 | bytes 2170880 | tf_op jit(solution)/shard_map/hcn,nhd->chd/dot_general | solution.py:30
  86.0 0.2 copy.100
  86.2 0.1 copy.138
  86.4 0.1 fusion.95
  86.4 2.2 %fusion.20 = bf16[8,256,128]{1,2,0:T(8,128)(2,1)S(1)} fusion(bf16[256,8,128]{0,2,1:T(8,128)(2,1)S(1)} %bitcast.184, bf16[256,8,128]{0,2,1:T(8,128)(2,1)S(1)} %bitcast.183, f32[8,256]{1,0:T(8,128)} %get-tuple-element.6, pred[256,256]{1,0:T(8,128)(4,1)} %get-tuple-element.24, f32[256,2048]{1,0:T(8,128)} %fusion.99), kind=kOutput, calls=%fused_computation.21 | convolution fusion | flops 272891904 | bytes 2170880 | tf_op jit(solution)/shard_map/hcn,nhd->chd/dot_general | solution.py:30
  88.7 0.2 copy.101
  88.9 1.4 copy.137
  90.2 0.9 fusion.96
  91.1 2.4 %fusion.19 = bf16[8,256,128]{1,2,0:T(8,128)(2,1)S(1)} fusion(bf16[256,8,128]{0,2,1:T(8,128)(2,1)} %bitcast.186, bf16[256,8,128]{0,2,1:T(8,128)(2,1)S(1)} %bitcast.185, f32[8,256]{1,0:T(8,128)} %get-tuple-element.7, pred[256,256]{1,0:T(8,128)(4,1)} %get-tuple-element.23, f32[256,2048]{1,0:T(8,128)} %fusion.99), kind=kOutput, calls=%fused_computation.20 | convolution fusion | flops 272891904 | bytes 2170880 | tf_op jit(solution)/shard_map/hcn,nhd->chd/dot_general | solution.py:30
  93.5 0.2 copy.102
  93.7 0.1 copy.136
  93.8 0.1 fusion.97
  93.9 2.2 %fusion.18 = bf16[8,256,128]{1,2,0:T(8,128)(2,1)S(1)} fusion(bf16[256,8,128]{0,2,1:T(8,128)(2,1)S(1)} %bitcast.180, bf16[256,8,128]{0,2,1:T(8,128)(2,1)S(1)} %bitcast.179, f32[8,256]{1,0:T(8,128)S(1)} %get-tuple-element.8, pred[256,256]{1,0:T(8,128)(4,1)} %get-tuple-element.22, f32[256,2048]{1,0:T(8,128)} %fusion.99), kind=kOutput, calls=%fused_computation.19 | convolution fusion | flops 272891904 | bytes 2170880 | tf_op jit(solution)/shard_map/hcn,nhd->chd/dot_general | solution.py:30
  96.1 0.0 copy-start.3
  96.1 0.0 copy-start.9
  96.2 0.2 copy.103
  96.4 0.4 multiply_reduce_fusion
  96.8 0.4 copy-done.3
  97.2 0.8 copy-done.1
  98.0 0.7 add_convert_fusion
  98.8 4.1 %gather_fusion = bf16[1024,1024]{1,0:T(8,128)(2,1)S(1)} fusion(bf16[256,1024]{1,0:T(8,128)(2,1)S(1)} %add_convert_fusion, s32[1024]{0:T(1024)S(1)} %fusion.66), kind=kCustom, calls=%fused_computation | custom fusion | bytes 4198400 | tf_op jit(solution)/shard_map/gather | solution.py:119
  102.8 0.2 broadcast_select_fusion
  103.1 38.0 %all_to_all.25 = bf16[32,32,1024]{2,1,0:T(8,128)(2,1)S(1)} all-to-all(bf16[32,32,1024]{2,1,0:T(8,128)(2,1)S(1)} %broadcast_select_fusion), channel_id=1, replica_groups=mesh['req'=4,'exp'=32] {'exp'}, dimensions={0} | all-to-all | bytes 4194304 | tf_op jit(solution)/shard_map/all_to_all | solution.py:124
  141.1 25.6 %fusion.9 = bf16[1024,1024]{1,0:T(8,128)(2,1)} fusion(bf16[1,4096,1024]{2,1,0:T(8,128)(2,1)} %param.24, bf16[1024,1024]{1,0:T(8,128)(2,1)S(1)} %bitcast.172, bf16[1,1024,4096]{2,1,0:T(8,128)(2,1)} %param.23), kind=kOutput, calls=%fused_computation.14 | convolution fusion | flops 17201889280 | bytes 20971520 | tf_op jit(solution)/shard_map/dot_general | solution.py:131
  166.6 4.2 %all-to-all-start.3 = ((bf16[32,32,1024]{2,1,0:T(8,128)(2,1)}), bf16[32,32,1024]{2,1,0:T(8,128)(2,1)S(1)}, u32[]{:S(2)}, u32[]{:S(2)}) async-start(bf16[32,32,1024]{2,1,0:T(8,128)(2,1)} %bitcast.171), calls=%async_computation.3 | async-start | bytes 4194304 | tf_op jit(solution)/shard_map/all_to_all | solution.py:132
  170.9 0.3 fusion.100
  171.2 0.1 multiply_reduce_fusion.1
  171.3 27.5 %all-to-all-done.3 = bf16[32,32,1024]{2,1,0:T(8,128)(2,1)S(1)} async-done(((bf16[32,32,1024]{2,1,0:T(8,128)(2,1)}), bf16[32,32,1024]{2,1,0:T(8,128)(2,1)S(1)}, u32[]{:S(2)}, u32[]{:S(2)}) %all-to-all-start.3) | async-done | bytes 2097184 | tf_op jit(solution)/shard_map/all_to_all | solution.py:132
  198.8 2.8 %gather_fusion.1 = bf16[512,1024]{1,0:T(8,128)(2,1)} fusion(bf16[1024,1024]{1,0:T(8,128)(2,1)S(1)} %bitcast.160, s32[1024]{0:T(1024)S(1)} %pad_clamp_fusion), kind=kCustom, calls=%fused_computation.1 | custom fusion | bytes 2099200 | tf_op jit(solution)/shard_map/gather | solution.py:140
  201.6 1.6 fusion.101
  203.2 0.1 copy.92
  203.3 0.7 fusion.98
  (33 shorter events, 0.2 us)
Async XLA Ops:
  0.0 170.9 %copy-start = (bf16[1024,192]{0,1:T(8,128)(2,1)S(1)}, bf16[1024,192]{0,1:T(8,128)(2,1)}, u32[]{:S(2)}) copy-start(bf16[1024,192]{0,1:T(8,128)(2,1)} %param.21) | copy-start | bytes 1179652
  1.4 22.8 %all-to-all-start = ((bf16[4,1,2]{2,1,0:T(2,128)(2,1)}), bf16[4,1,2]{2,1,0:T(2,128)(2,1)S(1)}, u32[]{:S(2)}, u32[]{:S(2)}) async-start(bf16[4,1,2]{2,1,0:T(2,128)(2,1)} %all_to_all.20), calls=%async_computation | async-start | bytes 4096 | tf_op jit(solution)/shard_map/all_to_all | solution.py:67
  21.2 0.5 copy-start.6
  24.2 5.3 %copy-start.8 = (s32[256]{0:T(256)S(1)}, s32[256]{0:T(256)}, u32[]{:S(2)}) copy-start(s32[256]{0:T(256)} %param.14) | copy-start | bytes 3076
  24.2 5.3 %copy-start.11 = (s32[2]{0:T(128)S(1)}, s32[2]{0:T(128)}, u32[]{:S(2)}) copy-start(s32[2]{0:T(128)} %param.15) | copy-start | bytes 28
  24.2 5.5 %copy-start.2 = (bf16[256,1024]{1,0:T(8,128)(2,1)S(1)}, bf16[256,1024]{1,0:T(8,128)(2,1)}, u32[]{:S(2)}) copy-start(bf16[256,1024]{1,0:T(8,128)(2,1)} %param.13) | copy-start | bytes 1572868
  24.2 53.1 %all-to-all-start.1 = ((bf16[4,2,128,2048]{2,1,3,0:T(2,128)(2,1)}), bf16[4,2,128,2048]{2,1,3,0:T(2,128)(2,1)}, u32[]{:S(2)}, u32[]{:S(2)}) async-start(bf16[4,2,128,2048]{2,1,3,0:T(2,128)(2,1)} %copy.74), calls=%async_computation.1 | async-start | bytes 8388608 | tf_op jit(solution)/shard_map/all_to_all | solution.py:60
  29.7 5.0 %copy-start.10 = (f32[8,4]{0,1:T(4,128)S(1)}, f32[8,4]{0,1:T(4,128)}, u32[]{:S(2)}) copy-start(f32[8,4]{0,1:T(4,128)} %param.19) | copy-start | bytes 388
  96.1 1.0 copy-start.3
  96.1 1.0 copy-start.9
  96.4 1.6 copy-start.1
  166.6 4.2 %copy-start.7 = (s32[512,1]{0,1:T(1,128)S(1)}, s32[512,1]{0,1:T(1,128)}, u32[]{:S(2)}) copy-start(s32[512,1]{0,1:T(1,128)} %copy-done.6) | copy-start | bytes 6148
  166.6 4.2 %copy-start.4 = (s32[256,2]{0,1:T(2,128)S(1)}, s32[256,2]{0,1:T(2,128)}, u32[]{:S(2)}) copy-start(s32[256,2]{0,1:T(2,128)} %param.22) | copy-start | bytes 6148
  166.6 32.2 %all-to-all-start.3 = ((bf16[32,32,1024]{2,1,0:T(8,128)(2,1)}), bf16[32,32,1024]{2,1,0:T(8,128)(2,1)S(1)}, u32[]{:S(2)}, u32[]{:S(2)}) async-start(bf16[32,32,1024]{2,1,0:T(8,128)(2,1)} %bitcast.171), calls=%async_computation.3 | async-start | bytes 4194304 | tf_op jit(solution)/shard_map/all_to_all | solution.py:132
  198.8 2.8 %copy-start.5 = (bf16[1024,6]{0,1:T(8,128)(2,1)S(1)}, bf16[1024,6]{0,1:T(8,128)(2,1)}, u32[]{:S(2)}) copy-start(bf16[1024,6]{0,1:T(8,128)(2,1)} %param.25) | copy-start | bytes 36868
where the time goes:
time: 206 us; the launch traced here: 204 us
  waiting for transfers between devices  68.5 us (33%)
  matrix products  41.5 us (20%)
  blocking collectives  38 us (18%)
  local copies, waits for them, and re-layouts  34.6 us (17%)
  starting transfers between devices  14.4 us (7%)
  other arithmetic  6.61 us (3%)
    all_to_all x1, waiting for transfers between devices, local(): lax.all_to_all(cache_kv.reshape(req_size, group_slots, block_len, 2 * fea...  41 us
    all_to_all x1, blocking collectives, local(): lax.all_to_all(outgoing, 'exp', split_axis=0, concat_axis=0, tiled=True)  38 us
    all_to_all x1, waiting for transfers between devices, local(): lax.all_to_all(produced.reshape(source_count, item_count, feature), 'exp'...  27.5 us
    dot_general x1, matrix products, local(): jnp.dot(hidden, down_matrix, preferred_element_type=jnp.float32)  25.6 us
    reshape x1, local copies, waits for them, and re-layouts, local(): cache_kv.reshape(req_size, group_slots, block_len, 2 * feature)  11.1 us
    dot_general x4, matrix products, attend(): jnp.einsum('hcn,nhd->chd', weights, value_part, preferred_element_type=jn...  9.17 us
    slice x1, local copies, waits for them, and re-layouts, local(): moved_kv[owner].reshape(group_slots * block_len, 2 * feature)  5.24 us
    all_to_all x1, starting transfers between devices, local(): lax.all_to_all(cache_kv.reshape(req_size, group_slots, block_len, 2 * fea...  5.18 us
  transfers between devices with their start and end apart: 3, of which 2 were waited for; matrix products, arithmetic and copies ran while one was open for 12% of the time, Pallas kernels for 0%

commit v1 on v0

v1 whole, which is shorter than its diff:
```python
import functools
import math

import jax
import jax.numpy as jnp
from jax import lax
from jax.experimental import pallas as pl
from jax.experimental.pallas import tpu as pltpu
from jax.sharding import PartitionSpec as P

EPSILON = 1e-05
F32 = jnp.float32
BF16 = jnp.bfloat16
NT = (((1,), (1,)), ((), ()))


def attend_kernel(
    heads_step,
    block_ref,
    hist_ref,
    bias_ref,
    req_ref,
    query_ref,
    k0,
    v0,
    k1,
    v1,
    k2,
    v2,
    k3,
    v3,
    cand_ref,
    update_ref,
    gain_ref,
    place_ref,
    out_ref,
    mixed_ref,
    attended,
):
    step = pl.program_id(0)
    rows = req_ref.shape[0]
    first = jnp.broadcast_to(req_ref[...], (rows, 128)) == 0
    for part in range(heads_step):
        head = step * heads_step + part
        cols = pl.ds(part * 128, 128)
        query = query_ref[:, cols]
        total = None
        for owner, (key_ref, value_ref) in enumerate(((k0, v0), (k1, v1), (k2, v2), (k3, v3))):
            scores = lax.dot_general(query, key_ref[:, cols], NT, preferred_element_type=F32)
            scores = jnp.where(first, scores[:, :128], scores[:, 128:])
            block_a = block_ref[owner, 0]
            block_b = block_ref[owner, 1]
            bias = jnp.where(first, bias_ref[head, block_a], bias_ref[head, block_b])
            half = (scores * (1.0 / math.sqrt(128.0)) + bias) * 0.5
            weight = half + half * jnp.tanh(half)
            live_a = jnp.where(block_a < hist_ref[0], 1.0, 0.0)
            live_b = jnp.where(block_b < hist_ref[1], 1.0, 0.0)
            weight_a = jnp.where(first, weight * live_a, 0.0)
            weight_b = jnp.where(first, 0.0, weight * live_b)
            weights = jnp.concatenate([weight_a, weight_b], axis=1).astype(BF16)
            partial = jnp.dot(weights, value_ref[:, cols], preferred_element_type=F32)
            total = partial if total is None else total + partial
        attended[step, :, cols] = total

    @pl.when(step == pl.num_programs(0) - 1)
    def _():
        steps = attended.shape[0]
        width = attended.shape[2]
        square = None
        for i in range(steps):
            item = attended[i]
            item = jnp.sum(item * item, axis=1, keepdims=True)
            square = item if square is None else square + item
        inv_rms = lax.rsqrt(square * (1.0 / (steps * width)) + EPSILON)
        for i in range(steps):
            cols = pl.ds(i * width, width)
            mixed = cand_ref[:, cols].astype(F32) + gain_ref[:, cols] * attended[i] * inv_rms * update_ref[:, cols]
            mixed = mixed.astype(BF16)
            mixed_ref[:, cols] = mixed
            out_ref[:, cols] = jnp.dot(place_ref[...], mixed, preferred_element_type=F32).astype(BF16)


def expert_kernel(row_tile, x_ref, up_ref, tower_ref, out_ref, total):
    step = pl.program_id(0)
    rows = x_ref.shape[0]

    @pl.when(step == 0)
    def _():
        total[...] = jnp.zeros_like(total)

    for start in range(0, rows, row_tile):
        at = pl.ds(start, row_tile)
        half = jnp.dot(x_ref[at, :], up_ref[...], preferred_element_type=F32) * 0.5
        hidden = (half + half * jnp.tanh(half)).astype(BF16)
        total[at, :] += jnp.dot(hidden, tower_ref[...], preferred_element_type=F32)

    @pl.when(step == pl.num_programs(0) - 1)
    def _():
        peers = out_ref.shape[0]
        share = rows // peers
        zero = jnp.zeros((8, 128 - share), F32)
        for tile in range(rows // 128):
            turned = jnp.transpose(total[pl.ds(tile * 128, 128), :])
            turned = turned[0:8, :] + turned[8:16, :]
            for i in range(128 // share):
                piece = turned[:, i * share : (i + 1) * share]
                out_ref[tile * (128 // share) + i] = jnp.concatenate([piece, zero], axis=1)


def combine_kernel(slot_ref, weight_ref, back_ref, out_ref):
    routes = slot_ref.shape[0]
    rows = routes // 2
    hot = slot_ref[...]
    back = back_ref[...]
    high = back.astype(BF16)
    rest = back - high.astype(F32)
    middle = rest.astype(BF16)
    low = (rest - middle.astype(F32)).astype(BF16)
    found = lax.dot_general(hot, high, NT, preferred_element_type=F32)
    found += lax.dot_general(hot, middle, NT, preferred_element_type=F32)
    found += lax.dot_general(hot, low, NT, preferred_element_type=F32)
    found = found * weight_ref[...]
    found = found[:rows] + found[rows:]
    found = found[:, :128] + found[:, 128:]
    for shift in (64, 32, 16, 8):
        found = found + pltpu.roll(found, shift, 1)
    out_ref[...] = found[:, : out_ref.shape[1]]


def local(
    cand_emb,
    cand_request,
    hist_blocks,
    cache_kv,
    block_map,
    w_query_update,
    rel_bias,
    norm_gain,
    w_gate,
    expert_ids,
    w_up,
    w_down,
    w_tower,
):
    rows, feature = cand_emb.shape
    owners = lax.axis_size("req")
    me = lax.axis_index("req")
    task_count = w_tower.shape[1]
    expert_count = w_gate.shape[1] // task_count
    top_count = expert_ids.shape[1]
    capacity = 2 * rows * top_count // expert_count
    slots = expert_count * capacity

    cache = cache_kv.reshape(owners, -1, 2 * feature)
    ids = block_map.reshape(owners, 1, -1)
    moved = [lax.dynamic_index_in_dim(cache, me, 0, False)]
    moved_ids = [lax.dynamic_index_in_dim(ids, me, 0, False)]
    for shift in (1, 3, 2):
        to = lax.rem(me + shift, owners)
        pairs = [(i, (i + shift) % owners) for i in range(owners)]
        moved_ids.append(lax.ppermute(lax.dynamic_index_in_dim(ids, to, 0, False), "req", pairs))
        moved.append(lax.ppermute(lax.dynamic_index_in_dim(cache, to, 0, False), "req", pairs))
    blocks = jnp.concatenate(moved_ids, axis=0)

    projected = jnp.dot(cand_emb, w_query_update, preferred_element_type=F32)
    queries = projected[:, :feature].astype(BF16)
    update = jax.nn.silu(projected[:, feature:])

    tower = jnp.dot(w_down[0], w_tower, preferred_element_type=F32)
    tower_high = lax.reduce_precision(tower, 8, 7)
    tower_low = tower - tower_high
    gap = jnp.zeros((tower.shape[0], 8 - task_count), BF16)
    tower_parts = jnp.concatenate(
        [
            tower_high.astype(BF16),
            gap,
            tower_low.astype(BF16),
            gap,
            jnp.zeros((tower.shape[0], 112), BF16),
        ],
        axis=1,
    )

    expert_range = jnp.arange(expert_count, dtype=jnp.int32)
    hot = (expert_ids[:, :, None] == expert_range).astype(BF16)
    hot_both = jnp.concatenate([hot[:, 0], hot[:, 1]], axis=0)
    routes = hot_both.shape[0]
    earlier = jnp.tril(jnp.ones((routes, routes), BF16), -1)
    counts = jnp.dot(earlier, hot_both, preferred_element_type=F32)
    position = jnp.sum(counts * hot_both.astype(F32), axis=1).astype(jnp.int32)
    flat_ids = jnp.concatenate([expert_ids[:, 0], expert_ids[:, 1]], axis=0)
    slot_of = flat_ids * capacity + position
    slot_range = jnp.arange(slots, dtype=jnp.int32)[:, None]
    place = (
        (slot_of[None, :rows] == slot_range) | (slot_of[None, rows:] == slot_range)
    ).astype(BF16)
    slot_hot = (position[:, None] == jnp.arange(128, dtype=jnp.int32)[None, :]).astype(BF16)

    heads_step = 2
    width = heads_step * 128
    steps = feature // width
    keys = moved[0].shape[0]
    whole = lambda *shape: pl.BlockSpec(shape, lambda i, *_: (0,) * len(shape))
    smem = pl.BlockSpec(memory_space=pltpu.SMEM)
    kv_specs = []
    kv_args = []
    for item in moved:
        kv_specs.append(pl.BlockSpec((keys, width), lambda i: (0, i)))
        kv_specs.append(pl.BlockSpec((keys, width), lambda i: (0, i + steps)))
        kv_args += [item, item]
    outgoing, mixed_rows = pl.pallas_call(
        functools.partial(attend_kernel, heads_step),
        grid=(steps,),
        in_specs=[
            smem,
            smem,
            smem,
            whole(rows, 1),
            pl.BlockSpec((rows, width), lambda i: (0, i)),
            *kv_specs,
            whole(rows, feature),
            whole(rows, feature),
            whole(1, feature),
            whole(slots, rows),
        ],
        out_specs=[whole(slots, feature), whole(rows, feature)],
        out_shape=[
            jax.ShapeDtypeStruct((slots, feature), BF16),
            jax.ShapeDtypeStruct((rows, feature), BF16),
        ],
        scratch_shapes=[pltpu.VMEM((steps, rows, width), F32)],
        compiler_params=pltpu.CompilerParams(vmem_limit_bytes=40 * 2**20),
        cost_estimate=pl.CostEstimate(flops=2 * 10**9, bytes_accessed=9 * 10**6, transcendentals=2**20),
        name="attend",
    )(
        blocks,
        hist_blocks,
        rel_bias,
        cand_request[:, None],
        queries,
        *kv_args,
        cand_emb,
        update,
        norm_gain[None, :],
        place,
    )

    arrived = lax.all_to_all(
        outgoing.reshape(expert_count, capacity, feature), "exp", split_axis=0, concat_axis=0, tiled=True
    )

    logits = jnp.dot(mixed_rows, w_gate, preferred_element_type=F32).reshape(
        rows, 1, task_count, expert_count
    )
    picked = jnp.sum(logits * hot.astype(F32)[:, :, None, :], axis=3)
    squashed = jax.nn.sigmoid(picked)
    gates = squashed / jnp.sum(squashed, axis=1, keepdims=True)
    gates = jnp.pad(gates, ((0, 0), (0, 0), (0, 8 - task_count)))
    spread = hot.astype(F32)[:, :, :, None] * gates[:, :, None, :]
    spread = spread.reshape(rows, top_count, expert_count * 8)
    spread = jnp.concatenate([spread[:, 0], spread[:, 1]], axis=0)

    hidden_count = w_up.shape[2]
    tile = 512
    produced = pl.pallas_call(
        functools.partial(expert_kernel, 256),
        grid=(hidden_count // tile,),
        in_specs=[
            whole(slots, feature),
            pl.BlockSpec((feature, tile), lambda i: (0, i)),
            pl.BlockSpec((tile, 128), lambda i: (i, 0)),
        ],
        out_specs=whole(expert_count, 8, 128),
        out_shape=jax.ShapeDtypeStruct((expert_count, 8, 128), F32),
        scratch_shapes=[pltpu.VMEM((slots, 128), F32)],
        compiler_params=pltpu.CompilerParams(vmem_limit_bytes=40 * 2**20),
        cost_estimate=pl.CostEstimate(flops=11 * 10**9, bytes_accessed=11 * 10**6, transcendentals=2**22),
        name="expert",
    )(arrived.reshape(slots, feature), w_up[0], tower_parts)

    came_back = lax.all_to_all(produced, "exp", split_axis=0, concat_axis=0, tiled=True)

    return pl.pallas_call(
        combine_kernel,
        out_shape=jax.ShapeDtypeStruct((rows, task_count), F32),
        cost_estimate=pl.CostEstimate(flops=10**8, bytes_accessed=10**6, transcendentals=0),
        name="combine",
    )(slot_hot, spread, came_back.reshape(expert_count * 8, 128))


def solution(mesh):
    placed = (
        P(("req", "exp"), None),
        P(("req", "exp")),
        P(("req", "exp")),
        P(("req", "exp"), None, None),
        P(("req", "exp")),
        P(),
        P(),
        P(),
        P(),
        P(("req", "exp"), None),
        P("exp", None, None),
        P("exp", None, None),
        P(),
    )
    return jax.shard_map(
        local, mesh=mesh, in_specs=placed, out_specs=P(("req", "exp"), None), check_vma=False
    )
```

time: 206 us -> 146 us (0.71)
  waiting for transfers between devices: 68.5 us -> 29.3 us
  blocking collectives: 38 us -> 0 us
  matrix products: 41.5 us -> 12.5 us
  Pallas kernels: 0 us -> 25.6 us
  starting transfers between devices: 14.4 us -> 27.2 us
  other arithmetic: 6.61 us -> 11.4 us
  local copies, waits for them, and re-layouts: 34.6 us -> 39.1 us
    all_to_all x3 -> x2, waiting for transfers between devices: 68.5 us -> 16.4 us  [the longest x1 10.8 us: local(): lax.all_to_all(outgoing.reshape(expert_count, capacity, feature), 'exp',...]
    all_to_all x1 -> x0, blocking collectives: 38 us -> none  [local(): lax.all_to_all(outgoing, 'exp', split_axis=0, concat_axis=0, tiled=True)]
    dot_general x8 -> x4, matrix products: 41.5 us -> 12.5 us  [the longest x1 6.38 us: local(): tower = jnp.dot(w_down[0], w_tower, preferred_element_type=F32)]
    pallas_call x0 -> x3, Pallas kernels: none -> 25.6 us  [the longest x1 16.1 us: local(): pl.pallas_call(functools.partial(expert_kernel, 256), grid=(hidden_count...]
    ppermute x0 -> x6, waiting for transfers between devices: none -> 12.9 us  [the longest x3 12.9 us: local(): lax.ppermute(lax.dynamic_index_in_dim(ids, to, 0, False), 'req', pairs)]
    reshape x2 -> x1, local copies, waits for them, and re-layouts: 11.3 us -> 0.08 us  [local(): ids = block_map.reshape(owners, 1, -1)]
    ppermute x0 -> x6, starting transfers between devices: none -> 10.5 us  [the longest x3 5.25 us: local(): lax.ppermute(lax.dynamic_index_in_dim(ids, to, 0, False), 'req', pairs)]
    unnamed x29 -> x33, local copies, waits for them, and re-layouts: 4.39 us -> 11.5 us
  transfers between devices with their start and end apart: 3 -> 8, of which waited for: 2 -> 4; matrix products, arithmetic and copies ran while one was open for 12% -> 32% of each run, Pallas kernels for 0% -> 0%
where the time goes in v1:
time: 146 us; the launch traced here: 145 us
  local copies, waits for them, and re-layouts  39.1 us (27%)
  waiting for transfers between devices  29.3 us (20%)
  starting transfers between devices  27.2 us (19%)
  Pallas kernels  25.6 us (18%)
  matrix products  12.5 us (9%)
  other arithmetic  11.4 us (8%)
    pallas_call x1, Pallas kernels, local(): pl.pallas_call(functools.partial(expert_kernel, 256), grid=(hidden_count...  16.1 us
    ppermute x3, waiting for transfers between devices, local(): lax.ppermute(lax.dynamic_index_in_dim(ids, to, 0, False), 'req', pairs)  12.9 us
    unnamed x33, local copies, waits for them, and re-layouts  11.5 us
    all_to_all x1, waiting for transfers between devices, local(): lax.all_to_all(outgoing.reshape(expert_count, capacity, feature), 'exp',...  10.8 us
    all_to_all x1, starting transfers between devices, local(): lax.all_to_all(outgoing.reshape(expert_count, capacity, feature), 'exp',...  10.8 us
    pallas_call x1, Pallas kernels, local(): pl.pallas_call(functools.partial(attend_kernel, heads_step), grid=(steps,...  7.1 us
    dot_general x1, matrix products, local(): tower = jnp.dot(w_down[0], w_tower, preferred_element_type=F32)  6.38 us
    concatenate x1, local copies, waits for them, and re-layouts, local(): jnp.concatenate([tower_high.astype(BF16), gap, tower_low.astype(BF16), ga...  6.31 us
  transfers between devices with their start and end apart: 8, of which 4 were waited for; matrix products, arithmetic and copies ran while one was open for 32% of the time, Pallas kernels for 0%

profile of v1, /device:TPU:1, one launch (start us, length us, event | category | flops | bytes accessed | tf_op | source)
XLA Modules:
  0.0 145.3 jit_solution(597581205139204610)
XLA Ops:
  0.0 0.0 copy-start
  0.0 4.1 %dynamic-slice_bitcast_fusion = (bf16[256,2048]{1,0:T(8,128)(2,1)}, bf16[256,2048]{1,0:T(8,128)(2,1)}, bf16[256,2048]{1,0:T(8,128)(2,1)}, bf16[256,2048]{1,0:T(8,128)(2,1)S(1)}) fusion(bf16[4,256,2048]{2,1,0:T(8,128)(2,1)} %bitcast.48, s32[]{:T(128)S(6)} %select_n.26, s32[]{:T(128)S(6)} %select_n.25, s32[]{:T(128)S(6)} %select_n.24, s32[]{:T(128)S(6)} %select_n.23), kind=kLoop, calls=%fused_computation.9 | loop fusion | bytes 8388624 | tf_op jit(solution)/shard_map/jit(dynamic_index_in_dim)/squeeze | solution.py:162
  4.1 2.1 %collective-permute-start.3 = (bf16[256,2048]{1,0:T(8,128)(2,1)}, bf16[256,2048]{1,0:T(8,128)(2,1)S(1)}, u32[]{:S(2)}, u32[]{:S(2)}) collective-permute-start(bf16[256,2048]{1,0:T(8,128)(2,1)} %get-tuple-element.11), channel_id=1, source_target_pairs={{0,32},{32,64},{64,96},{96,0},{1,33},{33,65},{65,97},{97,1},{2,34}... | collective-permute-start | bytes 3145736 | tf_op jit(solution)/shard_map/ppermute | solution.py:162
  6.2 1.4 collective-permute-start.4
  7.6 1.6 %collective-permute-start.5 = (bf16[256,2048]{1,0:T(8,128)(2,1)}, bf16[256,2048]{1,0:T(8,128)(2,1)}, u32[]{:S(2)}, u32[]{:S(2)}) collective-permute-start(bf16[256,2048]{1,0:T(8,128)(2,1)} %get-tuple-element.9), channel_id=1, source_target_pairs={{0,64},{32,96},{64,0},{96,32},{1,65},{33,97},{65,1},{97,33},{2,66}... | collective-permute-start | bytes 3145736 | tf_op jit(solution)/shard_map/ppermute | solution.py:162
  9.3 0.0 copy-done.14
  9.3 0.1 reshape.39
  9.4 0.6 fusion.17
  10.0 0.4 collective-permute-start
  10.4 2.3 %collective-permute-start.1 = (s32[1,2]{1,0:T(1,128)}, s32[1,2]{1,0:T(1,128)}, u32[]{:S(2)}, u32[]{:S(2)}) collective-permute-start(s32[1,2]{1,0:T(1,128)} %get-tuple-element.25), channel_id=1, source_target_pairs={{0,96},{32,0},{64,32},{96,64},{1,97},{33,1},{65,33},{97,65},{2,98}... | collective-permute-start | bytes 32 | tf_op jit(solution)/shard_map/ppermute | solution.py:161
  12.7 0.0 copy-done.12
  12.7 0.6 fusion.15
  13.3 0.6 fusion.27
  13.9 0.6 slice_bitcast_fusion.1
  14.5 3.6 %fusion.28 = f32[256,2048]{1,0:T(8,128)S(1)} fusion(bf16[256,1024]{1,0:T(8,128)(2,1)} %cand_ref.1, bf16[1024,2048]{1,0:T(8,128)(2,1)} %param.18), kind=kOutput, calls=%fused_computation.56 | convolution fusion | flops 1073741824 | bytes 6815744 | tf_op jit(solution)/shard_map/dot_general | solution.py:165
  18.1 0.0 copy-start.10
  18.1 1.3 copy-done.10
  19.4 0.9 slice.51.query_ref
  20.3 1.5 %copy.38.req_ref = s32[256,1]{1,0:T(8,128)} copy(s32[256,1]{0,1:T(1,128)} %bitcast.55) | data formatting | bytes 2048 | tf_op jit(solution)/shard_map/broadcast_in_dim | solution.py:239
  21.8 0.1 copy.37.bias_ref
  21.8 6.4 %fusion.25 = (f32[4096,6]{0,1:T(8,128)}, bf16[4096,6]{0,1:T(8,128)(2,1)}, f32[4096,6]{0,1:T(8,128)}) fusion(bf16[1024,6]{0,1:T(8,128)(2,1)} %param.25, bf16[1,4096,1024]{2,1,0:T(8,128)(2,1)} %param.24), kind=kOutput, calls=%fused_computation.53 | convolution fusion | flops 50380800 | bytes 8646656 | tf_op jit(solution)/shard_map/dot_general | solution.py:169
  28.2 2.9 %copy.41 = f32[4096,6]{1,0:T(8,128)} copy(f32[4096,6]{0,1:T(8,128)} %get-tuple-element.29) | data formatting | bytes 196608 | tf_op jit(solution)/shard_map/dot_general | solution.py:169
  31.1 2.9 %copy.42 = f32[4096,6]{1,0:T(8,128)} copy(f32[4096,6]{0,1:T(8,128)} %get-tuple-element.15) | data formatting | bytes 196608 | tf_op jit(solution)/shard_map/reduce_precision | solution.py:170
  34.0 2.2 %copy.43 = bf16[4096,6]{1,0:T(8,128)(2,1)} copy(bf16[4096,6]{0,1:T(8,128)(2,1)} %get-tuple-element.16) | data formatting | bytes 98304 | tf_op jit(solution)/shard_map/convert_element_type | solution.py:175
  36.2 1.2 fusion.2
  37.4 0.7 fusion.16
  38.1 0.2 fusion.5.place_ref
  38.3 1.5 %divide_multiply_fusion.update_ref = f32[256,1024]{1,0:T(8,128)S(1)} fusion(f32[256,2048]{1,0:T(8,128)} %copy-done.10), kind=kLoop, calls=%fused_computation.8 | loop fusion | flops 1048576 | bytes 2097152 | tf_op jit(solution)/shard_map/jit(silu)/mul | solution.py:167
  39.8 11.0 %collective-permute-done = s32[1,2]{1,0:T(1,128)} collective-permute-done((s32[1,2]{1,0:T(1,128)}, s32[1,2]{1,0:T(1,128)}, u32[]{:S(2)}, u32[]{:S(2)}) %collective-permute-start) | collective-permute-done | bytes 40 | tf_op jit(solution)/shard_map/ppermute | solution.py:161
  50.9 2.6 %collective-permute-start.2 = (s32[1,2]{1,0:T(1,128)}, s32[1,2]{1,0:T(1,128)S(1)}, u32[]{:S(2)}, u32[]{:S(2)}) collective-permute-start(s32[1,2]{1,0:T(1,128)} %get-tuple-element.24), channel_id=1, source_target_pairs={{0,64},{32,96},{64,0},{96,32},{1,65},{33,97},{65,1},{97,33},{2,66}... | collective-permute-start | bytes 32 | tf_op jit(solution)/shard_map/ppermute | solution.py:161
  53.4 0.0 collective-permute-done.1
  53.4 1.8 %collective-permute-done.2 = s32[1,2]{1,0:T(1,128)S(1)} collective-permute-done((s32[1,2]{1,0:T(1,128)}, s32[1,2]{1,0:T(1,128)S(1)}, u32[]{:S(2)}, u32[]{:S(2)}) %collective-permute-start.2) | collective-permute-done | bytes 40 | tf_op jit(solution)/shard_map/ppermute | solution.py:161
  55.3 0.7 pad_add_fusion.block_ref
  56.0 0.0 collective-permute-done.3.k1.v1
  56.0 0.0 collective-permute-done.4.k2.v2
  56.0 0.0 collective-permute-done.5.k3.v3
  56.0 1.0 copy-done.2
  57.1 0.9 copy-done.3
  58.0 1.0 copy-done.5
  59.0 7.1 %attend.1 = (bf16[1024,1024]{1,0:T(8,128)(2,1)S(1)}, bf16[256,1024]{1,0:T(8,128)(2,1)S(1)}) custom-call(s32[4,2]{1,0:T(4,128)S(1)} %pad_add_fusion.block_ref, s32[2]{0:T(128)S(1)} %copy-done.8, f32[8,4]{1,0:T(8,128)S(1)} %copy.37.bias_ref, s32[256,1]{1,0:T(8,128)S(1)} %copy-done.3, bf16[256,1024]{1,0:T(8,128)(2,1)S(1)} %copy-done.2, ...), custom_call_target="tpu_custom_call" | custom-call | flops 2000000000 | bytes 9000000 | tf_op jit(solution)/shard_map/attend/pallas_call | solution.py:211
  66.1 1.3 copy-done.1
  67.5 0.8 copy-done.4
  68.3 10.8 %all-to-all-start = ((bf16[32,32,1024]{2,1,0:T(8,128)(2,1)}), bf16[32,32,1024]{2,1,0:T(8,128)(2,1)S(1)}, u32[]{:S(2)}, u32[]{:S(2)}) async-start(bf16[32,32,1024]{2,1,0:T(8,128)(2,1)} %bitcast.44), calls=%async_computation | async-start | bytes 4194304 | tf_op jit(solution)/shard_map/all_to_all | solution.py:248
  79.0 3.4 %subtract_convert_fusion = bf16[4096,6]{1,0:T(8,128)(2,1)} fusion(f32[4096,6]{1,0:T(8,128)} %copy.41, f32[4096,6]{1,0:T(8,128)} %copy.42), kind=kLoop, calls=%fused_computation.2 | loop fusion | flops 49152 | bytes 245760 | tf_op jit(solution)/shard_map/convert_element_type | solution.py:177
  82.4 1.2 broadcast_in_dim.34
  83.6 1.2 broadcast_in_dim.35
  84.8 6.3 %concatenate.19.tower_ref = bf16[4096,128]{1,0:T(8,128)(2,1)S(1)} concatenate(bf16[4096,6]{1,0:T(8,128)(2,1)} %copy.43, bf16[4096,2]{1,0:T(8,128)(2,1)} %broadcast_in_dim.34, bf16[4096,6]{1,0:T(8,128)(2,1)} %subtract_convert_fusion, bf16[4096,2]{1,0:T(8,128)(2,1)} %broadcast_in_dim.34, bf16[4096,112]{1,0:T(8,128)(2,1)} %broadcast_in_dim.35), dimensions={1} | concatenate | bytes 2097152 | tf_op jit(solution)/shard_map/concatenate | solution.py:173
  91.1 0.8 fusion.10.slot_ref
  91.9 1.4 fusion.29
  93.3 0.9 multiply_reduce_fusion
  94.3 1.7 %multiply_bitcast_fusion = f32[256,2,256]{0,2,1:T(8,128)} fusion(f32[256,2,8]{0,2,1:T(8,128)S(1)} %pad.4, f32[256,2,32]{0,2,1:T(8,128)} %get-tuple-element.27), kind=kLoop, calls=%fused_computation.18 | loop fusion | flops 131072 | bytes 606208 | tf_op jit(solution)/shard_map/mul | solution.py:259
  96.0 10.8 %all-to-all-done = bf16[32,32,1024]{2,1,0:T(8,128)(2,1)S(1)} async-done(((bf16[32,32,1024]{2,1,0:T(8,128)(2,1)}), bf16[32,32,1024]{2,1,0:T(8,128)(2,1)S(1)}, u32[]{:S(2)}, u32[]{:S(2)}) %all-to-all-start) | async-done | bytes 2097184 | tf_op jit(solution)/shard_map/all_to_all | solution.py:248
  106.8 3.4 %copy-done.9 = bf16[1,1024,4096]{2,1,0:T(8,128)(2,1)S(1)} copy-done((bf16[1,1024,4096]{2,1,0:T(8,128)(2,1)S(1)}, bf16[1,1024,4096]{2,1,0:T(8,128)(2,1)}, u32[]{:S(2)}) %copy-start.9) | copy-done | bytes 8388632
  110.2 16.1 %expert.1 = f32[32,8,128]{2,1,0:T(8,128)S(1)} custom-call(bf16[1024,1024]{1,0:T(8,128)(2,1)S(1)} %bitcast.45, bf16[1024,4096]{1,0:T(8,128)(2,1)S(1)} %bitcast.47, bf16[4096,128]{1,0:T(8,128)(2,1)S(1)} %concatenate.19.tower_ref), custom_call_target="tpu_custom_call" | custom-call | flops 11000000512 | bytes 11000000 | tf_op jit(solution)/shard_map/expert/pallas_call | solution.py:265
  126.3 0.6 copy-done.6
  126.9 5.9 %all-to-all-start.1 = ((f32[32,8,128]{2,1,0:T(8,128)}), f32[32,8,128]{2,1,0:T(8,128)S(1)}, u32[]{:S(2)}, u32[]{:S(2)}) async-start(f32[32,8,128]{2,1,0:T(8,128)} %copy-done.6), calls=%async_computation.1 | async-start | bytes 262144 | tf_op jit(solution)/shard_map/all_to_all | solution.py:281
  132.9 1.1 fusion.24
  134.0 0.1 copy.45
  134.1 0.1 copy.46
  134.2 0.8 pad_maximum_fusion.weight_ref
  135.1 5.6 %all-to-all-done.1 = f32[32,8,128]{2,1,0:T(8,128)S(1)} async-done(((f32[32,8,128]{2,1,0:T(8,128)}), f32[32,8,128]{2,1,0:T(8,128)S(1)}, u32[]{:S(2)}, u32[]{:S(2)}) %all-to-all-start.1) | async-done | bytes 131104 | tf_op jit(solution)/shard_map/all_to_all | solution.py:281
  140.6 0.7 copy-done.11
  141.3 2.4 %combine.1 = f32[256,6]{1,0:T(8,128)} custom-call(bf16[512,128]{1,0:T(8,128)(2,1)} %fusion.10.slot_ref, f32[512,256]{1,0:T(8,128)} %pad_maximum_fusion.weight_ref, f32[256,128]{1,0:T(8,128)} %bitcast.52), custom_call_target="tpu_custom_call" | custom-call | flops 100000000 | bytes 1000000 | tf_op jit(solution)/shard_map/combine/pallas_call | solution.py:283
  143.7 1.6 %copy.44 = f32[256,6]{0,1:T(8,128)} copy(f32[256,6]{1,0:T(8,128)} %combine.1) | data formatting | bytes 12288 | tf_op jit(solution)/shard_map/combine/pallas_call | solution.py:283
  (23 shorter events, 0.1 us)
Async XLA Ops:
  0.0 91.9 %copy-start = (bf16[1024,192]{0,1:T(8,128)(2,1)S(1)}, bf16[1024,192]{0,1:T(8,128)(2,1)}, u32[]{:S(2)}) copy-start(bf16[1024,192]{0,1:T(8,128)(2,1)} %param.21) | copy-start | bytes 1179652
  0.0 9.3 %copy-start.14 = (s32[8]{0:T(128)S(1)}, s32[8]{0:T(128)}, u32[]{:S(2)}) copy-start(s32[8]{0:T(128)} %param.17) | copy-start | bytes 100
  0.0 12.7 %copy-start.12 = (s32[256,2]{0,1:T(2,128)S(1)}, s32[256,2]{0,1:T(2,128)}, u32[]{:S(2)}) copy-start(s32[256,2]{0,1:T(2,128)} %param.22) | copy-start | bytes 6148
  4.1 17.7 %copy-start.13 = (f32[8,4]{0,1:T(4,128)S(1)}, f32[8,4]{0,1:T(4,128)}, u32[]{:S(2)}) copy-start(f32[8,4]{0,1:T(4,128)} %param.19) | copy-start | bytes 388
  4.1 51.9 %collective-permute-start.3 = (bf16[256,2048]{1,0:T(8,128)(2,1)}, bf16[256,2048]{1,0:T(8,128)(2,1)S(1)}, u32[]{:S(2)}, u32[]{:S(2)}) collective-permute-start(bf16[256,2048]{1,0:T(8,128)(2,1)} %get-tuple-element.11), channel_id=1, source_target_pairs={{0,32},{32,64},{64,96},{96,0},{1,33},{33,65},{65,97},{97,1},{2,34}... | collective-permute-start | bytes 3145736 | tf_op jit(solution)/shard_map/ppermute | solution.py:162
  6.2 49.8 %collective-permute-start.4 = (bf16[256,2048]{1,0:T(8,128)(2,1)}, bf16[256,2048]{1,0:T(8,128)(2,1)S(1)}, u32[]{:S(2)}, u32[]{:S(2)}) collective-permute-start(bf16[256,2048]{1,0:T(8,128)(2,1)} %get-tuple-element.10), channel_id=1, source_target_pairs={{0,96},{32,0},{64,32},{96,64},{1,97},{33,1},{65,33},{97,65},{2,98}... | collective-permute-start | bytes 3145736 | tf_op jit(solution)/shard_map/ppermute | solution.py:162
  7.6 48.3 %collective-permute-start.5 = (bf16[256,2048]{1,0:T(8,128)(2,1)}, bf16[256,2048]{1,0:T(8,128)(2,1)}, u32[]{:S(2)}, u32[]{:S(2)}) collective-permute-start(bf16[256,2048]{1,0:T(8,128)(2,1)} %get-tuple-element.9), channel_id=1, source_target_pairs={{0,64},{32,96},{64,0},{96,32},{1,65},{33,97},{65,1},{97,33},{2,66}... | collective-permute-start | bytes 3145736 | tf_op jit(solution)/shard_map/ppermute | solution.py:162
  10.0 40.9 %collective-permute-start = (s32[1,2]{1,0:T(1,128)}, s32[1,2]{1,0:T(1,128)}, u32[]{:S(2)}, u32[]{:S(2)}) collective-permute-start(s32[1,2]{1,0:T(1,128)} %get-tuple-element.26), channel_id=1, source_target_pairs={{0,32},{32,64},{64,96},{96,0},{1,33},{33,65},{65,97},{97,1},{2,34}... | collective-permute-start | bytes 32 | tf_op jit(solution)/shard_map/ppermute | solution.py:161
  10.4 43.1 %collective-permute-start.1 = (s32[1,2]{1,0:T(1,128)}, s32[1,2]{1,0:T(1,128)}, u32[]{:S(2)}, u32[]{:S(2)}) collective-permute-start(s32[1,2]{1,0:T(1,128)} %get-tuple-element.25), channel_id=1, source_target_pairs={{0,96},{32,0},{64,32},{96,64},{1,97},{33,1},{65,33},{97,65},{2,98}... | collective-permute-start | bytes 32 | tf_op jit(solution)/shard_map/ppermute | solution.py:161
  18.1 1.3 copy-start.10
  28.2 27.8 %copy-start.7 = (f32[1024]{0:T(1024)S(1)}, f32[1024]{0:T(1024)}, u32[]{:S(2)}) copy-start(f32[1024]{0:T(1024)} %param.20) | copy-start | bytes 12292
  28.2 27.8 %copy-start.8 = (s32[2]{0:T(128)S(1)}, s32[2]{0:T(128)}, u32[]{:S(2)}) copy-start(s32[2]{0:T(128)} %hist_ref.1) | copy-start | bytes 28
  50.9 4.4 %collective-permute-start.2 = (s32[1,2]{1,0:T(1,128)}, s32[1,2]{1,0:T(1,128)S(1)}, u32[]{:S(2)}, u32[]{:S(2)}) collective-permute-start(s32[1,2]{1,0:T(1,128)} %get-tuple-element.24), channel_id=1, source_target_pairs={{0,64},{32,96},{64,0},{96,32},{1,65},{33,97},{65,1},{97,33},{2,66}... | collective-permute-start | bytes 32 | tf_op jit(solution)/shard_map/ppermute | solution.py:161
  56.0 1.0 copy-start.2
  57.1 0.9 copy-start.3
  58.0 1.0 copy-start.5
  66.1 1.3 copy-start.1
  67.5 0.8 copy-start.4
  68.3 38.5 %all-to-all-start = ((bf16[32,32,1024]{2,1,0:T(8,128)(2,1)}), bf16[32,32,1024]{2,1,0:T(8,128)(2,1)S(1)}, u32[]{:S(2)}, u32[]{:S(2)}) async-start(bf16[32,32,1024]{2,1,0:T(8,128)(2,1)} %bitcast.44), calls=%async_computation | async-start | bytes 4194304 | tf_op jit(solution)/shard_map/all_to_all | solution.py:248
  106.8 3.4 %copy-start.9 = (bf16[1,1024,4096]{2,1,0:T(8,128)(2,1)S(1)}, bf16[1,1024,4096]{2,1,0:T(8,128)(2,1)}, u32[]{:S(2)}) copy-start(bf16[1,1024,4096]{2,1,0:T(8,128)(2,1)} %param.23) | copy-start | bytes 25165828
  126.3 0.7 copy-start.6
  126.9 13.7 %all-to-all-start.1 = ((f32[32,8,128]{2,1,0:T(8,128)}), f32[32,8,128]{2,1,0:T(8,128)S(1)}, u32[]{:S(2)}, u32[]{:S(2)}) async-start(f32[32,8,128]{2,1,0:T(8,128)} %copy-done.6), calls=%async_computation.1 | async-start | bytes 262144 | tf_op jit(solution)/shard_map/all_to_all | solution.py:281
  140.6 0.7 copy-start.11

commit v2 on v0

v2 whole, which is shorter than its diff:
```python
import functools
import math

import jax
import jax.numpy as jnp
from jax import lax
from jax.experimental import pallas as pl
from jax.experimental.pallas import tpu as pltpu
from jax.sharding import PartitionSpec as P

EPSILON = 1e-05
F32 = jnp.float32
BF16 = jnp.bfloat16
NT = (((1,), (1,)), ((), ()))
TN = (((0,), (0,)), ((), ()))
SHIFTS = (1, 3, 2)
LIMIT = 63 * 2**20


def pack_kernel(me_ref, ids_ref, *refs):
    count = len(SHIFTS)
    ins, outs = refs[: 2 * count], refs[2 * count :]
    keys = ins[0].shape[1]
    heads = ins[0].shape[2] // 128
    for n, shift in enumerate(SHIFTS):
        for head in range(heads):
            cols = pl.ds(head * 128, 128)
            outs[n][pl.ds(head * keys, keys), :] = ins[2 * n][0, :, cols]
            outs[n][pl.ds((heads + head) * keys, keys), :] = ins[2 * n + 1][0, :, cols]
    if len(outs) > count:
        row = lax.broadcasted_iota(jnp.int32, (16, 128), 0)
        me = me_ref[0]

        def tile_of(owner):
            first = ids_ref[2 * owner].astype(F32)
            second = ids_ref[2 * owner + 1].astype(F32)
            return jnp.where(row == 0, first, second).astype(BF16)

        for n, shift in enumerate(SHIFTS):
            outs[n][pl.ds(2 * heads * keys, 16), :] = tile_of(lax.rem(me + shift, count + 1))
        outs[count][...] = tile_of(me)


def route_kernel(capacity, lane_ref, ids_ref, cand_ref, place_ref, slot_ref, out_ref):
    rows = ids_ref.shape[1]
    experts = place_ref.shape[0] // capacity
    ids = jnp.concatenate([ids_ref[0:1, :], ids_ref[1:2, :]], axis=1)
    hot = lax.broadcasted_iota(jnp.int32, (experts, 2 * rows), 0) == ids
    hot = jnp.where(hot, 1.0, 0.0)
    here = lax.broadcasted_iota(jnp.int32, (2 * rows, 2 * rows), 0)
    there = lax.broadcasted_iota(jnp.int32, (2 * rows, 2 * rows), 1)
    earlier = jnp.where(here < there, 1.0, 0.0).astype(BF16)
    counts = jnp.dot(hot.astype(BF16), earlier, preferred_element_type=F32)
    position = jnp.sum(counts * hot, axis=0, keepdims=True).astype(jnp.int32)
    slot = ids * capacity + position
    spot = lax.broadcasted_iota(jnp.int32, place_ref.shape, 0)
    place = (spot == slot[:, :rows]) | (spot == slot[:, rows:])
    place = jnp.where(place, 1.0, 0.0).astype(BF16)
    place_ref[...] = place
    lane = position + lane_ref[0]
    lanes = lax.broadcasted_iota(jnp.int32, slot_ref.shape, 0) == lane
    slot_ref[...] = jnp.where(lanes, 1.0, 0.0).astype(BF16)
    out_ref[...] = jnp.dot(place, cand_ref[...], preferred_element_type=F32).astype(BF16)


def project_kernel(feature, cand_ref, weight_ref, query_ref, update_ref):
    step = pl.program_id(0)
    half = pl.num_programs(0) // 2
    projected = jnp.dot(cand_ref[...], weight_ref[...], preferred_element_type=F32)

    @pl.when(step < half)
    def _():
        query_ref[...] = projected.astype(BF16)

    @pl.when(step >= half)
    def _():
        update_ref[...] = projected / (1.0 + jnp.exp(-projected))


def tower_kernel(down_ref, tower_ref, out_ref):
    product = lax.dot_general(tower_ref[...], down_ref[...], NT, preferred_element_type=F32)
    high = product.astype(BF16)
    low = (product - high.astype(F32)).astype(BF16)
    out_ref[...] = jnp.concatenate([high[0:8], low[0:8]], axis=0)


def attend_head(head, first, masks, query, parts, tiles, bias_ref):
    total = None
    for owner, (key, value) in enumerate(parts):
        scores = lax.dot_general(query, key, NT, preferred_element_type=F32)
        scores = jnp.where(first, scores[:, :128], scores[:, 128:])
        block_a, block_b = tiles[owner]
        bias_a = jnp.zeros_like(block_a)
        bias_b = jnp.zeros_like(block_b)
        for block in range(bias_ref.shape[1]):
            entry = bias_ref[head, block] * 0.5
            bias_a = jnp.where(block_a == block, entry, bias_a)
            bias_b = jnp.where(block_b == block, entry, bias_b)
        half = scores * (0.5 / math.sqrt(128.0)) + jnp.where(first, bias_a, bias_b)
        weight = (half + half * jnp.tanh(half)).astype(BF16)
        weight = jnp.concatenate([weight, weight], axis=1) * masks[owner]
        partial = jnp.dot(weight, value, preferred_element_type=F32)
        total = partial if total is None else total + partial
    return total


def block_rows(tile_refs):
    rows = []
    for ref in tile_refs:
        tile = ref[...].astype(F32)
        rows.append((tile[0:1, :], tile[1:2, :]))
    return rows


def fill_masks(first, tiles, hist_ref, masks):
    length_a = hist_ref[0].astype(F32)
    length_b = hist_ref[1].astype(F32)
    for owner, (block_a, block_b) in enumerate(tiles):
        live_a = jnp.where(block_a < length_a, 1.0, 0.0)
        live_b = jnp.where(block_b < length_b, 1.0, 0.0)
        mask_a = jnp.where(first, live_a, 0.0)
        mask_b = jnp.where(first, 0.0, live_b)
        masks[owner] = jnp.concatenate([mask_a, mask_b], axis=1).astype(BF16)


def attend_first_kernel(
    me_ref, hist_ref, bias_ref, req_ref, query_ref, k0, v0, k1, v1, k2, v2, k3, v3,
    t0, t1, t2, t3, update_ref, gain_ref, place_ref, out_ref, stuff_ref, square_ref, masks,
):
    head = pl.program_id(0)
    rows = req_ref.shape[0]
    first = jnp.broadcast_to(req_ref[...], (rows, 128)) == 0
    tiles = block_rows((t0, t1, t2, t3))

    @pl.when(head == 0)
    def _():
        fill_masks(first, tiles, hist_ref, masks)
        square_ref[...] = jnp.zeros_like(square_ref)

    parts = ((k0[0], v0[0]), (k1[...], v1[...]), (k2[...], v2[...]), (k3[...], v3[...]))
    attended = attend_head(head, first, masks, query_ref[...], parts, tiles, bias_ref)
    square_ref[...] += attended * attended
    stuff = (gain_ref[...] * attended * update_ref[...]).astype(BF16)
    stuff_ref[...] = stuff
    out_ref[...] = jnp.dot(place_ref[...], stuff, preferred_element_type=F32).astype(BF16)


def attend_last_kernel(
    me_ref, hist_ref, bias_ref, req_ref, query_ref, k0, v0, k1, v1, k2, v2, k3, v3,
    t0, t1, t2, t3, update_ref, gain_ref, place_ref, cand_ref, stuff_ref, square_ref,
    out_ref, mixed_ref, masks, attended,
):
    step = pl.program_id(0)
    heads = pl.num_programs(0)
    rows = req_ref.shape[0]
    first = jnp.broadcast_to(req_ref[...], (rows, 128)) == 0
    tiles = block_rows((t0, t1, t2, t3))

    @pl.when(step == 0)
    def _():
        fill_masks(first, tiles, hist_ref, masks)

    parts = ((k0[0], v0[0]), (k1[...], v1[...]), (k2[...], v2[...]), (k3[...], v3[...]))
    found = attend_head(step + heads, first, masks, query_ref[...], parts, tiles, bias_ref)
    attended[step] = found

    @pl.when(step == heads - 1)
    def _():
        count = attended.shape[0]
        feature = cand_ref.shape[1]
        early = feature - count * 128
        square = square_ref[...]
        for i in range(count):
            square = square + attended[i] * attended[i]
        mean = jnp.sum(square, axis=1, keepdims=True) * (1.0 / feature)
        inv_rms = lax.rsqrt(mean + EPSILON)
        mixed = cand_ref[:, :early].astype(F32) + stuff_ref[...].astype(F32) * inv_rms
        mixed_ref[:, :early] = mixed.astype(BF16)
        place = place_ref[...]
        peers = out_ref.shape[0]
        share = place.shape[0] // peers
        for i in range(count):
            cols = pl.ds(early + i * 128, 128)
            here = pl.ds(i * 128, 128)
            mixed = cand_ref[:, cols].astype(F32)
            mixed = mixed + gain_ref[:, here] * attended[i] * update_ref[:, here] * inv_rms
            mixed = mixed.astype(BF16)
            mixed_ref[:, cols] = mixed
            moved = jnp.dot(place, mixed, preferred_element_type=F32).astype(BF16)
            out_ref[:, pl.ds(i * share, share), :] = moved.reshape(peers, share, 128)
        lane = lax.broadcasted_iota(jnp.int32, (rows, 128), 1)
        high = inv_rms.astype(BF16).astype(F32)
        low = inv_rms - high
        scale = jnp.where(lane == 0, high, jnp.where(lane == 1, low, 0.0)).astype(BF16)
        moved = jnp.dot(place, scale, preferred_element_type=F32).reshape(peers, share, 128)
        early_part = moved[:, : share // 2, :]
        late_part = moved[:, share // 2 :, :].reshape(peers * share // 2, 128)
        late_part = pltpu.roll(late_part, 64, 1).reshape(peers, share // 2, 128)
        out_ref[:, pl.ds(count * share, share // 2), :] = (early_part + late_part).astype(BF16)


def gate_kernel(tasks, ids_ref, weight_ref, mixed_ref, out_ref):
    rows = mixed_ref.shape[0]
    experts = weight_ref.shape[0] // tasks
    logits = lax.dot_general(weight_ref[...], mixed_ref[...], NT, preferred_element_type=F32)
    squashed = []
    for k in range(2):
        hot = lax.broadcasted_iota(jnp.int32, (experts, rows), 0) == ids_ref[k : k + 1, :]
        picked = []
        for task in range(8):
            if task < tasks:
                here = logits[task * experts : (task + 1) * experts, :]
                picked.append(jnp.sum(jnp.where(hot, here, 0.0), axis=0, keepdims=True))
            else:
                picked.append(jnp.zeros((1, rows), F32))
        squashed.append(jax.nn.sigmoid(jnp.concatenate(picked, axis=0)))
    whole = squashed[0] + squashed[1]
    for k in range(2):
        gates = squashed[k] / whole
        ids = ids_ref[k : k + 1, :]
        for expert in range(experts):
            out_ref[pl.ds(expert * 8, 8), pl.ds(k * rows, rows)] = jnp.where(ids == expert, gates, 0.0)


def expert_kernel(
    cand_ref, stuff_ref, last_ref, up_ref, tower_ref, out_ref, total, turned
):
    step = pl.program_id(0)
    tile = up_ref.shape[1]
    peers, share, early = cand_ref.shape
    rows = peers * share

    @pl.when(step == 0)
    def _():
        total[...] = jnp.zeros_like(total)
        count = (last_ref.shape[1] - share // 2) // share
        scale = last_ref[:, pl.ds(count * share, share // 2), :].astype(F32)
        scale = scale.reshape(rows // 2, 128)
        scale = scale + pltpu.roll(scale, 127, 1)
        scale = scale.reshape(peers, share // 2, 128) * 0.5
        scale = jnp.concatenate([scale[:, :, 0:1], scale[:, :, 64:65]], axis=1)
        scale = jnp.broadcast_to(scale, (peers, share, 128))
        for i in range(early // 128):
            cols = pl.ds(i * 128, 128)
            block = cand_ref[:, :, cols].astype(F32) * 0.5
            block = block + stuff_ref[:, :, cols].astype(F32) * scale
            turned[cols, :] = jnp.transpose(block.astype(BF16).reshape(rows, 128))
        for i in range(count):
            block = last_ref[:, pl.ds(i * share, share), :].reshape(rows, 128)
            turned[pl.ds(early + i * 128, 128), :] = jnp.transpose(block * jnp.asarray(0.5, BF16))

    half = lax.dot_general(up_ref[...], turned[...], TN, preferred_element_type=F32)
    hidden = (half + half * jnp.tanh(half)).astype(BF16)
    tower = tower_ref[:, pl.ds(pl.multiple_of(step * tile, tile), tile)]
    total[...] += jnp.dot(tower, hidden, preferred_element_type=F32)

    @pl.when(step == pl.num_programs(0) - 1)
    def _():
        found = total[0:8, :] + total[8:16, :]
        each = 128 // share
        for peer in range(peers):
            out_ref[peer] = found[:, (peer // each) * 128 : (peer // each + 1) * 128]


def combine_kernel(slot_ref, weight_ref, back_ref, out_ref):
    rows = slot_ref.shape[1] // 2
    hot = slot_ref[...]
    back = back_ref[...]
    high = back.astype(BF16)
    rest = back - high.astype(F32)
    middle = rest.astype(BF16)
    low = (rest - middle.astype(F32)).astype(BF16)
    found = jnp.dot(high, hot, preferred_element_type=F32)
    found += jnp.dot(middle, hot, preferred_element_type=F32)
    found += jnp.dot(low, hot, preferred_element_type=F32)
    found = found * weight_ref[...]
    found = found[:, :rows] + found[:, rows:]
    total = found[0:8]
    for expert in range(1, found.shape[0] // 8):
        total = total + found[expert * 8 : (expert + 1) * 8]
    out_ref[...] = total[: out_ref.shape[0]]


def params():
    return pltpu.CompilerParams(vmem_limit_bytes=LIMIT)


def cost(flops, bytes_accessed, transcendentals=0):
    return pl.CostEstimate(flops=flops, bytes_accessed=bytes_accessed, transcendentals=transcendentals)


def whole(*shape):
    return pl.BlockSpec(shape, lambda i, *_: (0,) * len(shape))


def local(
    cand_emb,
    cand_request,
    hist_blocks,
    cache_kv,
    block_map,
    w_query_update,
    rel_bias,
    norm_gain,
    w_gate,
    expert_ids,
    w_up,
    w_down,
    w_tower,
):
    rows, feature = cand_emb.shape
    owners = lax.axis_size("req")
    me = lax.axis_index("req").astype(jnp.int32)
    head_count = rel_bias.shape[0]
    tasks = w_tower.shape[1]
    experts = w_gate.shape[1] // tasks
    capacity = 2 * rows * expert_ids.shape[1] // experts
    slots = experts * capacity
    heads = head_count // 2
    early = heads * 128
    keys = cache_kv.shape[0] // owners * cache_kv.shape[1]
    parts = 2 * heads
    me_scalar = me[None]
    smem = pl.BlockSpec(memory_space=pltpu.SMEM)

    cache = cache_kv.reshape(owners, keys, 2 * feature)

    def pack(chunk):
        def block(shift, half):
            return pl.BlockSpec(
                (1, keys, early),
                lambda i, me, ids: (lax.rem(me[0] + shift, owners), 0, 2 * half + chunk),
            )

        tail = 16 if chunk == 0 else 0
        shapes = [jax.ShapeDtypeStruct((parts * keys + tail, 128), BF16)] * len(SHIFTS)
        if chunk == 0:
            shapes.append(jax.ShapeDtypeStruct((16, 128), BF16))
        blocks = [block(shift, half) for shift in SHIFTS for half in range(2)]
        return pl.pallas_call(
            pack_kernel,
            grid_spec=pltpu.PrefetchScalarGridSpec(
                num_scalar_prefetch=2,
                grid=(1,),
                in_specs=blocks,
                out_specs=[whole(*shape.shape) for shape in shapes],
            ),
            out_shape=shapes,
            compiler_params=params(),
            cost_estimate=cost(0, 10**6),
            name="pack",
        )(me_scalar, block_map, *[cache] * len(blocks))

    def send(item, shift):
        pairs = [(i, (i + shift) % owners) for i in range(owners)]
        return lax.ppermute(item, "req", pairs)

    *packed, own_tile = pack(0)
    first_moved = [send(item, shift) for item, shift in zip(packed, SHIFTS)]
    packed_last = pack(1)
    last_moved = []
    for item, ahead, shift in zip(packed_last, first_moved, SHIFTS):
        item, _ = lax.optimization_barrier((item, ahead))
        last_moved.append(send(item, shift))

    ids_rows, _ = lax.optimization_barrier((expert_ids.T, own_tile))
    each = 128 // capacity
    lane = lax.rem(lax.axis_index("exp").astype(jnp.int32), each) * capacity
    place, slot_hot, cand_out = pl.pallas_call(
        functools.partial(route_kernel, capacity),
        grid=(1,),
        in_specs=[
            smem,
            whole(2, rows),
            pl.BlockSpec((rows, early), lambda i: (0, 0)),
        ],
        out_specs=[whole(slots, rows), whole(128, 2 * rows), whole(slots, early)],
        out_shape=[
            jax.ShapeDtypeStruct((slots, rows), BF16),
            jax.ShapeDtypeStruct((128, 2 * rows), BF16),
            jax.ShapeDtypeStruct((slots, early), BF16),
        ],
        compiler_params=params(),
        cost_estimate=cost(5 * 10**8, 3 * 10**6),
        name="route",
    )(lane[None], ids_rows, cand_emb)

    def exchange(item):
        return lax.all_to_all(item, "exp", split_axis=0, concat_axis=0, tiled=True)

    cand_in = exchange(cand_out.reshape(experts, capacity, early))

    cand_rows, _, _ = lax.optimization_barrier((cand_emb, place, packed_last[0]))
    steps = 4
    wide = 2 * feature // steps
    queries, update = pl.pallas_call(
        functools.partial(project_kernel, feature),
        grid=(steps,),
        in_specs=[whole(rows, feature), pl.BlockSpec((feature, wide), lambda i: (0, i))],
        out_specs=[
            pl.BlockSpec((rows, wide), lambda i: (0, jnp.minimum(i, 1))),
            pl.BlockSpec((rows, wide), lambda i: (0, jnp.maximum(i - 2, 0))),
        ],
        out_shape=[
            jax.ShapeDtypeStruct((rows, feature), BF16),
            jax.ShapeDtypeStruct((rows, feature), F32),
        ],
        compiler_params=params(),
        cost_estimate=cost(11 * 10**8, 6 * 10**6, 2**18),
        name="project",
    )(cand_rows, w_query_update)

    hidden_count = w_up.shape[2]
    tile = 512
    towers = pl.pallas_call(
        tower_kernel,
        grid=(hidden_count // tile,),
        in_specs=[
            pl.BlockSpec((None, tile, feature), lambda i: (0, i, 0)),
            whole(16, feature),
        ],
        out_specs=pl.BlockSpec((16, tile), lambda i: (0, i)),
        out_shape=jax.ShapeDtypeStruct((16, hidden_count), BF16),
        compiler_params=params(),
        cost_estimate=cost(10**8, 9 * 10**6),
        name="tower",
    )(w_down, jnp.pad(w_tower.T, ((0, 16 - tasks), (0, 0))))

    def attend_specs(chunk, moved):
        base = chunk * heads
        specs = [
            smem,
            smem,
            whole(rows, 1),
            pl.BlockSpec((rows, 128), lambda i, me: (0, base + i)),
            pl.BlockSpec((1, keys, 128), lambda i, me: (me[0], 0, base + i)),
            pl.BlockSpec((1, keys, 128), lambda i, me: (me[0], 0, head_count + base + i)),
        ]
        args = [hist_blocks, rel_bias, cand_request[:, None], queries, cache, cache]
        for item in moved:
            specs.append(pl.BlockSpec((keys, 128), lambda i, me: (i, 0)))
            specs.append(pl.BlockSpec((keys, 128), lambda i, me: (heads + i, 0)))
            args += [item, item]
        specs.append(whole(16, 128))
        args.append(own_tile)
        at = parts * keys // 16
        for item in first_moved:
            specs.append(pl.BlockSpec((16, 128), lambda i, me: (at, 0)))
            args.append(item)
        return specs, args

    gain = norm_gain[None, :]
    specs, args = attend_specs(0, first_moved)
    stuff_out, stuff, square = pl.pallas_call(
        attend_first_kernel,
        grid_spec=pltpu.PrefetchScalarGridSpec(
            num_scalar_prefetch=1,
            grid=(heads,),
            in_specs=[
                *specs,
                pl.BlockSpec((rows, 128), lambda i, me: (0, i)),
                pl.BlockSpec((1, 128), lambda i, me: (0, i)),
                whole(slots, rows),
            ],
            out_specs=[
                pl.BlockSpec((slots, 128), lambda i, me: (0, i)),
                pl.BlockSpec((rows, 128), lambda i, me: (0, i)),
                whole(rows, 128),
            ],
            scratch_shapes=[pltpu.VMEM((owners, rows, keys), BF16)],
        ),
        out_shape=[
            jax.ShapeDtypeStruct((slots, early), BF16),
            jax.ShapeDtypeStruct((rows, early), BF16),
            jax.ShapeDtypeStruct((rows, 128), F32),
        ],
        compiler_params=params(),
        cost_estimate=cost(30 * 10**9, 10**6),
        name="attend_first",
    )(me_scalar, *args, update, gain, place)

    stuff_in = exchange(stuff_out.reshape(experts, capacity, early))

    late = feature - early
    specs, args = attend_specs(1, last_moved)
    last_rows = (heads * capacity) + capacity // 2
    last_out, mixed_rows = pl.pallas_call(
        attend_last_kernel,
        grid_spec=pltpu.PrefetchScalarGridSpec(
            num_scalar_prefetch=1,
            grid=(heads,),
            in_specs=[
                *specs,
                pl.BlockSpec((rows, late), lambda i, me: (0, 1)),
                pl.BlockSpec((1, late), lambda i, me: (0, 1)),
                whole(slots, rows),
                whole(rows, feature),
                whole(rows, early),
                whole(rows, 128),
            ],
            out_specs=[whole(experts, last_rows, 128), whole(rows, feature)],
            scratch_shapes=[
                pltpu.VMEM((owners, rows, keys), BF16),
                pltpu.VMEM((heads, rows, 128), F32),
            ],
        ),
        out_shape=[
            jax.ShapeDtypeStruct((experts, last_rows, 128), BF16),
            jax.ShapeDtypeStruct((rows, feature), BF16),
        ],
        compiler_params=params(),
        cost_estimate=cost(100 * 10**9, 10**6),
        name="attend_last",
    )(me_scalar, *args, update, gain, place, cand_emb, stuff, square)

    last_in = exchange(last_out)

    gates = pl.pallas_call(
        functools.partial(gate_kernel, tasks),
        out_shape=jax.ShapeDtypeStruct((experts * 8, 2 * rows), F32),
        compiler_params=params(),
        cost_estimate=cost(10**8, 2 * 10**6, 4096),
        name="gate",
    )(ids_rows, w_gate.T, mixed_rows)

    produced = pl.pallas_call(
        expert_kernel,
        grid=(hidden_count // tile,),
        in_specs=[
            whole(experts, capacity, early),
            whole(experts, capacity, early),
            whole(experts, last_rows, 128),
            pl.BlockSpec((None, feature, tile), lambda i: (0, 0, i)),
            whole(16, hidden_count),
        ],
        out_specs=whole(experts, 8, 128),
        out_shape=jax.ShapeDtypeStruct((experts, 8, 128), F32),
        scratch_shapes=[pltpu.VMEM((16, slots), F32), pltpu.VMEM((feature, slots), BF16)],
        compiler_params=params(),
        cost_estimate=cost(11 * 10**9, 13 * 10**6, 2**22),
        name="expert",
    )(cand_in, stuff_in, last_in, w_up, towers)

    came_back = exchange(produced)

    scores = pl.pallas_call(
        combine_kernel,
        out_shape=jax.ShapeDtypeStruct((tasks, rows), F32),
        compiler_params=params(),
        cost_estimate=cost(10**8, 10**6),
        name="combine",
    )(slot_hot, gates, came_back.reshape(experts * 8, 128))
    return scores.T


def solution(mesh):
    placed = (
        P(("req", "exp"), None),
        P(("req", "exp")),
        P(("req", "exp")),
        P(("req", "exp"), None, None),
        P(("req", "exp")),
        P(),
        P(),
        P(),
        P(),
        P(("req", "exp"), None),
        P("exp", None, None),
        P("exp", None, None),
        P(),
    )
    return jax.shard_map(
        local, mesh=mesh, in_specs=placed, out_specs=P(("req", "exp"), None), check_vma=False
    )
```

time: 206 us -> 123 us (0.60)
  Pallas kernels: 0 us -> 57.5 us
  waiting for transfers between devices: 68.5 us -> 23.9 us
  matrix products: 41.5 us -> 0 us
  blocking collectives: 38 us -> 0 us
  local copies, waits for them, and re-layouts: 34.6 us -> 2.76 us
  starting transfers between devices: 14.4 us -> 37.7 us
  other arithmetic: 6.61 us -> 0 us
    pallas_call x0 -> x10, Pallas kernels: none -> 57.5 us  [the longest x1 15.2 us: local(): pl.pallas_call(expert_kernel, grid=(hidden_count // tile,), in_specs=[who...]
    all_to_all x3 -> x4, waiting for transfers between devices: 68.5 us -> 17.6 us  [exchange(): return lax.all_to_all(item, 'exp', split_axis=0, concat_axis=0, tiled=True)]
    dot_general x8 -> x0, matrix products: 41.5 us -> none  [the longest x1 25.6 us: local(): jnp.dot(hidden, down_matrix, preferred_element_type=jnp.float32)]
    all_to_all x1 -> x0, blocking collectives: 38 us -> none  [local(): lax.all_to_all(outgoing, 'exp', split_axis=0, concat_axis=0, tiled=True)]
    all_to_all x3 -> x4, starting transfers between devices: 14.4 us -> 29.7 us  [exchange(): return lax.all_to_all(item, 'exp', split_axis=0, concat_axis=0, tiled=True)]
    reshape x2 -> x0, local copies, waits for them, and re-layouts: 11.3 us -> none  [the longest x1 11.1 us: local(): cache_kv.reshape(req_size, group_slots, block_len, 2 * feature)]
    ppermute x0 -> x6, starting transfers between devices: none -> 8.01 us  [send(): return lax.ppermute(item, 'req', pairs)]
    slice x6 -> x0, local copies, waits for them, and re-layouts: 7.33 us -> none  [the longest x1 5.24 us: local(): moved_kv[owner].reshape(group_slots * block_len, 2 * feature)]
  transfers between devices with their start and end apart: 3 -> 10, of which waited for: 2 -> 4; matrix products, arithmetic and copies ran while one was open for 12% -> 2% of each run, Pallas kernels for 0% -> 30%
where the time goes in v2:
time: 123 us; the launch traced here: 122 us
  Pallas kernels  57.5 us (47%)
  starting transfers between devices  37.7 us (31%)
  waiting for transfers between devices  23.9 us (19%)
  local copies, waits for them, and re-layouts  2.76 us (2%)
    all_to_all x4, starting transfers between devices, exchange(): return lax.all_to_all(item, 'exp', split_axis=0, concat_axis=0, tiled=True)  29.7 us
    all_to_all x4, waiting for transfers between devices, exchange(): return lax.all_to_all(item, 'exp', split_axis=0, concat_axis=0, tiled=True)  17.6 us
    pallas_call x1, Pallas kernels, local(): pl.pallas_call(expert_kernel, grid=(hidden_count // tile,), in_specs=[who...  15.2 us
    ppermute x6, starting transfers between devices, send(): return lax.ppermute(item, 'req', pairs)  8.01 us
    pallas_call x1, Pallas kernels, local(): pl.pallas_call(tower_kernel, grid=(hidden_count // tile,), in_specs=[pl.B...  7.94 us
    pallas_call x1, Pallas kernels, local(): pl.pallas_call(attend_last_kernel, grid_spec=pltpu.PrefetchScalarGridSpec...  7.8 us
    pallas_call x2, Pallas kernels, pack(): pl.pallas_call(pack_kernel, grid_spec=pltpu.PrefetchScalarGridSpec(num_sc...  7.14 us
    pallas_call x1, Pallas kernels, local(): pl.pallas_call(attend_first_kernel, grid_spec=pltpu.PrefetchScalarGridSpe...  6.89 us
  transfers between devices with their start and end apart: 10, of which 4 were waited for; matrix products, arithmetic and copies ran while one was open for 2% of the time, Pallas kernels for 30%

profile of v2, /device:TPU:1, one launch (start us, length us, event | category | flops | bytes accessed | tf_op | source)
XLA Modules:
  0.0 122.0 jit_solution(11644306379215877365)
XLA Ops:
  0.0 3.5 %pack.2 = (bf16[2064,128]{1,0:T(8,128)(2,1)}, bf16[2064,128]{1,0:T(8,128)(2,1)}, bf16[2064,128]{1,0:T(8,128)(2,1)}, bf16[16,128]{1,0:T(8,128)(2,1)}) custom-call(s32[1]{0:T(128)} %bitcast.2.me_ref, s32[8]{0:T(128)} %ids_ref.3, bf16[4,256,2048]{2,1,0:T(8,128)(2,1)} %bitcast.12, bf16[4,256,2048]{2,1,0:T(8,128)(2,1)} %bitcast.13, ...), custom_call_target="tpu_custom_call" | custom-call | bytes 1000000 | tf_op jit(solution)/shard_map/pack/pallas_call | solution.py:340
  3.5 2.1 %collective-permute-start = (bf16[2064,128]{1,0:T(8,128)(2,1)}, bf16[2064,128]{1,0:T(8,128)(2,1)S(1)}, u32[]{:S(2)}, u32[]{:S(2)}) collective-permute-start(bf16[2064,128]{1,0:T(8,128)(2,1)} %get-tuple-element.34), channel_id=1, source_target_pairs={{0,32},{32,64},{64,96},{96,0},{1,33},{33,65},{65,97},{97,1},{2,34}... | collective-permute-start | bytes 1585160 | tf_op jit(solution)/shard_map/ppermute | solution.py:356
  5.7 1.5 %collective-permute-start.2 = (bf16[2064,128]{1,0:T(8,128)(2,1)}, bf16[2064,128]{1,0:T(8,128)(2,1)}, u32[]{:S(2)}, u32[]{:S(2)}) collective-permute-start(bf16[2064,128]{1,0:T(8,128)(2,1)} %get-tuple-element.37), channel_id=1, source_target_pairs={{0,96},{32,0},{64,32},{96,64},{1,97},{33,1},{65,33},{97,65},{2,98}... | collective-permute-start | bytes 1585160 | tf_op jit(solution)/shard_map/ppermute | solution.py:356
  7.1 1.6 %collective-permute-start.4 = (bf16[2064,128]{1,0:T(8,128)(2,1)}, bf16[2064,128]{1,0:T(8,128)(2,1)}, u32[]{:S(2)}, u32[]{:S(2)}) collective-permute-start(bf16[2064,128]{1,0:T(8,128)(2,1)} %get-tuple-element.40), channel_id=1, source_target_pairs={{0,64},{32,96},{64,0},{96,32},{1,65},{33,97},{65,1},{97,33},{2,66}... | collective-permute-start | bytes 1585160 | tf_op jit(solution)/shard_map/ppermute | solution.py:356
  8.8 2.7 %route.1 = (bf16[1024,256]{1,0:T(8,128)(2,1)}, bf16[128,512]{1,0:T(8,128)(2,1)}, bf16[1024,512]{1,0:T(8,128)(2,1)}) custom-call(s32[1]{0:T(128)} %bitcast.lane_ref, s32[2,256]{1,0:T(2,128)} %bitcast.33, bf16[256,1024]{1,0:T(8,128)(2,1)} %cand_ref.4), custom_call_target="tpu_custom_call" | custom-call | flops 500000000 | bytes 3000000 | tf_op jit(solution)/shard_map/route/pallas_call | solution.py:369
  11.5 9.5 %all-to-all-start = ((bf16[32,32,512]{2,1,0:T(8,128)(2,1)}), bf16[32,32,512]{2,1,0:T(8,128)(2,1)}, u32[]{:S(2)}, u32[]{:S(2)}) async-start(bf16[32,32,512]{2,1,0:T(8,128)(2,1)} %bitcast.28), calls=%async_computation | async-start | bytes 2097152 | tf_op jit(solution)/shard_map/all_to_all | solution.py:389
  21.0 0.0 copy-start.3
  21.0 0.0 copy-start.2
  21.0 3.6 %pack.3 = (bf16[2048,128]{1,0:T(8,128)(2,1)}, bf16[2048,128]{1,0:T(8,128)(2,1)}, bf16[2048,128]{1,0:T(8,128)(2,1)}) custom-call(s32[1]{0:T(128)} %bitcast.2.me_ref, s32[8]{0:T(128)} %ids_ref.3, bf16[4,256,2048]{2,1,0:T(8,128)(2,1)} %bitcast.18, bf16[4,256,2048]{2,1,0:T(8,128)(2,1)} %bitcast.19, bf16[4,256,2048]{2,1,0:T(8,128)(2,1)} %bitcast.20, ...), custom_call_target="tpu_custom_call" | custom-call | bytes 1000000 | tf_op jit(solution)/shard_map/pack/pallas_call | solution.py:340
  24.6 0.0 copy-done.3
  24.6 0.8 copy.19.req_ref
  25.4 0.0 copy-done.2
  25.4 0.7 copy.18.bias_ref
  26.1 5.4 %project.1 = (bf16[256,1024]{1,0:T(8,128)(2,1)}, f32[256,1024]{1,0:T(8,128)}) custom-call(bf16[256,1024]{1,0:T(8,128)(2,1)} %cand_ref.4, bf16[1024,2048]{1,0:T(8,128)(2,1)} %weight_ref.1), custom_call_target="tpu_custom_call" | custom-call | flops 1100000000 | bytes 6000000 | tf_op jit(solution)/shard_map/project/pallas_call | solution.py:396
  31.4 0.0 collective-permute-done.k1.v1.t1
  31.4 0.0 copy-start.4
  31.4 0.5 collective-permute-start.1
  31.9 0.0 collective-permute-done.2.k2.v2.t2
  31.9 2.3 %collective-permute-start.3 = (bf16[2048,128]{1,0:T(8,128)(2,1)}, bf16[2048,128]{1,0:T(8,128)(2,1)}, u32[]{:S(2)}, u32[]{:S(2)}) collective-permute-start(bf16[2048,128]{1,0:T(8,128)(2,1)} %get-tuple-element.38), channel_id=1, source_target_pairs={{0,96},{32,0},{64,32},{96,64},{1,97},{33,1},{65,33},{97,65},{2,98}... | collective-permute-start | bytes 1572872 | tf_op jit(solution)/shard_map/ppermute | solution.py:356
  34.2 0.0 collective-permute-done.4.k3.v3.t3
  34.2 0.1 collective-permute-start.5
  34.2 0.0 copy-done.4
  34.2 6.9 %attend_first.1 = (bf16[1024,512]{1,0:T(8,128)(2,1)}, bf16[256,512]{1,0:T(8,128)(2,1)}, f32[256,128]{1,0:T(8,128)}) custom-call(s32[1]{0:T(128)} %bitcast.2.me_ref, s32[2]{0:T(128)} %hist_ref.3, f32[8,4]{1,0:T(8,128)} %copy.18.bias_ref, s32[256,1]{1,0:T(8,128)} %copy.19.req_ref, bf16[256,1024]{1,0:T(8,128)(2,1)} %get-tuple-element.33.query_ref, ...), custom_call_target="tpu_custom_call" | custom-call | flops 30000001024 | bytes 1000000 | tf_op jit(solution)/shard_map/attend_first/pallas_call | solution.py:454
  41.1 0.0 all-to-all-done.cand_ref
  41.1 9.3 %all-to-all-start.1 = ((bf16[32,32,512]{2,1,0:T(8,128)(2,1)}), bf16[32,32,512]{2,1,0:T(8,128)(2,1)}, u32[]{:S(2)}, u32[]{:S(2)}) async-start(bf16[32,32,512]{2,1,0:T(8,128)(2,1)} %bitcast.29), calls=%async_computation.1 | async-start | bytes 2097152 | tf_op jit(solution)/shard_map/all_to_all | solution.py:389
  50.5 0.0 collective-permute-done.1.k1.v1
  50.5 0.0 collective-permute-done.3.k2.v2
  50.5 6.3 %collective-permute-done.5.k3.v3 = bf16[2048,128]{1,0:T(8,128)(2,1)} collective-permute-done((bf16[2048,128]{1,0:T(8,128)(2,1)}, bf16[2048,128]{1,0:T(8,128)(2,1)}, u32[]{:S(2)}, u32[]{:S(2)}) %collective-permute-start.5) | collective-permute-done | bytes 524320 | tf_op jit(solution)/shard_map/ppermute | solution.py:356
  56.8 0.0 copy-start.1
  56.8 7.8 %attend_last.1 = (bf16[32,144,128]{2,1,0:T(8,128)(2,1)}, bf16[256,1024]{1,0:T(8,128)(2,1)}) custom-call(s32[1]{0:T(128)} %bitcast.2.me_ref, s32[2]{0:T(128)} %hist_ref.3, f32[8,4]{1,0:T(8,128)} %copy.18.bias_ref, s32[256,1]{1,0:T(8,128)} %copy.19.req_ref, bf16[256,1024]{1,0:T(8,128)(2,1)} %get-tuple-element.33.query_ref, bf16[4,256,2048]{2,1,0:T(8,128)(2,1)} %bitcast.26, ...), custom_call_target="tpu_custom_call" | custom-call | flops 99999997952 | bytes 1000000 | tf_op jit(solution)/shard_map/attend_last/pallas_call | solution.py:487
  64.6 3.1 %all-to-all-done.1.stuff_ref = bf16[32,32,512]{2,1,0:T(8,128)(2,1)} async-done(((bf16[32,32,512]{2,1,0:T(8,128)(2,1)}), bf16[32,32,512]{2,1,0:T(8,128)(2,1)}, u32[]{:S(2)}, u32[]{:S(2)}) %all-to-all-start.1) | async-done | bytes 1048608 | tf_op jit(solution)/shard_map/all_to_all | solution.py:389
  67.7 5.8 %all-to-all-start.2 = ((bf16[32,144,128]{2,1,0:T(8,128)(2,1)}), bf16[32,144,128]{2,1,0:T(8,128)(2,1)}, u32[]{:S(2)}, u32[]{:S(2)}) async-start(bf16[32,144,128]{2,1,0:T(8,128)(2,1)} %get-tuple-element.48), calls=%async_computation.2 | async-start | bytes 2359296 | tf_op jit(solution)/shard_map/all_to_all | solution.py:389
  73.5 0.0 copy-done.1
  73.5 0.6 pad.4.tower_ref
  74.2 7.9 %tower.1.tower_ref = bf16[16,4096]{1,0:T(8,128)(2,1)} custom-call(bf16[1,4096,1024]{2,1,0:T(8,128)(2,1)} %down_ref.1, bf16[16,1024]{1,0:T(8,128)(2,1)} %pad.4.tower_ref), custom_call_target="tpu_custom_call" | custom-call | flops 100000000 | bytes 9000000 | tf_op jit(solution)/shard_map/tower/pallas_call | solution.py:415
  82.1 9.2 %all-to-all-done.2.last_ref = bf16[32,144,128]{2,1,0:T(8,128)(2,1)} async-done(((bf16[32,144,128]{2,1,0:T(8,128)(2,1)}), bf16[32,144,128]{2,1,0:T(8,128)(2,1)}, u32[]{:S(2)}, u32[]{:S(2)}) %all-to-all-start.2) | async-done | bytes 1179680 | tf_op jit(solution)/shard_map/all_to_all | solution.py:389
  91.3 15.2 %expert.1 = f32[32,8,128]{2,1,0:T(8,128)} custom-call(bf16[32,32,512]{2,1,0:T(8,128)(2,1)} %all-to-all-done.cand_ref, bf16[32,32,512]{2,1,0:T(8,128)(2,1)} %all-to-all-done.1.stuff_ref, bf16[32,144,128]{2,1,0:T(8,128)(2,1)} %all-to-all-done.2.last_ref, bf16[1,1024,4096]{2,1,0:T(8,128)(2,1)} %up_ref.1, bf16[16,4096]{1,0:T(8,128)(2,1)} %tower.1.tower_ref), custom_call_target="tpu_custom_call" | custom-call | flops 11000000512 | bytes 13000000 | tf_op jit(solution)/shard_map/expert/pallas_call | solution.py:526
  106.5 5.1 %all-to-all-start.3 = ((f32[32,8,128]{2,1,0:T(8,128)}), f32[32,8,128]{2,1,0:T(8,128)S(1)}, u32[]{:S(2)}, u32[]{:S(2)}) async-start(f32[32,8,128]{2,1,0:T(8,128)} %expert.1), calls=%async_computation.3 | async-start | bytes 262144 | tf_op jit(solution)/shard_map/all_to_all | solution.py:389
  111.6 2.4 %gate.1.weight_ref = f32[256,512]{1,0:T(8,128)} custom-call(s32[2,256]{1,0:T(2,128)} %bitcast.34, bf16[192,1024]{1,0:T(8,128)(2,1)} %bitcast.31, bf16[256,1024]{1,0:T(8,128)(2,1)} %get-tuple-element.45.mixed_ref), custom_call_target="tpu_custom_call" | custom-call | flops 100000000 | bytes 2000000 | tf_op jit(solution)/shard_map/gate/pallas_call | solution.py:518
  114.0 5.3 %all-to-all-done.3 = f32[32,8,128]{2,1,0:T(8,128)S(1)} async-done(((f32[32,8,128]{2,1,0:T(8,128)}), f32[32,8,128]{2,1,0:T(8,128)S(1)}, u32[]{:S(2)}, u32[]{:S(2)}) %all-to-all-start.3) | async-done | bytes 131104 | tf_op jit(solution)/shard_map/all_to_all | solution.py:389
  119.3 0.0 copy-start
  119.3 0.7 copy-done
  120.0 2.1 %combine.1 = f32[6,256]{1,0:T(8,128)} custom-call(bf16[128,512]{1,0:T(8,128)(2,1)} %get-tuple-element.29.slot_ref, f32[256,512]{1,0:T(8,128)} %gate.1.weight_ref, f32[256,128]{1,0:T(8,128)} %bitcast.30), custom_call_target="tpu_custom_call" | custom-call | flops 100000000 | bytes 1000000 | tf_op jit(solution)/shard_map/combine/pallas_call | solution.py:546
Async XLA Ops:
  3.5 27.9 %collective-permute-start = (bf16[2064,128]{1,0:T(8,128)(2,1)}, bf16[2064,128]{1,0:T(8,128)(2,1)S(1)}, u32[]{:S(2)}, u32[]{:S(2)}) collective-permute-start(bf16[2064,128]{1,0:T(8,128)(2,1)} %get-tuple-element.34), channel_id=1, source_target_pairs={{0,32},{32,64},{64,96},{96,0},{1,33},{33,65},{65,97},{97,1},{2,34}... | collective-permute-start | bytes 1585160 | tf_op jit(solution)/shard_map/ppermute | solution.py:356
  5.7 26.2 %collective-permute-start.2 = (bf16[2064,128]{1,0:T(8,128)(2,1)}, bf16[2064,128]{1,0:T(8,128)(2,1)}, u32[]{:S(2)}, u32[]{:S(2)}) collective-permute-start(bf16[2064,128]{1,0:T(8,128)(2,1)} %get-tuple-element.37), channel_id=1, source_target_pairs={{0,96},{32,0},{64,32},{96,64},{1,97},{33,1},{65,33},{97,65},{2,98}... | collective-permute-start | bytes 1585160 | tf_op jit(solution)/shard_map/ppermute | solution.py:356
  7.1 27.0 %collective-permute-start.4 = (bf16[2064,128]{1,0:T(8,128)(2,1)}, bf16[2064,128]{1,0:T(8,128)(2,1)}, u32[]{:S(2)}, u32[]{:S(2)}) collective-permute-start(bf16[2064,128]{1,0:T(8,128)(2,1)} %get-tuple-element.40), channel_id=1, source_target_pairs={{0,64},{32,96},{64,0},{96,32},{1,65},{33,97},{65,1},{97,33},{2,66}... | collective-permute-start | bytes 1585160 | tf_op jit(solution)/shard_map/ppermute | solution.py:356
  11.5 29.7 %all-to-all-start = ((bf16[32,32,512]{2,1,0:T(8,128)(2,1)}), bf16[32,32,512]{2,1,0:T(8,128)(2,1)}, u32[]{:S(2)}, u32[]{:S(2)}) async-start(bf16[32,32,512]{2,1,0:T(8,128)(2,1)} %bitcast.28), calls=%async_computation | async-start | bytes 2097152 | tf_op jit(solution)/shard_map/all_to_all | solution.py:389
  21.0 3.6 %copy-start.3 = (s32[256]{0:T(256)S(1)}, s32[256]{0:T(256)}, u32[]{:S(2)}) copy-start(s32[256]{0:T(256)} %param.14) | copy-start | bytes 3076
  21.0 4.4 %copy-start.2 = (f32[8,4]{0,1:T(4,128)S(1)}, f32[8,4]{0,1:T(4,128)}, u32[]{:S(2)}) copy-start(f32[8,4]{0,1:T(4,128)} %param.19) | copy-start | bytes 388
  31.4 2.8 %copy-start.4 = (bf16[2064,128]{1,0:T(8,128)(2,1)}, bf16[2064,128]{1,0:T(8,128)(2,1)S(1)}, u32[]{:S(2)}) copy-start(bf16[2064,128]{1,0:T(8,128)(2,1)S(1)} %collective-permute-done.k1.v1.t1) | copy-start | bytes 1585156
  31.4 19.0 %collective-permute-start.1 = (bf16[2048,128]{1,0:T(8,128)(2,1)}, bf16[2048,128]{1,0:T(8,128)(2,1)}, u32[]{:S(2)}, u32[]{:S(2)}) collective-permute-start(bf16[2048,128]{1,0:T(8,128)(2,1)} %get-tuple-element.35), channel_id=1, source_target_pairs={{0,32},{32,64},{64,96},{96,0},{1,33},{33,65},{65,97},{97,1},{2,34}... | collective-permute-start | bytes 1572872 | tf_op jit(solution)/shard_map/ppermute | solution.py:356
  31.9 18.6 %collective-permute-start.3 = (bf16[2048,128]{1,0:T(8,128)(2,1)}, bf16[2048,128]{1,0:T(8,128)(2,1)}, u32[]{:S(2)}, u32[]{:S(2)}) collective-permute-start(bf16[2048,128]{1,0:T(8,128)(2,1)} %get-tuple-element.38), channel_id=1, source_target_pairs={{0,96},{32,0},{64,32},{96,64},{1,97},{33,1},{65,33},{97,65},{2,98}... | collective-permute-start | bytes 1572872 | tf_op jit(solution)/shard_map/ppermute | solution.py:356
  34.2 22.6 %collective-permute-start.5 = (bf16[2048,128]{1,0:T(8,128)(2,1)}, bf16[2048,128]{1,0:T(8,128)(2,1)}, u32[]{:S(2)}, u32[]{:S(2)}) collective-permute-start(bf16[2048,128]{1,0:T(8,128)(2,1)} %get-tuple-element.41), channel_id=1, source_target_pairs={{0,64},{32,96},{64,0},{96,32},{1,65},{33,97},{65,1},{97,33},{2,66}... | collective-permute-start | bytes 1572872 | tf_op jit(solution)/shard_map/ppermute | solution.py:356
  41.1 26.6 %all-to-all-start.1 = ((bf16[32,32,512]{2,1,0:T(8,128)(2,1)}), bf16[32,32,512]{2,1,0:T(8,128)(2,1)}, u32[]{:S(2)}, u32[]{:S(2)}) async-start(bf16[32,32,512]{2,1,0:T(8,128)(2,1)} %bitcast.29), calls=%async_computation.1 | async-start | bytes 2097152 | tf_op jit(solution)/shard_map/all_to_all | solution.py:389
  56.8 16.8 %copy-start.1 = (bf16[1024,6]{0,1:T(8,128)(2,1)S(1)}, bf16[1024,6]{0,1:T(8,128)(2,1)}, u32[]{:S(2)}) copy-start(bf16[1024,6]{0,1:T(8,128)(2,1)} %param.25) | copy-start | bytes 36868
  67.7 23.6 %all-to-all-start.2 = ((bf16[32,144,128]{2,1,0:T(8,128)(2,1)}), bf16[32,144,128]{2,1,0:T(8,128)(2,1)}, u32[]{:S(2)}, u32[]{:S(2)}) async-start(bf16[32,144,128]{2,1,0:T(8,128)(2,1)} %get-tuple-element.48), calls=%async_computation.2 | async-start | bytes 2359296 | tf_op jit(solution)/shard_map/all_to_all | solution.py:389
  106.5 12.8 %all-to-all-start.3 = ((f32[32,8,128]{2,1,0:T(8,128)}), f32[32,8,128]{2,1,0:T(8,128)S(1)}, u32[]{:S(2)}, u32[]{:S(2)}) async-start(f32[32,8,128]{2,1,0:T(8,128)} %expert.1), calls=%async_computation.3 | async-start | bytes 262144 | tf_op jit(solution)/shard_map/all_to_all | solution.py:389
  119.3 0.7 copy-start

commit v3 on v2

v3 whole, which is shorter than its diff:
```python
import functools
import math

import jax
import jax.numpy as jnp
from jax import lax
from jax.experimental import pallas as pl
from jax.experimental.pallas import tpu as pltpu
from jax.sharding import PartitionSpec as P

EPSILON = 1e-05
F32 = jnp.float32
BF16 = jnp.bfloat16
NT = (((1,), (1,)), ((), ()))
TN = (((0,), (0,)), ((), ()))
SHIFTS = (1, 3, 2)
LIMIT = 63 * 2**20
AHEAD = 3
FIRST_COST = 30 * 10**9
EARLY_COST = 5 * 10**9
LAST_COST = 100 * 10**9


def pack_kernel(me_ref, ids_ref, *refs):
    count = len(SHIFTS)
    ins, outs = refs[: 2 * count], refs[2 * count :]
    keys = ins[0].shape[1]
    heads = ins[0].shape[2] // 128
    for n, shift in enumerate(SHIFTS):
        for head in range(heads):
            cols = pl.ds(head * 128, 128)
            outs[n][pl.ds(head * keys, keys), :] = ins[2 * n][0, :, cols]
            outs[n][pl.ds((heads + head) * keys, keys), :] = ins[2 * n + 1][0, :, cols]
    if len(outs) > count:
        row = lax.broadcasted_iota(jnp.int32, (16, 128), 0)
        me = me_ref[0]

        def tile_of(owner):
            first = ids_ref[2 * owner].astype(F32)
            second = ids_ref[2 * owner + 1].astype(F32)
            return jnp.where(row == 0, first, second).astype(BF16)

        for n, shift in enumerate(SHIFTS):
            outs[n][pl.ds(2 * heads * keys, 16), :] = tile_of(lax.rem(me + shift, count + 1))
        outs[count][...] = tile_of(me)


def route_kernel(capacity, lane_ref, ids_ref, req_ref, cand_ref, place_ref, slot_ref, first_ref, out_ref):
    rows = ids_ref.shape[1]
    experts = place_ref.shape[0] // capacity
    ids = jnp.concatenate([ids_ref[0:1, :], ids_ref[1:2, :]], axis=1)
    hot = lax.broadcasted_iota(jnp.int32, (experts, 2 * rows), 0) == ids
    hot = jnp.where(hot, 1.0, 0.0)
    here = lax.broadcasted_iota(jnp.int32, (2 * rows, 2 * rows), 0)
    there = lax.broadcasted_iota(jnp.int32, (2 * rows, 2 * rows), 1)
    earlier = jnp.where(here < there, 1.0, 0.0).astype(BF16)
    counts = jnp.dot(hot.astype(BF16), earlier, preferred_element_type=F32)
    position = jnp.sum(counts * hot, axis=0, keepdims=True).astype(jnp.int32)
    slot = ids * capacity + position
    spot = lax.broadcasted_iota(jnp.int32, place_ref.shape, 0)
    place = (spot == slot[:, :rows]) | (spot == slot[:, rows:])
    place = jnp.where(place, 1.0, 0.0).astype(BF16)
    place_ref[...] = place
    lane = position + lane_ref[0]
    lanes = lax.broadcasted_iota(jnp.int32, slot_ref.shape, 0) == lane
    slot_ref[...] = jnp.where(lanes, 1.0, 0.0).astype(BF16)
    out_ref[...] = jnp.dot(place, cand_ref[...], preferred_element_type=F32).astype(BF16)
    first = jnp.where(req_ref[...] == 0, 1.0, 0.0)
    first_ref[...] = jnp.transpose(jnp.broadcast_to(first, (128, rows))).astype(BF16)


def project_kernel(cand_ref, weight_ref, gain_ref, query_ref, update_ref):
    step = pl.program_id(0)
    half = pl.num_programs(0) // 2
    projected = jnp.dot(cand_ref[...], weight_ref[...], preferred_element_type=F32)

    @pl.when(step < half)
    def _():
        query_ref[...] = projected.astype(BF16)

    @pl.when(step >= half)
    def _():
        update_ref[...] = gain_ref[...] * projected / (1.0 + jnp.exp(-projected))


def tower_kernel(down_at, tower_ref, out_ref, down, sems):
    count, tile, _ = down.shape
    loads = []
    for i in range(count):
        here = pl.ds(i * tile, tile)
        loads.append(pltpu.make_async_copy(down_at.at[0, here, :], down.at[i], sems.at[i]))
    for i in range(2):
        loads[i].start()
    for i in range(count):
        if i + 2 < count:
            loads[i + 2].start()
        loads[i].wait()
        product = lax.dot_general(tower_ref[...], down[i], NT, preferred_element_type=F32)
        high = product.astype(BF16)
        low = (product - high.astype(F32)).astype(BF16)
        out_ref[:, pl.ds(i * tile, tile)] = jnp.concatenate([high[0:8], low[0:8]], axis=0)


def attend_head(head, first, mask, query, key, value, blocks, bias_ref):
    scores = lax.dot_general(query, key, NT, preferred_element_type=F32)
    weights = []
    for owner, (block_a, block_b) in enumerate(blocks):
        here = scores[:, owner * 256 : (owner + 1) * 256]
        here = jnp.where(first, here[:, :128], here[:, 128:])
        bias_a = jnp.zeros_like(block_a)
        bias_b = jnp.zeros_like(block_b)
        for block in range(bias_ref.shape[0]):
            entry = bias_ref[block, head] * 0.5
            bias_a = jnp.where(block_a == block, entry, bias_a)
            bias_b = jnp.where(block_b == block, entry, bias_b)
        half = here * (0.5 / math.sqrt(128.0)) + jnp.where(first, bias_a, bias_b)
        weight = (half + half * jnp.tanh(half)).astype(BF16)
        weights += [weight, weight]
    weights = jnp.concatenate(weights, axis=1) * mask
    return jnp.dot(weights, value, preferred_element_type=F32)


def attend_kernel(chunk, me_ref, hist_ref, bias_ref, *refs):
    last = chunk == 1
    query_at, cache_at, *refs = refs
    moved_at, refs = refs[:3], refs[3:]
    ids_at, refs = refs[:3], refs[3:]
    own_at, first_at, update_at, place_at, *refs = refs
    if last:
        cand_at, stuff_at, square_at, *refs = refs
        out_at, mixed_at, *refs = refs
    else:
        out_at, stuff_at, square_at, *refs = refs
    sems, kv, tiles, query, first_in, update, place, square, stuff, out, *refs = refs
    if last:
        cand, mixed, attended = refs
    owners, keys, width = cache_at.shape
    parts = kv.shape[0]
    heads = parts // 2
    early = heads * 128
    base = chunk * heads
    rows = query.shape[0]
    me = me_ref[0]
    used = []

    def copy(source, target):
        item = pltpu.make_async_copy(source, target, sems.at[len(used)])
        item.start()
        used.append(item)
        return item

    wanted = [copy(query_at.at[:, pl.ds(base * 128, early)], query)]
    wanted.append(copy(first_at, first_in))
    wanted.append(copy(own_at, tiles.at[0]))
    for n in range(3):
        wanted.append(copy(ids_at[n].at[pl.ds(parts * keys, 16), :], tiles.at[n + 1]))
    loads = []
    for head in range(heads):
        load = []
        for half in range(2):
            part = half * heads + head
            col = half * (width // 2) + (base + head) * 128
            load.append(copy(cache_at.at[me, :, pl.ds(col, 128)], kv.at[part, 0]))
            for n in range(3):
                load.append(copy(moved_at[n].at[pl.ds(part * keys, keys), :], kv.at[part, n + 1]))
        loads.append(load)
        if head == 0:
            later = [copy(update_at.at[:, pl.ds(base * 128, early)], update), copy(place_at, place)]
    if last:
        later += [copy(cand_at, cand), copy(stuff_at, stuff), copy(square_at, square)]
    for item in wanted:
        item.wait()
    first = first_in[...].astype(F32) > 0.5
    length_a = hist_ref[0].astype(F32)
    length_b = hist_ref[1].astype(F32)
    blocks = []
    masks = []
    for owner in range(owners):
        tile = tiles[owner].astype(F32)
        block_a, block_b = tile[0:1, :], tile[1:2, :]
        blocks.append((block_a, block_b))
        mask_a = jnp.where(first, jnp.where(block_a < length_a, 1.0, 0.0), 0.0)
        mask_b = jnp.where(first, 0.0, jnp.where(block_b < length_b, 1.0, 0.0))
        masks += [mask_a.astype(BF16), mask_b.astype(BF16)]
    mask = jnp.concatenate(masks, axis=1)
    total = None
    stores = []
    for load in loads:
        for item in load:
            item.wait()
    for item in later:
        item.wait()
    for head in range(heads):
        cols = pl.ds(head * 128, 128)
        key = kv[head].reshape(owners * keys, 128)
        value = kv[heads + head].reshape(owners * keys, 128)
        found = attend_head(base + head, first, mask, query[:, cols], key, value, blocks, bias_ref)
        total = found * found if total is None else total + found * found
        if last:
            attended[:, cols] = found * update[:, cols]
            continue
        stuff[:, cols] = (found * update[:, cols]).astype(BF16)
        if head % 2 == 1:
            here = pl.ds((head - 1) * 128, 256)
            out[:, here] = jnp.dot(place[...], stuff[:, here], preferred_element_type=F32).astype(BF16)
            stores.append(copy(out.at[:, here], out_at.at[:, here]))
    if not last:
        square[...] = total
        stores.append(copy(stuff, stuff_at))
        stores.append(copy(square, square_at))
        for item in stores:
            item.wait()
        return
    feature = cand.shape[1]
    mean = jnp.sum(total + square[...], axis=1, keepdims=True) * (1.0 / feature)
    inv_rms = lax.rsqrt(mean + EPSILON)
    peers = out.shape[0]
    share = place.shape[0] // peers
    for i in range(heads // 2):
        cols = pl.ds(early + i * 256, 256)
        block = cand[:, cols].astype(F32) + attended[:, pl.ds(i * 256, 256)] * inv_rms
        block = block.astype(BF16)
        mixed[:, cols] = block
        sent = jnp.dot(place[...], block, preferred_element_type=F32).astype(BF16)
        for j in range(2):
            here = pl.ds((2 * i + j) * share, share)
            out[:, here, :] = sent[:, j * 128 : (j + 1) * 128].reshape(peers, share, 128)
    scale = jnp.transpose(jnp.broadcast_to(inv_rms, (rows, 128)))[0:16, :]
    high = scale.astype(BF16).astype(F32)
    row = lax.broadcasted_iota(jnp.int32, scale.shape, 0)
    scale = jnp.where(row == 0, high, jnp.where(row == 1, scale - high, 0.0)).astype(BF16)
    scale = lax.dot_general(scale, place[...], NT, preferred_element_type=F32)
    each = 128 // share
    for peer in range(peers):
        tile = scale[:, (peer // each) * 128 : (peer // each + 1) * 128]
        if peer % each:
            tile = pltpu.roll(tile, 128 - (peer % each) * share, 1)
        out[peer, pl.ds(heads * share, 16), :] = tile.astype(BF16)
    stores.append(copy(out, out_at))
    mixed[:, :early] = (cand[:, :early].astype(F32) + stuff[...].astype(F32) * inv_rms).astype(BF16)
    stores.append(copy(mixed, mixed_at))
    for item in stores:
        item.wait()


def gate_kernel(tasks, ids_ref, weight_ref, mixed_ref, out_ref):
    rows = mixed_ref.shape[0]
    experts = weight_ref.shape[0] // tasks
    logits = lax.dot_general(weight_ref[...], mixed_ref[...], NT, preferred_element_type=F32)
    squashed = []
    for k in range(2):
        hot = lax.broadcasted_iota(jnp.int32, (experts, rows), 0) == ids_ref[k : k + 1, :]
        picked = []
        for task in range(8):
            if task < tasks:
                here = logits[task * experts : (task + 1) * experts, :]
                picked.append(jnp.sum(jnp.where(hot, here, 0.0), axis=0, keepdims=True))
            else:
                picked.append(jnp.zeros((1, rows), F32))
        squashed.append(jax.nn.sigmoid(jnp.concatenate(picked, axis=0)))
    whole = squashed[0] + squashed[1]
    for k in range(2):
        gates = squashed[k] / whole
        ids = ids_ref[k : k + 1, :]
        for expert in range(experts):
            out_ref[pl.ds(expert * 8, 8), pl.ds(k * rows, rows)] = jnp.where(ids == expert, gates, 0.0)


def early_kernel(rows_at, up_at, out_at, rows, up, turned, out, sems):
    peers, share, early = rows.shape
    count, _, tile = up.shape
    fetch = pltpu.make_async_copy(rows_at, rows, sems.at[0])
    fetch.start()
    ups = []
    for i in range(count):
        here = pl.ds(i * tile, tile)
        ups.append(pltpu.make_async_copy(up_at.at[0, pl.ds(0, early), here], up.at[i], sems.at[i + 1]))
    ups[0].start()
    fetch.wait()
    for i in range(early // 128):
        cols = pl.ds(i * 128, 128)
        block = rows[:, :, cols].reshape(peers * share, 128)
        turned[cols, :] = jnp.transpose(block * jnp.asarray(0.5, BF16))
    stores = []
    for i in range(count):
        ups[i].wait()
        if i + 1 < count:
            ups[i + 1].start()
        found = lax.dot_general(up[i], turned[...], TN, preferred_element_type=F32)
        out[i] = found.astype(BF16)
        store = pltpu.make_async_copy(out.at[i], out_at.at[pl.ds(i * tile, tile), :], sems.at[count + 1 + i])
        store.start()
        stores.append(store)
    for store in stores:
        store.wait()


def expert_kernel(
    last_at, cand_at, stuff_at, up_at, tower_at, out_ref, last, cand, stuff, up, tower, turned, scale, sems
):
    count, late, tile = up.shape
    peers = last.shape[0]
    share = (last.shape[1] - 16) // (late // 128)
    rows = peers * share
    each = 128 // share
    fetch = pltpu.make_async_copy(last_at, last, sems.at[0])
    fetch.start()
    loads = []
    for i in range(count):
        here = pl.ds(i * tile, tile)
        loads.append(
            (
                pltpu.make_async_copy(up_at.at[0, pl.ds(late, late), here], up.at[i], sems.at[3 * i + 2]),
                pltpu.make_async_copy(cand_at.at[here, :], cand.at[i], sems.at[3 * i + 3]),
                pltpu.make_async_copy(stuff_at.at[here, :], stuff.at[i], sems.at[3 * i + 4]),
            )
        )
    fetch_tower = pltpu.make_async_copy(tower_at, tower, sems.at[1])
    fetch_tower.start()
    for ahead in range(AHEAD):
        for item in loads[ahead]:
            item.start()
    fetch.wait()
    for i in range(late // 128):
        block = last[:, pl.ds(i * share, share), :].reshape(rows, 128)
        turned[pl.ds(i * 128, 128), :] = jnp.transpose(block * jnp.asarray(0.5, BF16))
    lane = lax.broadcasted_iota(jnp.int32, (16, 128), 1)
    for group in range(peers // each):
        whole_tile = None
        for i in range(each):
            part = last[group * each + i, pl.ds(late // 128 * share, 16), :].astype(F32)
            part = pltpu.roll(part, i * share, 1) if i else part
            part = jnp.where((lane >= i * share) & (lane < (i + 1) * share), part, 0.0)
            whole_tile = part if whole_tile is None else whole_tile + part
        scale[:, pl.ds(group * 128, 128)] = whole_tile[0:1, :] + whole_tile[1:2, :]
    fetch_tower.wait()
    total = None
    for i in range(count):
        if i + AHEAD < count:
            for item in loads[i + AHEAD]:
                item.start()
        for item in loads[i]:
            item.wait()
        half = lax.dot_general(up[i], turned[...], TN, preferred_element_type=F32)
        half = half + cand[i].astype(F32) + stuff[i].astype(F32) * scale[...]
        hidden = (half + half * jnp.tanh(half)).astype(BF16)
        part = jnp.dot(tower[:, pl.ds(i * tile, tile)], hidden, preferred_element_type=F32)
        total = part if total is None else total + part
    found = total[0:8, :] + total[8:16, :]
    for peer in range(peers):
        out_ref[peer] = found[:, (peer // each) * 128 : (peer // each + 1) * 128]


def combine_kernel(slot_ref, weight_ref, back_ref, out_ref):
    rows = slot_ref.shape[1] // 2
    hot = slot_ref[...]
    back = back_ref[...]
    high = back.astype(BF16)
    rest = back - high.astype(F32)
    middle = rest.astype(BF16)
    low = (rest - middle.astype(F32)).astype(BF16)
    found = jnp.dot(high, hot, preferred_element_type=F32)
    found += jnp.dot(middle, hot, preferred_element_type=F32)
    found += jnp.dot(low, hot, preferred_element_type=F32)
    found = found * weight_ref[...]
    found = found[:, :rows] + found[:, rows:]
    total = found[0:8]
    for expert in range(1, found.shape[0] // 8):
        total = total + found[expert * 8 : (expert + 1) * 8]
    out_ref[...] = total[: out_ref.shape[0]]


def params():
    return pltpu.CompilerParams(vmem_limit_bytes=LIMIT)


def cost(flops, bytes_accessed, transcendentals=0):
    return pl.CostEstimate(flops=flops, bytes_accessed=bytes_accessed, transcendentals=transcendentals)


def whole(*shape):
    return pl.BlockSpec(shape, lambda i, *_: (0,) * len(shape))


def local(
    cand_emb,
    cand_request,
    hist_blocks,
    cache_kv,
    block_map,
    w_query_update,
    rel_bias,
    norm_gain,
    w_gate,
    expert_ids,
    w_up,
    w_down,
    w_tower,
):
    rows, feature = cand_emb.shape
    owners = lax.axis_size("req")
    me = lax.axis_index("req").astype(jnp.int32)
    head_count = rel_bias.shape[0]
    tasks = w_tower.shape[1]
    experts = w_gate.shape[1] // tasks
    capacity = 2 * rows * expert_ids.shape[1] // experts
    slots = experts * capacity
    heads = head_count // 2
    early = heads * 128
    keys = cache_kv.shape[0] // owners * cache_kv.shape[1]
    parts = 2 * heads
    me_scalar = me[None]
    smem = pl.BlockSpec(memory_space=pltpu.SMEM)

    cache = cache_kv.reshape(owners, keys, 2 * feature)

    def pack(chunk):
        def block(shift, half):
            return pl.BlockSpec(
                (1, keys, early),
                lambda i, me, ids: (lax.rem(me[0] + shift, owners), 0, 2 * half + chunk),
            )

        tail = 16 if chunk == 0 else 0
        shapes = [jax.ShapeDtypeStruct((parts * keys + tail, 128), BF16)] * len(SHIFTS)
        if chunk == 0:
            shapes.append(jax.ShapeDtypeStruct((16, 128), BF16))
        blocks = [block(shift, half) for shift in SHIFTS for half in range(2)]
        return pl.pallas_call(
            pack_kernel,
            grid_spec=pltpu.PrefetchScalarGridSpec(
                num_scalar_prefetch=2,
                grid=(1,),
                in_specs=blocks,
                out_specs=[whole(*shape.shape) for shape in shapes],
            ),
            out_shape=shapes,
            compiler_params=params(),
            cost_estimate=cost(0, 10**6),
            name="pack",
        )(me_scalar, block_map, *[cache] * len(blocks))

    def send(item, shift):
        pairs = [(i, (i + shift) % owners) for i in range(owners)]
        return lax.ppermute(item, "req", pairs)

    *packed, own_tile = pack(0)
    first_moved = [send(item, shift) for item, shift in zip(packed, SHIFTS)]
    packed_last = pack(1)
    last_moved = []
    for item, ahead, shift in zip(packed_last, first_moved, SHIFTS):
        item, _ = lax.optimization_barrier((item, ahead))
        last_moved.append(send(item, shift))

    ids_rows, _ = lax.optimization_barrier((expert_ids.T, own_tile))
    each = 128 // capacity
    lane = lax.rem(lax.axis_index("exp").astype(jnp.int32), each) * capacity
    place, slot_hot, first, cand_out = pl.pallas_call(
        functools.partial(route_kernel, capacity),
        grid=(1,),
        in_specs=[
            smem,
            whole(2, rows),
            whole(1, rows),
            pl.BlockSpec((rows, early), lambda i: (0, 0)),
        ],
        out_specs=[whole(slots, rows), whole(128, 2 * rows), whole(rows, 128), whole(slots, early)],
        out_shape=[
            jax.ShapeDtypeStruct((slots, rows), BF16),
            jax.ShapeDtypeStruct((128, 2 * rows), BF16),
            jax.ShapeDtypeStruct((rows, 128), BF16),
            jax.ShapeDtypeStruct((slots, early), BF16),
        ],
        compiler_params=params(),
        cost_estimate=cost(5 * 10**8, 3 * 10**6),
        name="route",
    )(lane[None], ids_rows, cand_request[None, :], cand_emb)

    def exchange(item):
        return lax.all_to_all(item, "exp", split_axis=0, concat_axis=0, tiled=True)

    cand_in = exchange(cand_out.reshape(experts, capacity, early))

    cand_rows, _, _ = lax.optimization_barrier((cand_emb, place, packed_last[0]))
    steps = 4
    wide = 2 * feature // steps
    queries, update = pl.pallas_call(
        project_kernel,
        grid=(steps,),
        in_specs=[
            whole(rows, feature),
            pl.BlockSpec((feature, wide), lambda i: (0, i)),
            pl.BlockSpec((1, wide), lambda i: (0, jnp.maximum(i - 2, 0))),
        ],
        out_specs=[
            pl.BlockSpec((rows, wide), lambda i: (0, jnp.minimum(i, 1))),
            pl.BlockSpec((rows, wide), lambda i: (0, jnp.maximum(i - 2, 0))),
        ],
        out_shape=[
            jax.ShapeDtypeStruct((rows, feature), BF16),
            jax.ShapeDtypeStruct((rows, feature), F32),
        ],
        compiler_params=params(),
        cost_estimate=cost(11 * 10**8, 6 * 10**6, 2**18),
        name="project",
    )(cand_rows, w_query_update, norm_gain[None, :])

    hidden_count = w_up.shape[2]
    tile = 512
    towers = pl.pallas_call(
        tower_kernel,
        in_specs=[pl.BlockSpec(memory_space=pl.ANY), pl.BlockSpec(memory_space=pltpu.VMEM)],
        out_shape=jax.ShapeDtypeStruct((16, hidden_count), BF16),
        scratch_shapes=[
            pltpu.VMEM((hidden_count // tile, tile, feature), BF16),
            pltpu.SemaphoreType.DMA((hidden_count // tile,)),
        ],
        compiler_params=params(),
        cost_estimate=cost(10**8, 9 * 10**6),
        name="tower",
    )(w_down, jnp.pad(w_tower.T, ((0, 16 - tasks), (0, 0))))

    anywhere = pl.BlockSpec(memory_space=pl.ANY)
    hbm = pl.BlockSpec(memory_space=pltpu.HBM)

    def attend(chunk, moved, extra, out_shape, extra_scratch, name, flops):
        arrays = [queries, cache, *moved, *first_moved, own_tile, first, update, place, *extra]
        out_rows = out_shape[0].shape
        return pl.pallas_call(
            functools.partial(attend_kernel, chunk),
            in_specs=[smem] * 3 + [anywhere] * 2 + [hbm] * 6 + [anywhere] * (len(arrays) - 8),
            out_specs=[anywhere] * len(out_shape),
            out_shape=out_shape,
            scratch_shapes=[
                pltpu.SemaphoreType.DMA((16 + 8 * heads,)),
                pltpu.VMEM((parts, owners, keys, 128), BF16),
                pltpu.VMEM((owners, 16, 128), BF16),
                pltpu.VMEM((rows, early), BF16),
                pltpu.VMEM((rows, 128), BF16),
                pltpu.VMEM((rows, early), F32),
                pltpu.VMEM((slots, rows), BF16),
                pltpu.VMEM((rows, 128), F32),
                pltpu.VMEM((rows, early), BF16),
                pltpu.VMEM(out_rows, BF16),
                *extra_scratch,
            ],
            compiler_params=params(),
            cost_estimate=cost(flops, 10**6),
            name=name,
        )(me_scalar, hist_blocks, rel_bias.T, *arrays)

    stuff_out, stuff, square = attend(
        0,
        first_moved,
        [],
        [
            jax.ShapeDtypeStruct((slots, early), BF16),
            jax.ShapeDtypeStruct((rows, early), BF16),
            jax.ShapeDtypeStruct((rows, 128), F32),
        ],
        [],
        "attend_first",
        FIRST_COST,
    )
    stuff_in = exchange(stuff_out.reshape(experts, capacity, early))

    def early_product(item, name):
        count = 4
        wide = hidden_count // count
        return pl.pallas_call(
            early_kernel,
            in_specs=[hbm, anywhere],
            out_specs=anywhere,
            out_shape=jax.ShapeDtypeStruct((hidden_count, slots), BF16),
            scratch_shapes=[
                pltpu.VMEM((experts, capacity, early), BF16),
                pltpu.VMEM((count, early, wide), BF16),
                pltpu.VMEM((early, slots), BF16),
                pltpu.VMEM((count, wide, slots), BF16),
                pltpu.SemaphoreType.DMA((2 * count + 1,)),
            ],
            compiler_params=params(),
            cost_estimate=cost(EARLY_COST, 10**6),
            name=name,
        )(item, w_up)

    cand_product = early_product(cand_in, "early_cand")
    square, _ = lax.optimization_barrier((square, cand_product))
    last_rows = heads * capacity + 16
    last_out, mixed_rows = attend(
        1,
        last_moved,
        [cand_emb, stuff, square],
        [
            jax.ShapeDtypeStruct((experts, last_rows, 128), BF16),
            jax.ShapeDtypeStruct((rows, feature), BF16),
        ],
        [
            pltpu.VMEM((rows, feature), BF16),
            pltpu.VMEM((rows, feature), BF16),
            pltpu.VMEM((rows, early), F32),
        ],
        "attend_last",
        LAST_COST,
    )
    last_in = exchange(last_out)
    stuff_product = early_product(stuff_in, "early_stuff")

    gates = pl.pallas_call(
        functools.partial(gate_kernel, tasks),
        out_shape=jax.ShapeDtypeStruct((experts * 8, 2 * rows), F32),
        compiler_params=params(),
        cost_estimate=cost(10**8, 2 * 10**6, 4096),
        name="gate",
    )(ids_rows, w_gate.T, mixed_rows)

    late = feature - early
    late = feature - early
    count = hidden_count // tile
    produced = pl.pallas_call(
        expert_kernel,
        in_specs=[hbm, anywhere, anywhere, anywhere, anywhere],
        out_shape=jax.ShapeDtypeStruct((experts, 8, 128), F32),
        scratch_shapes=[
            pltpu.VMEM((experts, last_rows, 128), BF16),
            pltpu.VMEM((count, tile, slots), BF16),
            pltpu.VMEM((count, tile, slots), BF16),
            pltpu.VMEM((count, late, tile), BF16),
            pltpu.VMEM((16, hidden_count), BF16),
            pltpu.VMEM((late, slots), BF16),
            pltpu.VMEM((1, slots), F32),
            pltpu.SemaphoreType.DMA((3 * count + 2,)),
        ],
        compiler_params=params(),
        cost_estimate=cost(6 * 10**9, 25 * 10**6, 2**22),
        name="expert",
    )(last_in, cand_product, stuff_product, w_up, towers)

    came_back = exchange(produced)

    scores = pl.pallas_call(
        combine_kernel,
        out_shape=jax.ShapeDtypeStruct((tasks, rows), F32),
        compiler_params=params(),
        cost_estimate=cost(10**8, 10**6),
        name="combine",
    )(slot_hot, gates, came_back.reshape(experts * 8, 128))
    return scores.T


def solution(mesh):
    placed = (
        P(("req", "exp"), None),
        P(("req", "exp")),
        P(("req", "exp")),
        P(("req", "exp"), None, None),
        P(("req", "exp")),
        P(),
        P(),
        P(),
        P(),
        P(("req", "exp"), None),
        P("exp", None, None),
        P("exp", None, None),
        P(),
    )
    return jax.shard_map(
        local, mesh=mesh, in_specs=placed, out_specs=P(("req", "exp"), None), check_vma=False
    )
```

time: 123 us -> 119 us (0.967)
  waiting for transfers between devices: 23.9 us -> 8.32 us
  Pallas kernels: 57.5 us -> 67.8 us
  starting transfers between devices: 37.7 us -> 40.5 us
  local copies, waits for them, and re-layouts: 2.76 us -> 1.28 us
    pallas_call x5 -> x7, Pallas kernels: 43.2 us -> 53.6 us  [the longest x2 17.6 us: early_product(): pl.pallas_call(early_kernel, in_specs=[hbm, anywhere], out_specs=anywhere...]
    all_to_all x4, waiting for transfers between devices: 17.6 us -> 8.31 us  [exchange(): return lax.all_to_all(item, 'exp', split_axis=0, concat_axis=0, tiled=True)]
    ppermute x6, waiting for transfers between devices: 6.3 us -> 0.02 us  [send(): return lax.ppermute(item, 'req', pairs)]
    all_to_all x4, starting transfers between devices: 29.7 us -> 32.5 us  [exchange(): return lax.all_to_all(item, 'exp', split_axis=0, concat_axis=0, tiled=True)]
  transfers between devices with their start and end apart: 10 -> 10, of which waited for: 4 -> 3; matrix products, arithmetic and copies ran while one was open for 2% -> 1% of each run, Pallas kernels for 30% -> 43%
where the time goes in v3:
time: 119 us; the launch traced here: 118 us
  Pallas kernels  67.8 us (57%)
  starting transfers between devices  40.5 us (34%)
  waiting for transfers between devices  8.32 us (7%)
  local copies, waits for them, and re-layouts  1.28 us (1%)
    all_to_all x4, starting transfers between devices, exchange(): return lax.all_to_all(item, 'exp', split_axis=0, concat_axis=0, tiled=True)  32.5 us
    pallas_call x2, Pallas kernels, early_product(): pl.pallas_call(early_kernel, in_specs=[hbm, anywhere], out_specs=anywhere...  17.6 us
    pallas_call x2, Pallas kernels, attend(): pl.pallas_call(functools.partial(attend_kernel, chunk), in_specs=[smem] *...  12.9 us
    pallas_call x1, Pallas kernels, local(): pl.pallas_call(expert_kernel, in_specs=[hbm, anywhere, anywhere, anywhere...  11.1 us
    all_to_all x4, waiting for transfers between devices, exchange(): return lax.all_to_all(item, 'exp', split_axis=0, concat_axis=0, tiled=True)  8.31 us
    ppermute x6, starting transfers between devices, send(): return lax.ppermute(item, 'req', pairs)  8.01 us
    pallas_call x2, Pallas kernels, pack(): pl.pallas_call(pack_kernel, grid_spec=pltpu.PrefetchScalarGridSpec(num_sc...  7 us
    pallas_call x1, Pallas kernels, local(): pl.pallas_call(tower_kernel, in_specs=[pl.BlockSpec(memory_space=pl.ANY),...  6.62 us
  transfers between devices with their start and end apart: 10, of which 3 were waited for; matrix products, arithmetic and copies ran while one was open for 1% of the time, Pallas kernels for 43%

profile of v3, /device:TPU:1, one launch (start us, length us, event | category | flops | bytes accessed | tf_op | source)
XLA Modules:
  0.0 118.0 jit_solution(13440447560505736148)
XLA Ops:
  0.0 3.6 %pack.2 = (bf16[2064,128]{1,0:T(8,128)(2,1)}, bf16[2064,128]{1,0:T(8,128)(2,1)}, bf16[2064,128]{1,0:T(8,128)(2,1)}, bf16[16,128]{1,0:T(8,128)(2,1)}) custom-call(s32[1]{0:T(128)} %bitcast.2.me_ref, s32[8]{0:T(128)} %ids_ref.3, bf16[4,256,2048]{2,1,0:T(8,128)(2,1)} %bitcast.13, bf16[4,256,2048]{2,1,0:T(8,128)(2,1)} %bitcast.14, ...), custom_call_target="tpu_custom_call" | custom-call | bytes 1000000 | tf_op jit(solution)/shard_map/pack/pallas_call | solution.py:429
  3.6 2.1 %collective-permute-start = (bf16[2064,128]{1,0:T(8,128)(2,1)}, bf16[2064,128]{1,0:T(8,128)(2,1)S(1)}, u32[]{:S(2)}, u32[]{:S(2)}) collective-permute-start(bf16[2064,128]{1,0:T(8,128)(2,1)} %get-tuple-element.36), channel_id=1, source_target_pairs={{0,32},{32,64},{64,96},{96,0},{1,33},{33,65},{65,97},{97,1},{2,34}... | collective-permute-start | bytes 1585160 | tf_op jit(solution)/shard_map/ppermute | solution.py:445
  5.7 1.5 %collective-permute-start.2 = (bf16[2064,128]{1,0:T(8,128)(2,1)}, bf16[2064,128]{1,0:T(8,128)(2,1)}, u32[]{:S(2)}, u32[]{:S(2)}) collective-permute-start(bf16[2064,128]{1,0:T(8,128)(2,1)} %get-tuple-element.39), channel_id=1, source_target_pairs={{0,96},{32,0},{64,32},{96,64},{1,97},{33,1},{65,33},{97,65},{2,98}... | collective-permute-start | bytes 1585160 | tf_op jit(solution)/shard_map/ppermute | solution.py:445
  7.1 1.6 %collective-permute-start.4 = (bf16[2064,128]{1,0:T(8,128)(2,1)}, bf16[2064,128]{1,0:T(8,128)(2,1)}, u32[]{:S(2)}, u32[]{:S(2)}) collective-permute-start(bf16[2064,128]{1,0:T(8,128)(2,1)} %get-tuple-element.42), channel_id=1, source_target_pairs={{0,64},{32,96},{64,0},{96,32},{1,65},{33,97},{65,1},{97,33},{2,66}... | collective-permute-start | bytes 1585160 | tf_op jit(solution)/shard_map/ppermute | solution.py:445
  8.8 2.7 %route.1 = (bf16[1024,256]{1,0:T(8,128)(2,1)}, bf16[128,512]{1,0:T(8,128)(2,1)}, bf16[256,128]{1,0:T(8,128)(2,1)}, bf16[1024,512]{1,0:T(8,128)(2,1)}) custom-call(s32[1]{0:T(128)} %bitcast.lane_ref, s32[2,256]{1,0:T(2,128)} %bitcast.33, s32[1,256]{1,0:T(1,128)} %bitcast.37, bf16[256,1024]{1,0:T(8,128)(2,1)} %refs_12_.1), custom_call_target="tpu_custom_call" | custom-call | flops 500000000 | bytes 3000000 | tf_op jit(solution)/shard_map/route/pallas_call | solution.py:458
  11.5 9.5 %all-to-all-start = ((bf16[32,32,512]{2,1,0:T(8,128)(2,1)}), bf16[32,32,512]{2,1,0:T(8,128)(2,1)}, u32[]{:S(2)}, u32[]{:S(2)}) async-start(bf16[32,32,512]{2,1,0:T(8,128)(2,1)} %bitcast.27), calls=%async_computation | async-start | bytes 2097152 | tf_op jit(solution)/shard_map/all_to_all | solution.py:480
  21.0 3.5 %pack.3 = (bf16[2048,128]{1,0:T(8,128)(2,1)}, bf16[2048,128]{1,0:T(8,128)(2,1)}, bf16[2048,128]{1,0:T(8,128)(2,1)}) custom-call(s32[1]{0:T(128)} %bitcast.2.me_ref, s32[8]{0:T(128)} %ids_ref.3, bf16[4,256,2048]{2,1,0:T(8,128)(2,1)} %bitcast.19, bf16[4,256,2048]{2,1,0:T(8,128)(2,1)} %bitcast.20, bf16[4,256,2048]{2,1,0:T(8,128)(2,1)} %bitcast.21, ...), custom_call_target="tpu_custom_call" | custom-call | bytes 1000000 | tf_op jit(solution)/shard_map/pack/pallas_call | solution.py:429
  24.5 5.3 %project.1 = (bf16[256,1024]{1,0:T(8,128)(2,1)}, f32[256,1024]{1,0:T(8,128)}) custom-call(bf16[256,1024]{1,0:T(8,128)(2,1)} %refs_12_.1, bf16[1024,2048]{1,0:T(8,128)(2,1)} %weight_ref.1, f32[1,1024]{1,0:T(1,128)} %bitcast.32), custom_call_target="tpu_custom_call" | custom-call | flops 1100000000 | bytes 6000000 | tf_op jit(solution)/shard_map/project/pallas_call | solution.py:487
  29.8 0.0 collective-permute-done.refs_2_.refs_5_
  29.8 0.0 copy-start.2
  29.8 0.5 collective-permute-start.1
  30.3 0.0 collective-permute-done.2.refs_3_.refs_6_
  30.3 2.3 %collective-permute-start.3 = (bf16[2048,128]{1,0:T(8,128)(2,1)}, bf16[2048,128]{1,0:T(8,128)(2,1)}, u32[]{:S(2)}, u32[]{:S(2)}) collective-permute-start(bf16[2048,128]{1,0:T(8,128)(2,1)} %get-tuple-element.40), channel_id=1, source_target_pairs={{0,96},{32,0},{64,32},{96,64},{1,97},{33,1},{65,33},{97,65},{2,98}... | collective-permute-start | bytes 1572872 | tf_op jit(solution)/shard_map/ppermute | solution.py:445
  32.6 0.0 collective-permute-done.4.refs_4_.refs_7_
  32.6 0.1 collective-permute-start.5
  32.6 0.0 copy-done.2
  32.6 6.2 %attend_first.1 = (bf16[1024,512]{1,0:T(8,128)(2,1)}, bf16[256,512]{1,0:T(8,128)(2,1)}, f32[256,128]{1,0:T(8,128)}) custom-call(s32[1]{0:T(128)} %bitcast.2.me_ref, s32[2]{0:T(128)} %hist_ref.3, f32[4,8]{1,0:T(4,128)} %bitcast.35, bf16[256,1024]{1,0:T(8,128)(2,1)} %get-tuple-element.35.refs_0_, bf16[4,256,2048]{2,1,0:T(8,128)(2,1)} %bitcast.25, ...), custom_call_target="tpu_custom_call" | custom-call | flops 30000001024 | bytes 1000000 | tf_op jit(solution)/shard_map/attend_first/pallas_call | solution.py:529
  38.8 0.0 all-to-all-done.rows_at
  38.8 11.0 %all-to-all-start.2 = ((bf16[32,32,512]{2,1,0:T(8,128)(2,1)}), bf16[32,32,512]{2,1,0:T(8,128)(2,1)}, u32[]{:S(2)}, u32[]{:S(2)}) async-start(bf16[32,32,512]{2,1,0:T(8,128)(2,1)} %bitcast.28), calls=%async_computation.2 | async-start | bytes 2097152 | tf_op jit(solution)/shard_map/all_to_all | solution.py:480
  49.8 8.8 %early_cand.1.cand_at = bf16[4096,1024]{1,0:T(8,128)(2,1)} custom-call(bf16[32,32,512]{2,1,0:T(8,128)(2,1)} %all-to-all-done.rows_at, bf16[1,1024,4096]{2,1,0:T(8,128)(2,1)} %up_at.5), custom_call_target="tpu_custom_call" | custom-call | flops 5000000000 | bytes 1000000 | tf_op jit(solution)/shard_map/early_cand/pallas_call | solution.py:570
  58.7 0.0 collective-permute-done.1.refs_2_
  58.7 0.0 collective-permute-done.3.refs_3_
  58.7 0.0 collective-permute-done.5.refs_4_
  58.7 0.0 copy-start.1
  58.7 6.7 %attend_last.1 = (bf16[32,144,128]{2,1,0:T(8,128)(2,1)}, bf16[256,1024]{1,0:T(8,128)(2,1)}) custom-call(s32[1]{0:T(128)} %bitcast.2.me_ref, s32[2]{0:T(128)} %hist_ref.3, f32[4,8]{1,0:T(4,128)} %bitcast.36, bf16[256,1024]{1,0:T(8,128)(2,1)} %get-tuple-element.35.refs_0_, bf16[4,256,2048]{2,1,0:T(8,128)(2,1)} %bitcast.26, ...), custom_call_target="tpu_custom_call" | custom-call | flops 99999997952 | bytes 1000000 | tf_op jit(solution)/shard_map/attend_last/pallas_call | solution.py:529
  65.4 1.6 %all-to-all-done.2.rows_at = bf16[32,32,512]{2,1,0:T(8,128)(2,1)} async-done(((bf16[32,32,512]{2,1,0:T(8,128)(2,1)}), bf16[32,32,512]{2,1,0:T(8,128)(2,1)}, u32[]{:S(2)}, u32[]{:S(2)}) %all-to-all-start.2) | async-done | bytes 1048608 | tf_op jit(solution)/shard_map/all_to_all | solution.py:480
  67.0 6.0 %all-to-all-start.1 = ((bf16[32,144,128]{2,1,0:T(8,128)(2,1)}), bf16[32,144,128]{2,1,0:T(8,128)(2,1)}, u32[]{:S(2)}, u32[]{:S(2)}) async-start(bf16[32,144,128]{2,1,0:T(8,128)(2,1)} %get-tuple-element.51), calls=%async_computation.1 | async-start | bytes 2359296 | tf_op jit(solution)/shard_map/all_to_all | solution.py:480
  73.1 0.0 copy-done.1
  73.1 0.6 pad.4.tower_ref
  73.7 6.6 %tower.1.tower_at = bf16[16,4096]{1,0:T(8,128)(2,1)} custom-call(bf16[1,4096,1024]{2,1,0:T(8,128)(2,1)} %down_at.1, bf16[16,1024]{1,0:T(8,128)(2,1)} %pad.4.tower_ref), custom_call_target="tpu_custom_call" | custom-call | flops 100000000 | bytes 9000000 | tf_op jit(solution)/shard_map/tower/pallas_call | solution.py:510
  80.3 8.8 %early_stuff.1.stuff_at = bf16[4096,1024]{1,0:T(8,128)(2,1)} custom-call(bf16[32,32,512]{2,1,0:T(8,128)(2,1)} %all-to-all-done.2.rows_at, bf16[1,1024,4096]{2,1,0:T(8,128)(2,1)} %up_at.5), custom_call_target="tpu_custom_call" | custom-call | flops 5000000000 | bytes 1000000 | tf_op jit(solution)/shard_map/early_stuff/pallas_call | solution.py:570
  89.1 1.5 %all-to-all-done.1.last_at = bf16[32,144,128]{2,1,0:T(8,128)(2,1)} async-done(((bf16[32,144,128]{2,1,0:T(8,128)(2,1)}), bf16[32,144,128]{2,1,0:T(8,128)(2,1)}, u32[]{:S(2)}, u32[]{:S(2)}) %all-to-all-start.1) | async-done | bytes 1179680 | tf_op jit(solution)/shard_map/all_to_all | solution.py:480
  90.6 11.1 %expert.1 = f32[32,8,128]{2,1,0:T(8,128)} custom-call(bf16[32,144,128]{2,1,0:T(8,128)(2,1)} %all-to-all-done.1.last_at, bf16[4096,1024]{1,0:T(8,128)(2,1)} %early_cand.1.cand_at, bf16[4096,1024]{1,0:T(8,128)(2,1)} %early_stuff.1.stuff_at, bf16[1,1024,4096]{2,1,0:T(8,128)(2,1)} %up_at.5, bf16[16,4096]{1,0:T(8,128)(2,1)} %tower.1.tower_at), custom_call_target="tpu_custom_call" | custom-call | flops 6000000000 | bytes 25000000 | tf_op jit(solution)/shard_map/expert/pallas_call | solution.py:620
  101.7 5.9 %all-to-all-start.3 = ((f32[32,8,128]{2,1,0:T(8,128)}), f32[32,8,128]{2,1,0:T(8,128)S(1)}, u32[]{:S(2)}, u32[]{:S(2)}) async-start(f32[32,8,128]{2,1,0:T(8,128)} %expert.1), calls=%async_computation.3 | async-start | bytes 262144 | tf_op jit(solution)/shard_map/all_to_all | solution.py:480
  107.7 2.4 %gate.1.weight_ref = f32[256,512]{1,0:T(8,128)} custom-call(s32[2,256]{1,0:T(2,128)} %bitcast.34, bf16[192,1024]{1,0:T(8,128)(2,1)} %bitcast.30, bf16[256,1024]{1,0:T(8,128)(2,1)} %get-tuple-element.50.mixed_ref), custom_call_target="tpu_custom_call" | custom-call | flops 100000000 | bytes 2000000 | tf_op jit(solution)/shard_map/gate/pallas_call | solution.py:609
  110.1 5.2 %all-to-all-done.3 = f32[32,8,128]{2,1,0:T(8,128)S(1)} async-done(((f32[32,8,128]{2,1,0:T(8,128)}), f32[32,8,128]{2,1,0:T(8,128)S(1)}, u32[]{:S(2)}, u32[]{:S(2)}) %all-to-all-start.3) | async-done | bytes 131104 | tf_op jit(solution)/shard_map/all_to_all | solution.py:480
  115.3 0.0 copy-start
  115.3 0.7 copy-done
  116.0 2.1 %combine.1 = f32[6,256]{1,0:T(8,128)} custom-call(bf16[128,512]{1,0:T(8,128)(2,1)} %get-tuple-element.31.slot_ref, f32[256,512]{1,0:T(8,128)} %gate.1.weight_ref, f32[256,128]{1,0:T(8,128)} %bitcast.29), custom_call_target="tpu_custom_call" | custom-call | flops 100000000 | bytes 1000000 | tf_op jit(solution)/shard_map/combine/pallas_call | solution.py:641
Async XLA Ops:
  3.6 26.2 %collective-permute-start = (bf16[2064,128]{1,0:T(8,128)(2,1)}, bf16[2064,128]{1,0:T(8,128)(2,1)S(1)}, u32[]{:S(2)}, u32[]{:S(2)}) collective-permute-start(bf16[2064,128]{1,0:T(8,128)(2,1)} %get-tuple-element.36), channel_id=1, source_target_pairs={{0,32},{32,64},{64,96},{96,0},{1,33},{33,65},{65,97},{97,1},{2,34}... | collective-permute-start | bytes 1585160 | tf_op jit(solution)/shard_map/ppermute | solution.py:445
  5.7 24.6 %collective-permute-start.2 = (bf16[2064,128]{1,0:T(8,128)(2,1)}, bf16[2064,128]{1,0:T(8,128)(2,1)}, u32[]{:S(2)}, u32[]{:S(2)}) collective-permute-start(bf16[2064,128]{1,0:T(8,128)(2,1)} %get-tuple-element.39), channel_id=1, source_target_pairs={{0,96},{32,0},{64,32},{96,64},{1,97},{33,1},{65,33},{97,65},{2,98}... | collective-permute-start | bytes 1585160 | tf_op jit(solution)/shard_map/ppermute | solution.py:445
  7.1 25.4 %collective-permute-start.4 = (bf16[2064,128]{1,0:T(8,128)(2,1)}, bf16[2064,128]{1,0:T(8,128)(2,1)}, u32[]{:S(2)}, u32[]{:S(2)}) collective-permute-start(bf16[2064,128]{1,0:T(8,128)(2,1)} %get-tuple-element.42), channel_id=1, source_target_pairs={{0,64},{32,96},{64,0},{96,32},{1,65},{33,97},{65,1},{97,33},{2,66}... | collective-permute-start | bytes 1585160 | tf_op jit(solution)/shard_map/ppermute | solution.py:445
  11.5 27.3 %all-to-all-start = ((bf16[32,32,512]{2,1,0:T(8,128)(2,1)}), bf16[32,32,512]{2,1,0:T(8,128)(2,1)}, u32[]{:S(2)}, u32[]{:S(2)}) async-start(bf16[32,32,512]{2,1,0:T(8,128)(2,1)} %bitcast.27), calls=%async_computation | async-start | bytes 2097152 | tf_op jit(solution)/shard_map/all_to_all | solution.py:480
  29.8 2.8 %copy-start.2 = (bf16[2064,128]{1,0:T(8,128)(2,1)}, bf16[2064,128]{1,0:T(8,128)(2,1)S(1)}, u32[]{:S(2)}) copy-start(bf16[2064,128]{1,0:T(8,128)(2,1)S(1)} %collective-permute-done.refs_2_.refs_5_) | copy-start | bytes 1585156
  29.8 28.9 %collective-permute-start.1 = (bf16[2048,128]{1,0:T(8,128)(2,1)}, bf16[2048,128]{1,0:T(8,128)(2,1)}, u32[]{:S(2)}, u32[]{:S(2)}) collective-permute-start(bf16[2048,128]{1,0:T(8,128)(2,1)} %get-tuple-element.37), channel_id=1, source_target_pairs={{0,32},{32,64},{64,96},{96,0},{1,33},{33,65},{65,97},{97,1},{2,34}... | collective-permute-start | bytes 1572872 | tf_op jit(solution)/shard_map/ppermute | solution.py:445
  30.3 28.4 %collective-permute-start.3 = (bf16[2048,128]{1,0:T(8,128)(2,1)}, bf16[2048,128]{1,0:T(8,128)(2,1)}, u32[]{:S(2)}, u32[]{:S(2)}) collective-permute-start(bf16[2048,128]{1,0:T(8,128)(2,1)} %get-tuple-element.40), channel_id=1, source_target_pairs={{0,96},{32,0},{64,32},{96,64},{1,97},{33,1},{65,33},{97,65},{2,98}... | collective-permute-start | bytes 1572872 | tf_op jit(solution)/shard_map/ppermute | solution.py:445
  32.6 26.1 %collective-permute-start.5 = (bf16[2048,128]{1,0:T(8,128)(2,1)}, bf16[2048,128]{1,0:T(8,128)(2,1)}, u32[]{:S(2)}, u32[]{:S(2)}) collective-permute-start(bf16[2048,128]{1,0:T(8,128)(2,1)} %get-tuple-element.43), channel_id=1, source_target_pairs={{0,64},{32,96},{64,0},{96,32},{1,65},{33,97},{65,1},{97,33},{2,66}... | collective-permute-start | bytes 1572872 | tf_op jit(solution)/shard_map/ppermute | solution.py:445
  38.8 28.2 %all-to-all-start.2 = ((bf16[32,32,512]{2,1,0:T(8,128)(2,1)}), bf16[32,32,512]{2,1,0:T(8,128)(2,1)}, u32[]{:S(2)}, u32[]{:S(2)}) async-start(bf16[32,32,512]{2,1,0:T(8,128)(2,1)} %bitcast.28), calls=%async_computation.2 | async-start | bytes 2097152 | tf_op jit(solution)/shard_map/all_to_all | solution.py:480
  58.7 14.4 %copy-start.1 = (bf16[1024,6]{0,1:T(8,128)(2,1)S(1)}, bf16[1024,6]{0,1:T(8,128)(2,1)}, u32[]{:S(2)}) copy-start(bf16[1024,6]{0,1:T(8,128)(2,1)} %param.25) | copy-start | bytes 36868
  67.0 23.6 %all-to-all-start.1 = ((bf16[32,144,128]{2,1,0:T(8,128)(2,1)}), bf16[32,144,128]{2,1,0:T(8,128)(2,1)}, u32[]{:S(2)}, u32[]{:S(2)}) async-start(bf16[32,144,128]{2,1,0:T(8,128)(2,1)} %get-tuple-element.51), calls=%async_computation.1 | async-start | bytes 2359296 | tf_op jit(solution)/shard_map/all_to_all | solution.py:480
  101.7 13.6 %all-to-all-start.3 = ((f32[32,8,128]{2,1,0:T(8,128)}), f32[32,8,128]{2,1,0:T(8,128)S(1)}, u32[]{:S(2)}, u32[]{:S(2)}) async-start(f32[32,8,128]{2,1,0:T(8,128)} %expert.1), calls=%async_computation.3 | async-start | bytes 262144 | tf_op jit(solution)/shard_map/all_to_all | solution.py:480
  115.3 0.7 copy-start

commit v4 on v3

v4 whole, which is shorter than its diff:
```python
import functools
import math

import jax
import jax.numpy as jnp
from jax import lax
from jax.experimental import pallas as pl
from jax.experimental.pallas import tpu as pltpu
from jax.sharding import PartitionSpec as P

EPSILON = 1e-05
F32 = jnp.float32
BF16 = jnp.bfloat16
NT = (((1,), (1,)), ((), ()))
TN = (((0,), (0,)), ((), ()))
SHIFTS = (1, 3, 2)
HEADS_FIRST = 4
GATE_LIMIT = 8
COMBINE_LIMIT = 8
AHEAD = 3
FIRST_COST = 30 * 10**9
EARLY_COST = 5 * 10**9
LAST_COST = 100 * 10**9


def pack_kernel(chunk, me_ref, ids_ref, cache_at, *refs):
    count = len(SHIFTS)
    packed, sems = refs[-2:]
    outs = refs[:-2]
    owners, keys, width = cache_at.shape
    parts = packed.shape[1] // keys
    heads = parts // 2
    first = chunk * (width // 256 - heads)
    me = me_ref[0]
    loads = []
    for n, shift in enumerate(SHIFTS):
        to = lax.rem(me + shift, owners)
        for part in range(parts):
            col = (first + part % heads) * 128 + (part // heads) * (width // 2)
            here = packed.at[n, pl.ds(part * keys, keys), :]
            load = pltpu.make_async_copy(cache_at.at[to, :, pl.ds(col, 128)], here, sems.at[0, n, part])
            load.start()
            store = pltpu.make_async_copy(here, outs[n].at[pl.ds(part * keys, keys), :], sems.at[1, n, part])
            loads.append((load, store))
    stores = []
    if len(outs) > count:
        row = lax.broadcasted_iota(jnp.int32, (16, 128), 0)

        def tile_of(owner):
            one = ids_ref[2 * owner].astype(F32)
            two = ids_ref[2 * owner + 1].astype(F32)
            return jnp.where(row == 0, one, two).astype(BF16)

        for n, shift in enumerate(SHIFTS):
            here = pl.ds(parts * keys, 16)
            packed[n, here, :] = tile_of(lax.rem(me + shift, owners))
            store = pltpu.make_async_copy(packed.at[n, here, :], outs[n].at[here, :], sems.at[1, n, parts])
            store.start()
            stores.append(store)
        outs[count][...] = tile_of(me)
    for load, store in loads:
        load.wait()
        store.start()
        stores.append(store)
    for store in stores:
        store.wait()


def place_of(slot, slots):
    rows = slot.shape[1] // 2
    spot = lax.broadcasted_iota(jnp.int32, (slots, rows), 0)
    place = (spot == slot[:, :rows]) | (spot == slot[:, rows:])
    return jnp.where(place, 1.0, 0.0).astype(BF16)


def route_kernel(capacity, ids_ref, req_ref, cand_ref, spot_ref, first_ref, out_ref):
    rows = ids_ref.shape[1]
    experts = out_ref.shape[0] // capacity
    ids = jnp.concatenate([ids_ref[0:1, :], ids_ref[1:2, :]], axis=1)
    hot = lax.broadcasted_iota(jnp.int32, (experts, 2 * rows), 0) == ids
    hot = jnp.where(hot, 1.0, 0.0)
    here = lax.broadcasted_iota(jnp.int32, (2 * rows, 2 * rows), 0)
    there = lax.broadcasted_iota(jnp.int32, (2 * rows, 2 * rows), 1)
    earlier = jnp.where(here < there, 1.0, 0.0).astype(BF16)
    counts = jnp.dot(hot.astype(BF16), earlier, preferred_element_type=F32)
    position = jnp.sum(counts * hot, axis=0, keepdims=True).astype(jnp.int32)
    slot = ids * capacity + position
    spot_ref[...] = jnp.broadcast_to(slot, spot_ref.shape)
    place = place_of(slot, out_ref.shape[0])
    out_ref[...] = jnp.dot(place, cand_ref[...], preferred_element_type=F32).astype(BF16)
    first = jnp.where(req_ref[...] == 0, 1.0, 0.0)
    first_ref[...] = jnp.transpose(jnp.broadcast_to(first, (128, rows))).astype(BF16)


def project_kernel(cand_ref, weight_at, gain_ref, query_ref, update_ref, weight, sems):
    count, _, wide = weight.shape
    loads = []
    for i in range(count):
        here = pl.ds(i * wide, wide)
        loads.append(pltpu.make_async_copy(weight_at.at[:, here], weight.at[i], sems.at[i]))
        loads[i].start()
    for i in range(count):
        loads[i].wait()
        projected = jnp.dot(cand_ref[...], weight[i], preferred_element_type=F32)
        cols = pl.ds(i % (count // 2) * wide, wide)
        if i < count // 2:
            query_ref[:, cols] = projected.astype(BF16)
        else:
            update_ref[:, cols] = gain_ref[:, cols] * projected / (1.0 + jnp.exp(-projected))


def tower_kernel(down_at, tower_ref, out_ref, down, sems):
    count, tile, _ = down.shape
    loads = []
    for i in range(count):
        here = pl.ds(i * tile, tile)
        loads.append(pltpu.make_async_copy(down_at.at[0, here, :], down.at[i], sems.at[i]))
    for i in range(2):
        loads[i].start()
    for i in range(count):
        if i + 2 < count:
            loads[i + 2].start()
        loads[i].wait()
        product = lax.dot_general(tower_ref[...], down[i], NT, preferred_element_type=F32)
        high = product.astype(BF16)
        low = (product - high.astype(F32)).astype(BF16)
        out_ref[:, pl.ds(i * tile, tile)] = jnp.concatenate([high[0:8], low[0:8]], axis=0)


def attend_head(head, first, mask, query, key, value, blocks, bias_ref):
    scores = lax.dot_general(query, key, NT, preferred_element_type=F32)
    weights = []
    for owner, (block_a, block_b) in enumerate(blocks):
        here = scores[:, owner * 256 : (owner + 1) * 256]
        here = jnp.where(first, here[:, :128], here[:, 128:])
        bias_a = jnp.zeros_like(block_a)
        bias_b = jnp.zeros_like(block_b)
        for block in range(bias_ref.shape[0]):
            entry = bias_ref[block, head] * 0.5
            bias_a = jnp.where(block_a == block, entry, bias_a)
            bias_b = jnp.where(block_b == block, entry, bias_b)
        half = here * (0.5 / math.sqrt(128.0)) + jnp.where(first, bias_a, bias_b)
        weight = (half + half * jnp.tanh(half)).astype(BF16)
        weights += [weight, weight]
    weights = jnp.concatenate(weights, axis=1) * mask
    return jnp.dot(weights, value, preferred_element_type=F32)


def attend_kernel(chunk, me_ref, hist_ref, bias_ref, *refs):
    last = chunk == 1
    query_at, cache_at, *refs = refs
    moved_at, refs = refs[:3], refs[3:]
    ids_at, refs = refs[:3], refs[3:]
    own_at, first_at, update_at, spot_at, *refs = refs
    if last:
        cand_at, square_at, *refs = refs
        out_at, mixed_at, scale_at, *refs = refs
    else:
        out_at, stuff_at, square_at, *refs = refs
    sems, kv, own, tiles, query, first_in, update, spot, place, square, stuff, out, *refs = refs
    if last:
        cand, attended = refs
    owners, keys, width = cache_at.shape
    heads = own.shape[2] // 128
    early = heads * 128
    base = chunk * (width // 256 - heads)
    id_row = ids_at[0].shape[0] - 16
    rows = query.shape[0]
    me = me_ref[0]
    used = []

    def copy(source, target):
        item = pltpu.make_async_copy(source, target, sems.at[len(used)])
        item.start()
        used.append(item)
        return item

    wanted = [copy(query_at.at[:, pl.ds(base * 128, early)], query)]
    wanted.append(copy(first_at, first_in))
    wanted.append(copy(own_at, tiles.at[0]))
    wanted.append(copy(spot_at, spot))
    if last:
        for n in range(3):
            wanted.append(copy(ids_at[n].at[pl.ds(id_row, 16), :], tiles.at[n + 1]))
    loads = [[copy(moved_at[n], kv.at[n])] for n in range(3)]
    for half in range(2):
        here = pl.ds(half * (width // 2) + base * 128, early)
        loads.append([copy(cache_at.at[me, :, here], own.at[half])])
    later = [copy(update_at.at[:, pl.ds(base * 128, early)], update)]
    if last:
        later += [copy(cand_at.at[:, pl.ds(base * 128, early)], cand), copy(square_at, square)]
    for item in wanted:
        item.wait()
    if not last:
        for n in range(3):
            loads[n][0].wait()
            tiles[n + 1] = kv[n, pl.ds(id_row, 16), :]
        loads = loads[3:]
    first = first_in[...].astype(F32) > 0.5
    length_a = hist_ref[0].astype(F32)
    length_b = hist_ref[1].astype(F32)
    blocks = []
    masks = []
    for owner in range(owners):
        tile = tiles[owner].astype(F32)
        block_a, block_b = tile[0:1, :], tile[1:2, :]
        blocks.append((block_a, block_b))
        mask_a = jnp.where(first, jnp.where(block_a < length_a, 1.0, 0.0), 0.0)
        mask_b = jnp.where(first, 0.0, jnp.where(block_b < length_b, 1.0, 0.0))
        masks += [mask_a.astype(BF16), mask_b.astype(BF16)]
    mask = jnp.concatenate(masks, axis=1)
    place[...] = place_of(spot[0:1, :], place.shape[0])
    total = None
    stores = []
    for load in loads:
        for item in load:
            item.wait()
    for item in later:
        item.wait()
    for head in range(heads):
        cols = pl.ds(head * 128, 128)
        at_key, at_value = pl.ds(head * keys, keys), pl.ds((heads + head) * keys, keys)
        key = jnp.concatenate([own[0, :, cols]] + [kv[n, at_key, :] for n in range(3)], axis=0)
        value = jnp.concatenate([own[1, :, cols]] + [kv[n, at_value, :] for n in range(3)], axis=0)
        found = attend_head(base + head, first, mask, query[:, cols], key, value, blocks, bias_ref)
        total = found * found if total is None else total + found * found
        if last:
            attended[:, cols] = found * update[:, cols]
            continue
        stuff[:, cols] = (found * update[:, cols]).astype(BF16)
        if head % 2 == 1 or head == heads - 1:
            here = pl.ds(head // 2 * 256, 256 if head % 2 else 128)
            out[:, here] = jnp.dot(place[...], stuff[:, here], preferred_element_type=F32).astype(BF16)
            stores.append(copy(out.at[:, here], out_at.at[:, here]))
    if not last:
        square[...] = total
        stores.append(copy(stuff, stuff_at))
        stores.append(copy(square, square_at))
        for item in stores:
            item.wait()
        return
    feature = width // 2
    mean = jnp.sum(total + square[...], axis=1, keepdims=True) * (1.0 / feature)
    inv_rms = lax.rsqrt(mean + EPSILON)
    peers = out.shape[0]
    share = place.shape[0] // peers
    for i in range((heads + 1) // 2):
        some = min(2, heads - 2 * i)
        cols = pl.ds(i * 256, some * 128)
        block = (cand[:, cols].astype(F32) + attended[:, cols] * inv_rms).astype(BF16)
        stuff[:, cols] = block
        sent = jnp.dot(place[...], block, preferred_element_type=F32).astype(BF16)
        for j in range(some):
            here = pl.ds((2 * i + j) * share, share)
            out[:, here, :] = sent[:, j * 128 : (j + 1) * 128].reshape(peers, share, 128)
    scale = jnp.transpose(jnp.broadcast_to(inv_rms, (rows, 128)))[0:16, :]
    high = scale.astype(BF16).astype(F32)
    row = lax.broadcasted_iota(jnp.int32, scale.shape, 0)
    scale = jnp.where(row == 0, high, jnp.where(row == 1, scale - high, 0.0)).astype(BF16)
    scale = lax.dot_general(scale, place[...], NT, preferred_element_type=F32)
    each = 128 // share
    for peer in range(peers):
        tile = scale[:, (peer // each) * 128 : (peer // each + 1) * 128]
        if peer % each:
            tile = pltpu.roll(tile, 128 - (peer % each) * share, 1)
        out[peer, pl.ds(heads * share, 16), :] = tile.astype(BF16)
    stores.append(copy(out, out_at))
    square[...] = jnp.broadcast_to(inv_rms, square.shape)
    stores.append(copy(stuff, mixed_at))
    stores.append(copy(square, scale_at))
    for item in stores:
        item.wait()


def gate_kernel(tasks, ids_ref, weight_ref, cand_ref, stuff_ref, late_ref, scale_ref, out_ref):
    rows, early = stuff_ref.shape
    experts = weight_ref.shape[0] // tasks
    mixed = cand_ref[:, :early].astype(F32) + stuff_ref[...].astype(F32) * scale_ref[:, 0:1]
    logits = lax.dot_general(weight_ref[:, :early], mixed.astype(BF16), NT, preferred_element_type=F32)
    logits += lax.dot_general(weight_ref[:, early:], late_ref[...], NT, preferred_element_type=F32)
    squashed = []
    for k in range(2):
        hot = lax.broadcasted_iota(jnp.int32, (experts, rows), 0) == ids_ref[k : k + 1, :]
        picked = []
        for task in range(8):
            if task < tasks:
                here = logits[task * experts : (task + 1) * experts, :]
                picked.append(jnp.sum(jnp.where(hot, here, 0.0), axis=0, keepdims=True))
            else:
                picked.append(jnp.zeros((1, rows), F32))
        squashed.append(jax.nn.sigmoid(jnp.concatenate(picked, axis=0)))
    whole = squashed[0] + squashed[1]
    for k in range(2):
        out_ref[:, pl.ds(k * rows, rows)] = squashed[k] / whole


def early_kernel(cand_at, stuff_at, up_at, cand_out_at, stuff_out_at, rows, up, turned, out, sems):
    _, peers, share, early = rows.shape
    count, _, tile = up.shape
    used = []

    def copy(source, target):
        item = pltpu.make_async_copy(source, target, sems.at[len(used)])
        used.append(item)
        return item

    fetch = [copy(cand_at, rows.at[0]), copy(stuff_at, rows.at[1])]
    ups = []
    for i in range(count):
        here = pl.ds(i * tile, tile)
        ups.append(copy(up_at.at[0, pl.ds(0, early), here], up.at[i]))
    fetch[0].start()
    ups[0].start()
    fetch[1].start()
    stores = []
    for k, out_at in enumerate((cand_out_at, stuff_out_at)):
        fetch[k].wait()
        for i in range(early // 128):
            cols = pl.ds(i * 128, 128)
            block = rows[k, :, :, cols].reshape(peers * share, 128)
            turned[k, cols, :] = jnp.transpose(block * jnp.asarray(0.5, BF16))
        for i in range(count):
            if k == 0:
                ups[i].wait()
                if i + 1 < count:
                    ups[i + 1].start()
            found = lax.dot_general(up[i], turned[k], TN, preferred_element_type=F32)
            out[k, i] = found.astype(BF16)
            store = copy(out.at[k, i], out_at.at[pl.ds(i * tile, tile), :])
            store.start()
            stores.append(store)
    for store in stores:
        store.wait()


def expert_kernel(
    last_at, cand_product_at, stuff_product_at, up_at, tower_at, out_ref,
    last, cand_product, stuff_product, up, tower, turned, scale, sems,
):
    count, late, tile = up.shape
    early = up_at.shape[1] - late
    peers = last.shape[0]
    share = (last.shape[1] - 16) // (late // 128)
    rows = peers * share
    each = 128 // share
    fetch = pltpu.make_async_copy(last_at, last, sems.at[0])
    fetch.start()
    fetch_tower = pltpu.make_async_copy(tower_at, tower, sems.at[1])
    fetch_tower.start()
    loads = []
    for i in range(count):
        here = pl.ds(i * tile, tile)
        loads.append(
            (
                pltpu.make_async_copy(up_at.at[0, pl.ds(early, late), here], up.at[i], sems.at[3 * i + 2]),
                pltpu.make_async_copy(cand_product_at.at[here, :], cand_product.at[i], sems.at[3 * i + 3]),
                pltpu.make_async_copy(stuff_product_at.at[here, :], stuff_product.at[i], sems.at[3 * i + 4]),
            )
        )
    for item in loads[0]:
        item.start()
    fetch.wait()
    for ahead in range(1, AHEAD):
        for item in loads[ahead]:
            item.start()
    lane = lax.broadcasted_iota(jnp.int32, (16, 128), 1)
    for group in range(peers // each):
        whole_tile = None
        for i in range(each):
            part = last[group * each + i, pl.ds(late // 128 * share, 16), :].astype(F32)
            part = pltpu.roll(part, i * share, 1) if i else part
            part = jnp.where((lane >= i * share) & (lane < (i + 1) * share), part, 0.0)
            whole_tile = part if whole_tile is None else whole_tile + part
        scale[:, pl.ds(group * 128, 128)] = whole_tile[0:1, :] + whole_tile[1:2, :]
    for i in range(late // 128):
        block = last[:, pl.ds(i * share, share), :].reshape(rows, 128)
        turned[pl.ds(i * 128, 128), :] = jnp.transpose(block * jnp.asarray(0.5, BF16))
    fetch_tower.wait()
    total = None
    row_scale = scale[...].astype(BF16)
    for i in range(count):
        if i + AHEAD < count:
            for item in loads[i + AHEAD]:
                item.start()
        for item in loads[i]:
            item.wait()
        half = lax.dot_general(up[i], turned[...], TN, preferred_element_type=F32)
        half = half + (cand_product[i] + stuff_product[i] * row_scale).astype(F32)
        hidden = (half + half * jnp.tanh(half)).astype(BF16)
        part = jnp.dot(tower[:, pl.ds(i * tile, tile)], hidden, preferred_element_type=F32)
        total = part if total is None else total + part
    found = total[0:8, :] + total[8:16, :]
    for peer in range(peers):
        out_ref[peer] = found[:, (peer // each) * 128 : (peer // each + 1) * 128]


def combine_kernel(capacity, lane_ref, spot_ref, ids_ref, gate_ref, back_ref, out_ref):
    rows = ids_ref.shape[1]
    experts = back_ref.shape[0] // 8
    ids = jnp.concatenate([ids_ref[0:1, :], ids_ref[1:2, :]], axis=1)
    lane = spot_ref[0:1, :] - ids * capacity + lane_ref[0]
    hot = lax.broadcasted_iota(jnp.int32, (128, 2 * rows), 0) == lane
    hot = jnp.where(hot, 1.0, 0.0).astype(BF16)
    back = back_ref[...]
    high = back.astype(BF16)
    rest = back - high.astype(F32)
    middle = rest.astype(BF16)
    low = (rest - middle.astype(F32)).astype(BF16)
    found = jnp.dot(high, hot, preferred_element_type=F32)
    found += jnp.dot(middle, hot, preferred_element_type=F32)
    found += jnp.dot(low, hot, preferred_element_type=F32)
    total = jnp.zeros((8, 2 * rows), F32)
    for expert in range(experts):
        total = jnp.where(ids == expert, found[expert * 8 : (expert + 1) * 8], total)
    total = total * gate_ref[...]
    total = total[:, :rows] + total[:, rows:]
    out_ref[...] = total[: out_ref.shape[0]]


def params(mib=63):
    return pltpu.CompilerParams(vmem_limit_bytes=mib * 2**20)


def cost(flops, bytes_accessed, transcendentals=0):
    return pl.CostEstimate(flops=flops, bytes_accessed=bytes_accessed, transcendentals=transcendentals)


def whole(*shape):
    return pl.BlockSpec(shape, lambda i, *_: (0,) * len(shape))


def local(
    cand_emb,
    cand_request,
    hist_blocks,
    cache_kv,
    block_map,
    w_query_update,
    rel_bias,
    norm_gain,
    w_gate,
    expert_ids,
    w_up,
    w_down,
    w_tower,
):
    rows, feature = cand_emb.shape
    owners = lax.axis_size("req")
    me = lax.axis_index("req").astype(jnp.int32)
    head_count = rel_bias.shape[0]
    tasks = w_tower.shape[1]
    experts = w_gate.shape[1] // tasks
    capacity = 2 * rows * expert_ids.shape[1] // experts
    slots = experts * capacity
    chunk_heads = (HEADS_FIRST, head_count - HEADS_FIRST)
    early = HEADS_FIRST * 128
    keys = cache_kv.shape[0] // owners * cache_kv.shape[1]
    me_scalar = me[None]
    smem = pl.BlockSpec(memory_space=pltpu.SMEM)
    anywhere = pl.BlockSpec(memory_space=pl.ANY)
    hbm = pl.BlockSpec(memory_space=pltpu.HBM)

    cache = cache_kv.reshape(owners, keys, 2 * feature)

    def pack(chunk):
        parts = 2 * chunk_heads[chunk]
        tail = 16 if chunk == 0 else 0
        shapes = [jax.ShapeDtypeStruct((parts * keys + tail, 128), BF16)] * len(SHIFTS)
        specs = [anywhere] * len(SHIFTS)
        if chunk == 0:
            shapes.append(jax.ShapeDtypeStruct((16, 128), BF16))
            specs.append(pl.BlockSpec(memory_space=pltpu.VMEM))
        return pl.pallas_call(
            functools.partial(pack_kernel, chunk),
            in_specs=[smem, smem, anywhere],
            out_specs=specs,
            out_shape=shapes,
            scratch_shapes=[
                pltpu.VMEM((len(SHIFTS), parts * keys + tail, 128), BF16),
                pltpu.SemaphoreType.DMA((2, len(SHIFTS), parts + 1)),
            ],
            compiler_params=params(),
            cost_estimate=cost(0, 10**6),
            name="pack",
        )(me_scalar, block_map, cache)

    def send(item, shift):
        pairs = [(i, (i + shift) % owners) for i in range(owners)]
        return lax.ppermute(item, "req", pairs)

    *packed, own_tile = pack(0)
    first_moved = [send(item, shift) for item, shift in zip(packed, SHIFTS)]
    packed_last = pack(1)
    last_moved = []
    for item, ahead, shift in zip(packed_last, first_moved, SHIFTS):
        item, _ = lax.optimization_barrier((item, ahead))
        last_moved.append(send(item, shift))

    ids_rows, _ = lax.optimization_barrier((expert_ids.T, own_tile))
    each = 128 // capacity
    lane = lax.rem(lax.axis_index("exp").astype(jnp.int32), each) * capacity
    spots, first, cand_out = pl.pallas_call(
        functools.partial(route_kernel, capacity),
        grid=(1,),
        in_specs=[
            whole(2, rows),
            whole(1, rows),
            pl.BlockSpec((rows, early), lambda i: (0, 0)),
        ],
        out_specs=[whole(8, 2 * rows), whole(rows, 128), whole(slots, early)],
        out_shape=[
            jax.ShapeDtypeStruct((8, 2 * rows), jnp.int32),
            jax.ShapeDtypeStruct((rows, 128), BF16),
            jax.ShapeDtypeStruct((slots, early), BF16),
        ],
        compiler_params=params(),
        cost_estimate=cost(5 * 10**8, 3 * 10**6),
        name="route",
    )(ids_rows, cand_request[None, :], cand_emb)

    def exchange(item):
        return lax.all_to_all(item, "exp", split_axis=0, concat_axis=0, tiled=True)

    cand_in = exchange(cand_out.reshape(experts, capacity, early))

    cand_rows, _, _ = lax.optimization_barrier((cand_emb, spots, packed_last[0]))
    steps = 4
    wide = 2 * feature // steps
    queries, update = pl.pallas_call(
        project_kernel,
        in_specs=[
            pl.BlockSpec(memory_space=pltpu.VMEM),
            anywhere,
            pl.BlockSpec(memory_space=pltpu.VMEM),
        ],
        out_shape=[
            jax.ShapeDtypeStruct((rows, feature), BF16),
            jax.ShapeDtypeStruct((rows, feature), F32),
        ],
        scratch_shapes=[pltpu.VMEM((steps, feature, wide), BF16), pltpu.SemaphoreType.DMA((steps,))],
        compiler_params=params(),
        cost_estimate=cost(11 * 10**8, 6 * 10**6, 2**18),
        name="project",
    )(cand_rows, w_query_update, norm_gain[None, :])

    hidden_count = w_up.shape[2]
    tile = 512
    def attend(chunk, moved, extra, out_shape, extra_scratch, name, flops):
        arrays = [queries, cache, *moved, *first_moved, own_tile, first, update, spots, *extra]
        out_rows = out_shape[0].shape
        parts = 2 * chunk_heads[chunk]
        wide = parts * 64
        return pl.pallas_call(
            functools.partial(attend_kernel, chunk),
            in_specs=[smem] * 3 + [anywhere] * len(arrays),
            out_specs=[anywhere] * len(out_shape),
            out_shape=out_shape,
            scratch_shapes=[
                pltpu.SemaphoreType.DMA((16 + 4 * parts,)),
                pltpu.VMEM((owners - 1, *moved[0].shape), BF16),
                pltpu.VMEM((2, keys, wide), BF16),
                pltpu.VMEM((owners, 16, 128), BF16),
                pltpu.VMEM((rows, wide), BF16),
                pltpu.VMEM((rows, 128), BF16),
                pltpu.VMEM((rows, wide), F32),
                pltpu.VMEM((8, 2 * rows), jnp.int32),
                pltpu.VMEM((slots, rows), BF16),
                pltpu.VMEM((rows, 128), F32),
                pltpu.VMEM((rows, wide), BF16),
                pltpu.VMEM(out_rows, BF16),
                *extra_scratch,
            ],
            compiler_params=params(),
            cost_estimate=cost(flops, 10**6),
            name=name,
        )(me_scalar, hist_blocks, rel_bias.T, *arrays)

    stuff_out, stuff, square = attend(
        0,
        first_moved,
        [],
        [
            jax.ShapeDtypeStruct((slots, early), BF16),
            jax.ShapeDtypeStruct((rows, early), BF16),
            jax.ShapeDtypeStruct((rows, 128), F32),
        ],
        [],
        "attend_first",
        FIRST_COST,
    )
    stuff_in = exchange(stuff_out.reshape(experts, capacity, early))

    tower_rows = jnp.pad(w_tower.T, ((0, 16 - tasks), (0, 0)))
    tower_rows, _ = lax.optimization_barrier((tower_rows, cand_in))
    towers = pl.pallas_call(
        tower_kernel,
        in_specs=[pl.BlockSpec(memory_space=pl.ANY), pl.BlockSpec(memory_space=pltpu.VMEM)],
        out_shape=jax.ShapeDtypeStruct((16, hidden_count), BF16),
        scratch_shapes=[
            pltpu.VMEM((hidden_count // tile, tile, feature), BF16),
            pltpu.SemaphoreType.DMA((hidden_count // tile,)),
        ],
        compiler_params=params(),
        cost_estimate=cost(10**8, 9 * 10**6),
        name="tower",
    )(w_down, tower_rows)


    square, _ = lax.optimization_barrier((square, towers))
    last_rows = chunk_heads[1] * capacity + 16
    late = feature - early
    last_out, late_mixed, row_scale = attend(
        1,
        last_moved,
        [cand_emb, square],
        [
            jax.ShapeDtypeStruct((experts, last_rows, 128), BF16),
            jax.ShapeDtypeStruct((rows, late), BF16),
            jax.ShapeDtypeStruct((rows, 128), F32),
        ],
        [pltpu.VMEM((rows, late), BF16), pltpu.VMEM((rows, late), F32)],
        "attend_last",
        LAST_COST,
    )
    last_in = exchange(last_out)
    wide = hidden_count // 4
    products = [jax.ShapeDtypeStruct((hidden_count, slots), BF16)] * 2
    cand_product, stuff_product = pl.pallas_call(
        early_kernel,
        in_specs=[anywhere] * 3,
        out_specs=[anywhere] * 2,
        out_shape=products,
        scratch_shapes=[
            pltpu.VMEM((2, experts, capacity, early), BF16),
            pltpu.VMEM((4, early, wide), BF16),
            pltpu.VMEM((2, early, slots), BF16),
            pltpu.VMEM((2, 4, wide, slots), BF16),
            pltpu.SemaphoreType.DMA((16,)),
        ],
        compiler_params=params(),
        cost_estimate=cost(EARLY_COST, 10**6),
        name="early",
    )(cand_in, stuff_in, w_up)

    gates = pl.pallas_call(
        functools.partial(gate_kernel, tasks),
        out_shape=jax.ShapeDtypeStruct((8, 2 * rows), F32),
        compiler_params=params(GATE_LIMIT),
        cost_estimate=cost(10**8, 2 * 10**6, 4096),
        name="gate",
    )(ids_rows, w_gate.T, cand_emb, stuff, late_mixed, row_scale)

    late = feature - early
    count = hidden_count // tile
    produced = pl.pallas_call(
        expert_kernel,
        in_specs=[anywhere] * 5,
        out_shape=jax.ShapeDtypeStruct((experts, 8, 128), F32),
        scratch_shapes=[
            pltpu.VMEM((experts, last_rows, 128), BF16),
            pltpu.VMEM((count, tile, slots), BF16),
            pltpu.VMEM((count, tile, slots), BF16),
            pltpu.VMEM((count, late, tile), BF16),
            pltpu.VMEM((16, hidden_count), BF16),
            pltpu.VMEM((late, slots), BF16),
            pltpu.VMEM((1, slots), F32),
            pltpu.SemaphoreType.DMA((3 * count + 2,)),
        ],
        compiler_params=params(),
        cost_estimate=cost(6 * 10**9, 25 * 10**6, 2**22),
        name="expert",
    )(last_in, cand_product, stuff_product, w_up, towers)

    came_back = exchange(produced)

    vmem = pl.BlockSpec(memory_space=pltpu.VMEM)
    scores = pl.pallas_call(
        functools.partial(combine_kernel, capacity),
        in_specs=[smem, vmem, vmem, vmem, vmem],
        out_shape=jax.ShapeDtypeStruct((tasks, rows), F32),
        compiler_params=params(COMBINE_LIMIT),
        cost_estimate=cost(10**8, 10**6),
        name="combine",
    )(lane[None], spots, ids_rows, gates, came_back.reshape(experts * 8, 128))
    return scores.T


def solution(mesh):
    placed = (
        P(("req", "exp"), None),
        P(("req", "exp")),
        P(("req", "exp")),
        P(("req", "exp"), None, None),
        P(("req", "exp")),
        P(),
        P(),
        P(),
        P(),
        P(("req", "exp"), None),
        P("exp", None, None),
        P("exp", None, None),
        P(),
    )
    return jax.shard_map(
        local, mesh=mesh, in_specs=placed, out_specs=P(("req", "exp"), None), check_vma=False
    )
```

time: 119 us -> 116 us (0.975)
  Pallas kernels: 67.8 us -> 59.5 us
  waiting for transfers between devices: 8.32 us -> 12.9 us
  starting transfers between devices: 40.5 us -> 38.3 us
  local copies, waits for them, and re-layouts: 1.28 us -> 3.42 us
    pallas_call x7 -> x6, Pallas kernels: 43.2 us -> 37.5 us  [the longest x1 13.5 us: local(): pl.pallas_call(early_kernel, in_specs=[anywhere] * 3, out_specs=[anywhere...]
    all_to_all x4, waiting for transfers between devices: 8.31 us -> 12.9 us  [exchange(): return lax.all_to_all(item, 'exp', split_axis=0, concat_axis=0, tiled=True)]
    all_to_all x4, starting transfers between devices: 32.5 us -> 30.3 us  [exchange(): return lax.all_to_all(item, 'exp', split_axis=0, concat_axis=0, tiled=True)]
    unnamed x6 -> x18, local copies, waits for them, and re-layouts: 0.66 us -> 2.82 us
    pallas_call x1, Pallas kernels: 2.41 us -> 0.45 us  [local(): pl.pallas_call(functools.partial(gate_kernel, tasks), out_shape=jax.Shape...]
  transfers between devices with their start and end apart: 10 -> 10, of which waited for: 3 -> 3; matrix products, arithmetic and copies ran while one was open for 1% -> 1% of each run, Pallas kernels for 43% -> 38%
where the time goes in v4:
time: 116 us; the launch traced here: 114 us
  Pallas kernels  59.5 us (51%)
  starting transfers between devices  38.3 us (33%)
  waiting for transfers between devices  12.9 us (11%)
  local copies, waits for them, and re-layouts  3.42 us (3%)
    all_to_all x4, starting transfers between devices, exchange(): return lax.all_to_all(item, 'exp', split_axis=0, concat_axis=0, tiled=True)  30.3 us
    pallas_call x1, Pallas kernels, local(): pl.pallas_call(early_kernel, in_specs=[anywhere] * 3, out_specs=[anywhere...  13.5 us
    all_to_all x4, waiting for transfers between devices, exchange(): return lax.all_to_all(item, 'exp', split_axis=0, concat_axis=0, tiled=True)  12.9 us
    pallas_call x2, Pallas kernels, attend(): pl.pallas_call(functools.partial(attend_kernel, chunk), in_specs=[smem] *...  12.4 us
    pallas_call x1, Pallas kernels, local(): pl.pallas_call(expert_kernel, in_specs=[anywhere] * 5, out_shape=jax.Shap...  10.7 us
    ppermute x6, starting transfers between devices, send(): return lax.ppermute(item, 'req', pairs)  8.08 us
    pallas_call x2, Pallas kernels, pack(): pl.pallas_call(functools.partial(pack_kernel, chunk), in_specs=[smem, sme...  7.2 us
    pallas_call x1, Pallas kernels, local(): pl.pallas_call(tower_kernel, in_specs=[pl.BlockSpec(memory_space=pl.ANY),...  6.63 us
  transfers between devices with their start and end apart: 10, of which 3 were waited for; matrix products, arithmetic and copies ran while one was open for 1% of the time, Pallas kernels for 38%

profile of v4, /device:TPU:1, one launch (start us, length us, event | category | flops | bytes accessed | tf_op | source)
XLA Modules:
  0.0 114.4 jit_solution(1933228049360202161)
XLA Ops:
  0.0 0.0 copy-start.7
  0.0 4.0 %pack.2 = (bf16[2064,128]{1,0:T(8,128)(2,1)}, bf16[2064,128]{1,0:T(8,128)(2,1)}, bf16[2064,128]{1,0:T(8,128)(2,1)}, bf16[16,128]{1,0:T(8,128)(2,1)}) custom-call(s32[1]{0:T(128)} %bitcast.2.me_ref, s32[8]{0:T(128)} %ids_ref.3, bf16[4,256,2048]{2,1,0:T(8,128)(2,1)} %bitcast.18), custom_call_target="tpu_custom_call" | custom-call | bytes 1000000 | tf_op jit(solution)/shard_map/pack/pallas_call | solution.py:473
  4.0 2.2 %collective-permute-start = (bf16[2064,128]{1,0:T(8,128)(2,1)}, bf16[2064,128]{1,0:T(8,128)(2,1)S(1)}, u32[]{:S(2)}, u32[]{:S(2)}) collective-permute-start(bf16[2064,128]{1,0:T(8,128)(2,1)} %get-tuple-element.38), channel_id=1, source_target_pairs={{0,32},{32,64},{64,96},{96,0},{1,33},{33,65},{65,97},{97,1},{2,34}... | collective-permute-start | bytes 1585160 | tf_op jit(solution)/shard_map/ppermute | solution.py:489
  6.2 1.5 %collective-permute-start.1 = (bf16[2064,128]{1,0:T(8,128)(2,1)}, bf16[2064,128]{1,0:T(8,128)(2,1)}, u32[]{:S(2)}, u32[]{:S(2)}) collective-permute-start(bf16[2064,128]{1,0:T(8,128)(2,1)} %get-tuple-element.39), channel_id=1, source_target_pairs={{0,96},{32,0},{64,32},{96,64},{1,97},{33,1},{65,33},{97,65},{2,98}... | collective-permute-start | bytes 1585160 | tf_op jit(solution)/shard_map/ppermute | solution.py:489
  7.7 1.6 %collective-permute-start.2 = (bf16[2064,128]{1,0:T(8,128)(2,1)}, bf16[2064,128]{1,0:T(8,128)(2,1)}, u32[]{:S(2)}, u32[]{:S(2)}) collective-permute-start(bf16[2064,128]{1,0:T(8,128)(2,1)} %get-tuple-element.40), channel_id=1, source_target_pairs={{0,64},{32,96},{64,0},{96,32},{1,65},{33,97},{65,1},{97,33},{2,66}... | collective-permute-start | bytes 1585160 | tf_op jit(solution)/shard_map/ppermute | solution.py:489
  9.3 2.6 %route.1 = (s32[8,512]{1,0:T(8,128)}, bf16[256,128]{1,0:T(8,128)(2,1)}, bf16[1024,512]{1,0:T(8,128)(2,1)}) custom-call(s32[2,256]{1,0:T(2,128)} %bitcast.15, s32[1,256]{1,0:T(1,128)} %bitcast.28, bf16[256,1024]{1,0:T(8,128)(2,1)} %cand_ref.4), custom_call_target="tpu_custom_call" | custom-call | flops 500000000 | bytes 3000000 | tf_op jit(solution)/shard_map/route/pallas_call | solution.py:502
  11.8 9.5 %all-to-all-start = ((bf16[32,32,512]{2,1,0:T(8,128)(2,1)}), bf16[32,32,512]{2,1,0:T(8,128)(2,1)}, u32[]{:S(2)}, u32[]{:S(2)}) async-start(bf16[32,32,512]{2,1,0:T(8,128)(2,1)} %bitcast.22), calls=%async_computation | async-start | bytes 2097152 | tf_op jit(solution)/shard_map/all_to_all | solution.py:522
  21.3 3.2 %pack.3 = (bf16[2048,128]{1,0:T(8,128)(2,1)}, bf16[2048,128]{1,0:T(8,128)(2,1)}, bf16[2048,128]{1,0:T(8,128)(2,1)}) custom-call(s32[1]{0:T(128)} %bitcast.2.me_ref, s32[8]{0:T(128)} %ids_ref.3, bf16[4,256,2048]{2,1,0:T(8,128)(2,1)} %bitcast.19), custom_call_target="tpu_custom_call" | custom-call | bytes 1000000 | tf_op jit(solution)/shard_map/pack/pallas_call | solution.py:473
  24.6 0.0 copy-done.7
  24.6 0.6 pad.4.tower_ref
  25.2 5.2 %project.1 = (bf16[256,1024]{1,0:T(8,128)(2,1)}, f32[256,1024]{1,0:T(8,128)}) custom-call(bf16[256,1024]{1,0:T(8,128)(2,1)} %cand_ref.4, bf16[1024,2048]{1,0:T(8,128)(2,1)} %weight_at.1, f32[1,1024]{1,0:T(1,128)} %bitcast.25), custom_call_target="tpu_custom_call" | custom-call | flops 1100000000 | bytes 6000000 | tf_op jit(solution)/shard_map/project/pallas_call | solution.py:529
  30.4 0.0 collective-permute-done.refs_2_.refs_5_
  30.4 0.0 copy-start.8
  30.4 0.5 collective-permute-start.3
  30.9 0.0 collective-permute-done.1.refs_3_.refs_6_
  30.9 2.3 %collective-permute-start.4 = (bf16[2048,128]{1,0:T(8,128)(2,1)}, bf16[2048,128]{1,0:T(8,128)(2,1)}, u32[]{:S(2)}, u32[]{:S(2)}) collective-permute-start(bf16[2048,128]{1,0:T(8,128)(2,1)} %get-tuple-element.46), channel_id=1, source_target_pairs={{0,96},{32,0},{64,32},{96,64},{1,97},{33,1},{65,33},{97,65},{2,98}... | collective-permute-start | bytes 1572872 | tf_op jit(solution)/shard_map/ppermute | solution.py:489
  33.2 0.0 collective-permute-done.2.refs_4_.refs_7_
  33.2 0.1 collective-permute-start.5
  33.2 0.0 copy-done.8
  33.2 6.1 %attend_first.1 = (bf16[1024,512]{1,0:T(8,128)(2,1)}, bf16[256,512]{1,0:T(8,128)(2,1)}, f32[256,128]{1,0:T(8,128)}) custom-call(s32[1]{0:T(128)} %bitcast.2.me_ref, s32[2]{0:T(128)} %hist_ref.3, f32[4,8]{1,0:T(4,128)} %bitcast.26, bf16[256,1024]{1,0:T(8,128)(2,1)} %get-tuple-element.37.refs_0_, bf16[4,256,2048]{2,1,0:T(8,128)(2,1)} %bitcast.20, ...), custom_call_target="tpu_custom_call" | custom-call | flops 30000001024 | bytes 1000000 | tf_op jit(solution)/shard_map/attend_first/pallas_call | solution.py:553
  39.3 0.0 all-to-all-done.cand_at
  39.3 10.8 %all-to-all-start.2 = ((bf16[32,32,512]{2,1,0:T(8,128)(2,1)}), bf16[32,32,512]{2,1,0:T(8,128)(2,1)}, u32[]{:S(2)}, u32[]{:S(2)}) async-start(bf16[32,32,512]{2,1,0:T(8,128)(2,1)} %bitcast.23), calls=%async_computation.2 | async-start | bytes 2097152 | tf_op jit(solution)/shard_map/all_to_all | solution.py:522
  50.2 6.6 %tower.1.tower_at = bf16[16,4096]{1,0:T(8,128)(2,1)} custom-call(bf16[1,4096,1024]{2,1,0:T(8,128)(2,1)} %down_at.1, bf16[16,1024]{1,0:T(8,128)(2,1)} %pad.4.tower_ref), custom_call_target="tpu_custom_call" | custom-call | flops 100000000 | bytes 9000000 | tf_op jit(solution)/shard_map/tower/pallas_call | solution.py:595
  56.8 0.0 collective-permute-done.3.refs_2_
  56.8 0.0 collective-permute-done.4.refs_3_
  56.8 0.0 collective-permute-done.5.refs_4_
  56.8 6.3 %attend_last.1 = (bf16[32,144,128]{2,1,0:T(8,128)(2,1)}, bf16[256,512]{1,0:T(8,128)(2,1)}, f32[256,128]{1,0:T(8,128)}) custom-call(s32[1]{0:T(128)} %bitcast.2.me_ref, s32[2]{0:T(128)} %hist_ref.3, f32[4,8]{1,0:T(4,128)} %bitcast.27, bf16[256,1024]{1,0:T(8,128)(2,1)} %get-tuple-element.37.refs_0_, bf16[4,256,2048]{2,1,0:T(8,128)(2,1)} %bitcast.21, ...), custom_call_target="tpu_custom_call" | custom-call | flops 99999997952 | bytes 1000000 | tf_op jit(solution)/shard_map/attend_last/pallas_call | solution.py:553
  63.1 4.3 %all-to-all-done.2.stuff_at = bf16[32,32,512]{2,1,0:T(8,128)(2,1)} async-done(((bf16[32,32,512]{2,1,0:T(8,128)(2,1)}), bf16[32,32,512]{2,1,0:T(8,128)(2,1)}, u32[]{:S(2)}, u32[]{:S(2)}) %all-to-all-start.2) | async-done | bytes 1048608 | tf_op jit(solution)/shard_map/all_to_all | solution.py:522
  67.4 4.8 %all-to-all-start.1 = ((bf16[32,144,128]{2,1,0:T(8,128)(2,1)}), bf16[32,144,128]{2,1,0:T(8,128)(2,1)}, u32[]{:S(2)}, u32[]{:S(2)}) async-start(bf16[32,144,128]{2,1,0:T(8,128)(2,1)} %get-tuple-element.55), calls=%async_computation.1 | async-start | bytes 2359296 | tf_op jit(solution)/shard_map/all_to_all | solution.py:522
  72.2 13.5 %early.1 = (bf16[4096,1024]{1,0:T(8,128)(2,1)}, bf16[4096,1024]{1,0:T(8,128)(2,1)}) custom-call(bf16[32,32,512]{2,1,0:T(8,128)(2,1)} %all-to-all-done.cand_at, bf16[32,32,512]{2,1,0:T(8,128)(2,1)} %all-to-all-done.2.stuff_at, bf16[1,1024,4096]{2,1,0:T(8,128)(2,1)} %up_at.3), custom_call_target="tpu_custom_call" | custom-call | flops 5000000000 | bytes 1000000 | tf_op jit(solution)/shard_map/early/pallas_call | solution.py:628
  85.7 4.2 %all-to-all-done.1.last_at = bf16[32,144,128]{2,1,0:T(8,128)(2,1)} async-done(((bf16[32,144,128]{2,1,0:T(8,128)(2,1)}), bf16[32,144,128]{2,1,0:T(8,128)(2,1)}, u32[]{:S(2)}, u32[]{:S(2)}) %all-to-all-start.1) | async-done | bytes 1179680 | tf_op jit(solution)/shard_map/all_to_all | solution.py:522
  89.9 0.0 copy-start
  89.9 0.0 copy-start.1
  89.9 0.0 copy-start.5
  89.9 0.0 copy-start.6
  89.9 10.7 %expert.1 = f32[32,8,128]{2,1,0:T(8,128)} custom-call(bf16[32,144,128]{2,1,0:T(8,128)(2,1)} %all-to-all-done.1.last_at, bf16[4096,1024]{1,0:T(8,128)(2,1)} %get-tuple-element.57.cand_product_at, bf16[4096,1024]{1,0:T(8,128)(2,1)} %get-tuple-element.58.stuff_product_at, bf16[1,1024,4096]{2,1,0:T(8,128)(2,1)} %up_at.3, bf16[16,4096]{1,0:T(8,128)(2,1)} %tower.1.tower_at), custom_call_target="tpu_custom_call" | custom-call | flops 6000000000 | bytes 25000000 | tf_op jit(solution)/shard_map/expert/pallas_call | solution.py:655
  100.6 5.1 %all-to-all-start.3 = ((f32[32,8,128]{2,1,0:T(8,128)}), f32[32,8,128]{2,1,0:T(8,128)S(1)}, u32[]{:S(2)}, u32[]{:S(2)}) async-start(f32[32,8,128]{2,1,0:T(8,128)} %expert.1), calls=%async_computation.3 | async-start | bytes 262144 | tf_op jit(solution)/shard_map/all_to_all | solution.py:522
  105.7 0.0 copy-done
  105.7 0.0 copy-done.1
  105.7 0.0 copy-done.5
  105.7 0.0 copy-start.2
  105.7 0.9 copy-done.2
  106.7 0.0 copy-start.3
  106.7 0.9 copy-done.3
  107.6 0.0 copy-start.4
  107.6 0.9 copy-done.4
  108.5 0.4 gate.1.gate_ref
  109.0 4.4 %all-to-all-done.3 = f32[32,8,128]{2,1,0:T(8,128)S(1)} async-done(((f32[32,8,128]{2,1,0:T(8,128)}), f32[32,8,128]{2,1,0:T(8,128)S(1)}, u32[]{:S(2)}, u32[]{:S(2)}) %all-to-all-start.3) | async-done | bytes 131104 | tf_op jit(solution)/shard_map/all_to_all | solution.py:522
  113.4 0.0 copy-done.6
  113.4 1.0 combine.1
Async XLA Ops:
  0.0 24.6 %copy-start.7 = (bf16[1024,6]{0,1:T(8,128)(2,1)S(1)}, bf16[1024,6]{0,1:T(8,128)(2,1)}, u32[]{:S(2)}) copy-start(bf16[1024,6]{0,1:T(8,128)(2,1)} %param.25) | copy-start | bytes 36868
  4.0 26.4 %collective-permute-start = (bf16[2064,128]{1,0:T(8,128)(2,1)}, bf16[2064,128]{1,0:T(8,128)(2,1)S(1)}, u32[]{:S(2)}, u32[]{:S(2)}) collective-permute-start(bf16[2064,128]{1,0:T(8,128)(2,1)} %get-tuple-element.38), channel_id=1, source_target_pairs={{0,32},{32,64},{64,96},{96,0},{1,33},{33,65},{65,97},{97,1},{2,34}... | collective-permute-start | bytes 1585160 | tf_op jit(solution)/shard_map/ppermute | solution.py:489
  6.2 24.7 %collective-permute-start.1 = (bf16[2064,128]{1,0:T(8,128)(2,1)}, bf16[2064,128]{1,0:T(8,128)(2,1)}, u32[]{:S(2)}, u32[]{:S(2)}) collective-permute-start(bf16[2064,128]{1,0:T(8,128)(2,1)} %get-tuple-element.39), channel_id=1, source_target_pairs={{0,96},{32,0},{64,32},{96,64},{1,97},{33,1},{65,33},{97,65},{2,98}... | collective-permute-start | bytes 1585160 | tf_op jit(solution)/shard_map/ppermute | solution.py:489
  7.7 25.5 %collective-permute-start.2 = (bf16[2064,128]{1,0:T(8,128)(2,1)}, bf16[2064,128]{1,0:T(8,128)(2,1)}, u32[]{:S(2)}, u32[]{:S(2)}) collective-permute-start(bf16[2064,128]{1,0:T(8,128)(2,1)} %get-tuple-element.40), channel_id=1, source_target_pairs={{0,64},{32,96},{64,0},{96,32},{1,65},{33,97},{65,1},{97,33},{2,66}... | collective-permute-start | bytes 1585160 | tf_op jit(solution)/shard_map/ppermute | solution.py:489
  11.8 27.5 %all-to-all-start = ((bf16[32,32,512]{2,1,0:T(8,128)(2,1)}), bf16[32,32,512]{2,1,0:T(8,128)(2,1)}, u32[]{:S(2)}, u32[]{:S(2)}) async-start(bf16[32,32,512]{2,1,0:T(8,128)(2,1)} %bitcast.22), calls=%async_computation | async-start | bytes 2097152 | tf_op jit(solution)/shard_map/all_to_all | solution.py:522
  30.4 2.8 %copy-start.8 = (bf16[2064,128]{1,0:T(8,128)(2,1)}, bf16[2064,128]{1,0:T(8,128)(2,1)S(1)}, u32[]{:S(2)}) copy-start(bf16[2064,128]{1,0:T(8,128)(2,1)S(1)} %collective-permute-done.refs_2_.refs_5_) | copy-start | bytes 1585156
  30.4 26.4 %collective-permute-start.3 = (bf16[2048,128]{1,0:T(8,128)(2,1)}, bf16[2048,128]{1,0:T(8,128)(2,1)}, u32[]{:S(2)}, u32[]{:S(2)}) collective-permute-start(bf16[2048,128]{1,0:T(8,128)(2,1)} %get-tuple-element.44), channel_id=1, source_target_pairs={{0,32},{32,64},{64,96},{96,0},{1,33},{33,65},{65,97},{97,1},{2,34}... | collective-permute-start | bytes 1572872 | tf_op jit(solution)/shard_map/ppermute | solution.py:489
  30.9 25.9 %collective-permute-start.4 = (bf16[2048,128]{1,0:T(8,128)(2,1)}, bf16[2048,128]{1,0:T(8,128)(2,1)}, u32[]{:S(2)}, u32[]{:S(2)}) collective-permute-start(bf16[2048,128]{1,0:T(8,128)(2,1)} %get-tuple-element.46), channel_id=1, source_target_pairs={{0,96},{32,0},{64,32},{96,64},{1,97},{33,1},{65,33},{97,65},{2,98}... | collective-permute-start | bytes 1572872 | tf_op jit(solution)/shard_map/ppermute | solution.py:489
  33.2 23.7 %collective-permute-start.5 = (bf16[2048,128]{1,0:T(8,128)(2,1)}, bf16[2048,128]{1,0:T(8,128)(2,1)}, u32[]{:S(2)}, u32[]{:S(2)}) collective-permute-start(bf16[2048,128]{1,0:T(8,128)(2,1)} %get-tuple-element.48), channel_id=1, source_target_pairs={{0,64},{32,96},{64,0},{96,32},{1,65},{33,97},{65,1},{97,33},{2,66}... | collective-permute-start | bytes 1572872 | tf_op jit(solution)/shard_map/ppermute | solution.py:489
  39.3 28.1 %all-to-all-start.2 = ((bf16[32,32,512]{2,1,0:T(8,128)(2,1)}), bf16[32,32,512]{2,1,0:T(8,128)(2,1)}, u32[]{:S(2)}, u32[]{:S(2)}) async-start(bf16[32,32,512]{2,1,0:T(8,128)(2,1)} %bitcast.23), calls=%async_computation.2 | async-start | bytes 2097152 | tf_op jit(solution)/shard_map/all_to_all | solution.py:522
  67.4 22.5 %all-to-all-start.1 = ((bf16[32,144,128]{2,1,0:T(8,128)(2,1)}), bf16[32,144,128]{2,1,0:T(8,128)(2,1)}, u32[]{:S(2)}, u32[]{:S(2)}) async-start(bf16[32,144,128]{2,1,0:T(8,128)(2,1)} %get-tuple-element.55), calls=%async_computation.1 | async-start | bytes 2359296 | tf_op jit(solution)/shard_map/all_to_all | solution.py:522
  89.9 15.8 %copy-start = (bf16[256,1024]{1,0:T(8,128)(2,1)S(1)}, bf16[256,1024]{1,0:T(8,128)(2,1)}, u32[]{:S(2)}) copy-start(bf16[256,1024]{1,0:T(8,128)(2,1)} %cand_ref.4) | copy-start | bytes 1572868
  89.9 15.8 %copy-start.1 = (bf16[1024,192]{0,1:T(8,128)(2,1)S(1)}, bf16[1024,192]{0,1:T(8,128)(2,1)}, u32[]{:S(2)}) copy-start(bf16[1024,192]{0,1:T(8,128)(2,1)} %param.21) | copy-start | bytes 1179652
  89.9 15.8 %copy-start.5 = (s32[256,2]{0,1:T(2,128)S(1)}, s32[256,2]{0,1:T(2,128)}, u32[]{:S(2)}) copy-start(s32[256,2]{0,1:T(2,128)} %param.22) | copy-start | bytes 6148
  89.9 23.5 %copy-start.6 = (s32[8,512]{1,0:T(8,128)S(1)}, s32[8,512]{1,0:T(8,128)}, u32[]{:S(2)}) copy-start(s32[8,512]{1,0:T(8,128)} %get-tuple-element.34.refs_11_.spot_ref) | copy-start | bytes 49156
  100.6 12.8 %all-to-all-start.3 = ((f32[32,8,128]{2,1,0:T(8,128)}), f32[32,8,128]{2,1,0:T(8,128)S(1)}, u32[]{:S(2)}, u32[]{:S(2)}) async-start(f32[32,8,128]{2,1,0:T(8,128)} %expert.1), calls=%async_computation.3 | async-start | bytes 262144 | tf_op jit(solution)/shard_map/all_to_all | solution.py:522
  105.7 1.0 copy-start.2
  106.7 0.9 copy-start.3
  107.6 0.9 copy-start.4

commit v5 on v4

--- a/solution.py
+++ b/solution.py
@@ -390,29 +390,54 @@
         part = jnp.dot(tower[:, pl.ds(i * tile, tile)], hidden, preferred_element_type=F32)
         total = part if total is None else total + part
     found = total[0:8, :] + total[8:16, :]
-    for peer in range(peers):
-        out_ref[peer] = found[:, (peer // each) * 128 : (peer // each + 1) * 128]
-
-
-def combine_kernel(capacity, lane_ref, spot_ref, ids_ref, gate_ref, back_ref, out_ref):
+    row = lax.broadcasted_iota(jnp.int32, (8, 128), 0)
+    mine = lax.broadcasted_iota(jnp.int32, (8, 128), 1) // share == row % each
+    for group in range(peers // each):
+        tile = found[:, group * 128 : (group + 1) * 128]
+        turns = [tile] + [pltpu.roll(tile, k * share, 1) for k in range(1, each)]
+        for i in range(each):
+            kept = jnp.zeros((8, 128), F32)
+            for k in range(each):
+                kept = jnp.where(mine & (row % each == (i + k) % each), turns[k], kept)
+            rows_out = []
+            for half in range(2):
+                line = kept[half * 4 : half * 4 + 1]
+                for j in range(1, 4):
+                    line = line + kept[half * 4 + j : half * 4 + j + 1]
+                rows_out.append(line)
+            out_ref[group * each + i] = jnp.concatenate(rows_out, axis=0)
+
+
+def combine_kernel(capacity, spot_ref, ids_ref, gate_ref, back_ref, out_ref):
     rows = ids_ref.shape[1]
-    experts = back_ref.shape[0] // 8
+    experts = back_ref.shape[0] // 2
     ids = jnp.concatenate([ids_ref[0:1, :], ids_ref[1:2, :]], axis=1)
-    lane = spot_ref[0:1, :] - ids * capacity + lane_ref[0]
-    hot = lax.broadcasted_iota(jnp.int32, (128, 2 * rows), 0) == lane
-    hot = jnp.where(hot, 1.0, 0.0).astype(BF16)
+    position = spot_ref[0:1, :] - ids * capacity
     back = back_ref[...]
     high = back.astype(BF16)
     rest = back - high.astype(F32)
     middle = rest.astype(BF16)
     low = (rest - middle.astype(F32)).astype(BF16)
-    found = jnp.dot(high, hot, preferred_element_type=F32)
-    found += jnp.dot(middle, hot, preferred_element_type=F32)
-    found += jnp.dot(low, hot, preferred_element_type=F32)
-    total = jnp.zeros((8, 2 * rows), F32)
-    for expert in range(experts):
-        total = jnp.where(ids == expert, found[expert * 8 : (expert + 1) * 8], total)
-    total = total * gate_ref[...]
+    lanes = lax.broadcasted_iota(jnp.int32, (128, 2 * rows), 0)
+    picked = []
+    for task in range(128 // capacity):
+        hot = jnp.where(lanes == position + task * capacity, 1.0, 0.0).astype(BF16)
+        found = jnp.dot(high, hot, preferred_element_type=F32)
+        found += jnp.dot(middle, hot, preferred_element_type=F32)
+        found += jnp.dot(low, hot, preferred_element_type=F32)
+        total = jnp.zeros((8, 2 * rows), F32)
+        for group in range(experts // 4):
+            owner = group * 4 + lax.broadcasted_iota(jnp.int32, (8, 2 * rows), 0) // 2
+            total = total + jnp.where(ids == owner, found[group * 8 : (group + 1) * 8], 0.0)
+        picked.append(total)
+    lines = []
+    for half in range(2):
+        for total in picked:
+            line = total[half : half + 1]
+            for pair in range(1, 4):
+                line = line + total[2 * pair + half : 2 * pair + half + 1]
+            lines.append(line)
+    total = jnp.concatenate(lines, axis=0) * gate_ref[...]
     total = total[:, :rows] + total[:, rows:]
     out_ref[...] = total[: out_ref.shape[0]]
 
@@ -497,8 +522,6 @@
         last_moved.append(send(item, shift))
 
     ids_rows, _ = lax.optimization_barrier((expert_ids.T, own_tile))
-    each = 128 // capacity
-    lane = lax.rem(lax.axis_index("exp").astype(jnp.int32), each) * capacity
     spots, first, cand_out = pl.pallas_call(
         functools.partial(route_kernel, capacity),
         grid=(1,),
@@ -655,7 +678,7 @@
     produced = pl.pallas_call(
         expert_kernel,
         in_specs=[anywhere] * 5,
-        out_shape=jax.ShapeDtypeStruct((experts, 8, 128), F32),
+        out_shape=jax.ShapeDtypeStruct((experts, 2, 128), F32),
         scratch_shapes=[
             pltpu.VMEM((experts, last_rows, 128), BF16),
             pltpu.VMEM((count, tile, slots), BF16),
@@ -676,12 +699,12 @@
     vmem = pl.BlockSpec(memory_space=pltpu.VMEM)
     scores = pl.pallas_call(
         functools.partial(combine_kernel, capacity),
-        in_specs=[smem, vmem, vmem, vmem, vmem],
+        in_specs=[vmem, vmem, vmem, vmem],
         out_shape=jax.ShapeDtypeStruct((tasks, rows), F32),
         compiler_params=params(COMBINE_LIMIT),
         cost_estimate=cost(10**8, 10**6),
         name="combine",
-    )(lane[None], spots, ids_rows, gates, came_back.reshape(experts * 8, 128))
+    )(spots, ids_rows, gates, came_back.reshape(experts * 2, 128))
     return scores.T
 
 

time: 116 us -> 115 us (level)
  no operation moved by 1% of the time
where the time goes in v5:
time: 115 us; the launch traced here: 114 us
  Pallas kernels  59.6 us (52%)
  starting transfers between devices  38.3 us (33%)
  waiting for transfers between devices  12.5 us (11%)
  local copies, waits for them, and re-layouts  3.42 us (3%)
    all_to_all x4, starting transfers between devices, exchange(): return lax.all_to_all(item, 'exp', split_axis=0, concat_axis=0, tiled=True)  30.2 us
    pallas_call x1, Pallas kernels, local(): pl.pallas_call(early_kernel, in_specs=[anywhere] * 3, out_specs=[anywhere...  13.5 us
    all_to_all x4, waiting for transfers between devices, exchange(): return lax.all_to_all(item, 'exp', split_axis=0, concat_axis=0, tiled=True)  12.5 us
    pallas_call x2, Pallas kernels, attend(): pl.pallas_call(functools.partial(attend_kernel, chunk), in_specs=[smem] *...  12.4 us
    pallas_call x1, Pallas kernels, local(): pl.pallas_call(expert_kernel, in_specs=[anywhere] * 5, out_shape=jax.Shap...  10.7 us
    ppermute x6, starting transfers between devices, send(): return lax.ppermute(item, 'req', pairs)  8.08 us
    pallas_call x2, Pallas kernels, pack(): pl.pallas_call(functools.partial(pack_kernel, chunk), in_specs=[smem, sme...  7.2 us
    pallas_call x1, Pallas kernels, local(): pl.pallas_call(tower_kernel, in_specs=[pl.BlockSpec(memory_space=pl.ANY),...  6.63 us
  transfers between devices with their start and end apart: 10, of which 3 were waited for; matrix products, arithmetic and copies ran while one was open for 1% of the time, Pallas kernels for 38%

profile of v5, /device:TPU:1, one launch (start us, length us, event | category | flops | bytes accessed | tf_op | source)
XLA Modules:
  0.0 114.1 jit_solution(7242662621091116188)
XLA Ops:
  0.0 0.0 copy-start.7
  0.0 4.0 %pack.2 = (bf16[2064,128]{1,0:T(8,128)(2,1)}, bf16[2064,128]{1,0:T(8,128)(2,1)}, bf16[2064,128]{1,0:T(8,128)(2,1)}, bf16[16,128]{1,0:T(8,128)(2,1)}) custom-call(s32[1]{0:T(128)} %bitcast.1.me_ref, s32[8]{0:T(128)} %ids_ref.3, bf16[4,256,2048]{2,1,0:T(8,128)(2,1)} %bitcast.17), custom_call_target="tpu_custom_call" | custom-call | bytes 1000000 | tf_op jit(solution)/shard_map/pack/pallas_call | solution.py:498
  4.0 2.2 %collective-permute-start = (bf16[2064,128]{1,0:T(8,128)(2,1)}, bf16[2064,128]{1,0:T(8,128)(2,1)S(1)}, u32[]{:S(2)}, u32[]{:S(2)}) collective-permute-start(bf16[2064,128]{1,0:T(8,128)(2,1)} %get-tuple-element.38), channel_id=1, source_target_pairs={{0,32},{32,64},{64,96},{96,0},{1,33},{33,65},{65,97},{97,1},{2,34}... | collective-permute-start | bytes 1585160 | tf_op jit(solution)/shard_map/ppermute | solution.py:514
  6.2 1.5 %collective-permute-start.1 = (bf16[2064,128]{1,0:T(8,128)(2,1)}, bf16[2064,128]{1,0:T(8,128)(2,1)}, u32[]{:S(2)}, u32[]{:S(2)}) collective-permute-start(bf16[2064,128]{1,0:T(8,128)(2,1)} %get-tuple-element.39), channel_id=1, source_target_pairs={{0,96},{32,0},{64,32},{96,64},{1,97},{33,1},{65,33},{97,65},{2,98}... | collective-permute-start | bytes 1585160 | tf_op jit(solution)/shard_map/ppermute | solution.py:514
  7.7 1.6 %collective-permute-start.2 = (bf16[2064,128]{1,0:T(8,128)(2,1)}, bf16[2064,128]{1,0:T(8,128)(2,1)}, u32[]{:S(2)}, u32[]{:S(2)}) collective-permute-start(bf16[2064,128]{1,0:T(8,128)(2,1)} %get-tuple-element.40), channel_id=1, source_target_pairs={{0,64},{32,96},{64,0},{96,32},{1,65},{33,97},{65,1},{97,33},{2,66}... | collective-permute-start | bytes 1585160 | tf_op jit(solution)/shard_map/ppermute | solution.py:514
  9.3 2.6 %route.1 = (s32[8,512]{1,0:T(8,128)}, bf16[256,128]{1,0:T(8,128)(2,1)}, bf16[1024,512]{1,0:T(8,128)(2,1)}) custom-call(s32[2,256]{1,0:T(2,128)} %bitcast.14, s32[1,256]{1,0:T(1,128)} %bitcast.27, bf16[256,1024]{1,0:T(8,128)(2,1)} %cand_ref.4), custom_call_target="tpu_custom_call" | custom-call | flops 500000000 | bytes 3000000 | tf_op jit(solution)/shard_map/route/pallas_call | solution.py:525
  11.8 9.5 %all-to-all-start = ((bf16[32,32,512]{2,1,0:T(8,128)(2,1)}), bf16[32,32,512]{2,1,0:T(8,128)(2,1)}, u32[]{:S(2)}, u32[]{:S(2)}) async-start(bf16[32,32,512]{2,1,0:T(8,128)(2,1)} %bitcast.21), calls=%async_computation | async-start | bytes 2097152 | tf_op jit(solution)/shard_map/all_to_all | solution.py:545
  21.3 3.2 %pack.3 = (bf16[2048,128]{1,0:T(8,128)(2,1)}, bf16[2048,128]{1,0:T(8,128)(2,1)}, bf16[2048,128]{1,0:T(8,128)(2,1)}) custom-call(s32[1]{0:T(128)} %bitcast.1.me_ref, s32[8]{0:T(128)} %ids_ref.3, bf16[4,256,2048]{2,1,0:T(8,128)(2,1)} %bitcast.18), custom_call_target="tpu_custom_call" | custom-call | bytes 1000000 | tf_op jit(solution)/shard_map/pack/pallas_call | solution.py:498
  24.6 0.0 copy-done.7
  24.6 0.6 pad.4.tower_ref
  25.2 5.2 %project.1 = (bf16[256,1024]{1,0:T(8,128)(2,1)}, f32[256,1024]{1,0:T(8,128)}) custom-call(bf16[256,1024]{1,0:T(8,128)(2,1)} %cand_ref.4, bf16[1024,2048]{1,0:T(8,128)(2,1)} %weight_at.1, f32[1,1024]{1,0:T(1,128)} %bitcast.24), custom_call_target="tpu_custom_call" | custom-call | flops 1100000000 | bytes 6000000 | tf_op jit(solution)/shard_map/project/pallas_call | solution.py:552
  30.4 0.0 collective-permute-done.refs_2_.refs_5_
  30.4 0.0 copy-start.8
  30.4 0.5 collective-permute-start.3
  30.9 0.0 collective-permute-done.1.refs_3_.refs_6_
  30.9 2.3 %collective-permute-start.4 = (bf16[2048,128]{1,0:T(8,128)(2,1)}, bf16[2048,128]{1,0:T(8,128)(2,1)}, u32[]{:S(2)}, u32[]{:S(2)}) collective-permute-start(bf16[2048,128]{1,0:T(8,128)(2,1)} %get-tuple-element.46), channel_id=1, source_target_pairs={{0,96},{32,0},{64,32},{96,64},{1,97},{33,1},{65,33},{97,65},{2,98}... | collective-permute-start | bytes 1572872 | tf_op jit(solution)/shard_map/ppermute | solution.py:514
  33.2 0.0 collective-permute-done.2.refs_4_.refs_7_
  33.2 0.1 collective-permute-start.5
  33.2 0.0 copy-done.8
  33.2 6.1 %attend_first.1 = (bf16[1024,512]{1,0:T(8,128)(2,1)}, bf16[256,512]{1,0:T(8,128)(2,1)}, f32[256,128]{1,0:T(8,128)}) custom-call(s32[1]{0:T(128)} %bitcast.1.me_ref, s32[2]{0:T(128)} %hist_ref.3, f32[4,8]{1,0:T(4,128)} %bitcast.25, bf16[256,1024]{1,0:T(8,128)(2,1)} %get-tuple-element.37.refs_0_, bf16[4,256,2048]{2,1,0:T(8,128)(2,1)} %bitcast.19, ...), custom_call_target="tpu_custom_call" | custom-call | flops 30000001024 | bytes 1000000 | tf_op jit(solution)/shard_map/attend_first/pallas_call | solution.py:576
  39.3 0.0 all-to-all-done.cand_at
  39.3 10.8 %all-to-all-start.2 = ((bf16[32,32,512]{2,1,0:T(8,128)(2,1)}), bf16[32,32,512]{2,1,0:T(8,128)(2,1)}, u32[]{:S(2)}, u32[]{:S(2)}) async-start(bf16[32,32,512]{2,1,0:T(8,128)(2,1)} %bitcast.22), calls=%async_computation.2 | async-start | bytes 2097152 | tf_op jit(solution)/shard_map/all_to_all | solution.py:545
  50.2 6.6 %tower.1.tower_at = bf16[16,4096]{1,0:T(8,128)(2,1)} custom-call(bf16[1,4096,1024]{2,1,0:T(8,128)(2,1)} %down_at.1, bf16[16,1024]{1,0:T(8,128)(2,1)} %pad.4.tower_ref), custom_call_target="tpu_custom_call" | custom-call | flops 100000000 | bytes 9000000 | tf_op jit(solution)/shard_map/tower/pallas_call | solution.py:618
  56.8 0.0 collective-permute-done.3.refs_2_
  56.8 0.0 collective-permute-done.4.refs_3_
  56.8 0.0 collective-permute-done.5.refs_4_
  56.8 6.3 %attend_last.1 = (bf16[32,144,128]{2,1,0:T(8,128)(2,1)}, bf16[256,512]{1,0:T(8,128)(2,1)}, f32[256,128]{1,0:T(8,128)}) custom-call(s32[1]{0:T(128)} %bitcast.1.me_ref, s32[2]{0:T(128)} %hist_ref.3, f32[4,8]{1,0:T(4,128)} %bitcast.26, bf16[256,1024]{1,0:T(8,128)(2,1)} %get-tuple-element.37.refs_0_, bf16[4,256,2048]{2,1,0:T(8,128)(2,1)} %bitcast.20, ...), custom_call_target="tpu_custom_call" | custom-call | flops 99999997952 | bytes 1000000 | tf_op jit(solution)/shard_map/attend_last/pallas_call | solution.py:576
  63.1 4.3 %all-to-all-done.2.stuff_at = bf16[32,32,512]{2,1,0:T(8,128)(2,1)} async-done(((bf16[32,32,512]{2,1,0:T(8,128)(2,1)}), bf16[32,32,512]{2,1,0:T(8,128)(2,1)}, u32[]{:S(2)}, u32[]{:S(2)}) %all-to-all-start.2) | async-done | bytes 1048608 | tf_op jit(solution)/shard_map/all_to_all | solution.py:545
  67.4 4.8 %all-to-all-start.1 = ((bf16[32,144,128]{2,1,0:T(8,128)(2,1)}), bf16[32,144,128]{2,1,0:T(8,128)(2,1)}, u32[]{:S(2)}, u32[]{:S(2)}) async-start(bf16[32,144,128]{2,1,0:T(8,128)(2,1)} %get-tuple-element.55), calls=%async_computation.1 | async-start | bytes 2359296 | tf_op jit(solution)/shard_map/all_to_all | solution.py:545
  72.2 13.5 %early.1 = (bf16[4096,1024]{1,0:T(8,128)(2,1)}, bf16[4096,1024]{1,0:T(8,128)(2,1)}) custom-call(bf16[32,32,512]{2,1,0:T(8,128)(2,1)} %all-to-all-done.cand_at, bf16[32,32,512]{2,1,0:T(8,128)(2,1)} %all-to-all-done.2.stuff_at, bf16[1,1024,4096]{2,1,0:T(8,128)(2,1)} %up_at.3), custom_call_target="tpu_custom_call" | custom-call | flops 5000000000 | bytes 1000000 | tf_op jit(solution)/shard_map/early/pallas_call | solution.py:651
  85.7 4.2 %all-to-all-done.1.last_at = bf16[32,144,128]{2,1,0:T(8,128)(2,1)} async-done(((bf16[32,144,128]{2,1,0:T(8,128)(2,1)}), bf16[32,144,128]{2,1,0:T(8,128)(2,1)}, u32[]{:S(2)}, u32[]{:S(2)}) %all-to-all-start.1) | async-done | bytes 1179680 | tf_op jit(solution)/shard_map/all_to_all | solution.py:545
  89.9 0.0 copy-start
  89.9 0.0 copy-start.1
  89.9 0.0 copy-start.5
  89.9 0.0 copy-start.6
  89.9 10.7 %expert.1 = f32[32,2,128]{2,1,0:T(2,128)} custom-call(bf16[32,144,128]{2,1,0:T(8,128)(2,1)} %all-to-all-done.1.last_at, bf16[4096,1024]{1,0:T(8,128)(2,1)} %get-tuple-element.57.cand_product_at, bf16[4096,1024]{1,0:T(8,128)(2,1)} %get-tuple-element.58.stuff_product_at, bf16[1,1024,4096]{2,1,0:T(8,128)(2,1)} %up_at.3, bf16[16,4096]{1,0:T(8,128)(2,1)} %tower.1.tower_at), custom_call_target="tpu_custom_call" | custom-call | flops 6000000000 | bytes 25000000 | tf_op jit(solution)/shard_map/expert/pallas_call | solution.py:678
  100.7 5.0 %all-to-all-start.3 = ((f32[32,2,128]{2,1,0:T(2,128)}), f32[32,2,128]{2,1,0:T(2,128)S(1)}, u32[]{:S(2)}, u32[]{:S(2)}) async-start(f32[32,2,128]{2,1,0:T(2,128)} %expert.1), calls=%async_computation.3 | async-start | bytes 65536 | tf_op jit(solution)/shard_map/all_to_all | solution.py:545
  105.7 0.0 copy-done
  105.7 0.0 copy-done.1
  105.7 0.0 copy-done.5
  105.7 0.0 copy-start.2
  105.7 0.9 copy-done.2
  106.7 0.0 copy-start.3
  106.7 0.9 copy-done.3
  107.6 0.0 copy-start.4
  107.6 0.9 copy-done.4
  108.5 0.5 gate.1.gate_ref
  109.0 4.1 %all-to-all-done.3 = f32[32,2,128]{2,1,0:T(2,128)S(1)} async-done(((f32[32,2,128]{2,1,0:T(2,128)}), f32[32,2,128]{2,1,0:T(2,128)S(1)}, u32[]{:S(2)}, u32[]{:S(2)}) %all-to-all-start.3) | async-done | bytes 32800 | tf_op jit(solution)/shard_map/all_to_all | solution.py:545
  113.1 0.0 copy-done.6
  113.1 1.0 combine.1
Async XLA Ops:
  0.0 24.6 %copy-start.7 = (bf16[1024,6]{0,1:T(8,128)(2,1)S(1)}, bf16[1024,6]{0,1:T(8,128)(2,1)}, u32[]{:S(2)}) copy-start(bf16[1024,6]{0,1:T(8,128)(2,1)} %param.25) | copy-start | bytes 36868
  4.0 26.4 %collective-permute-start = (bf16[2064,128]{1,0:T(8,128)(2,1)}, bf16[2064,128]{1,0:T(8,128)(2,1)S(1)}, u32[]{:S(2)}, u32[]{:S(2)}) collective-permute-start(bf16[2064,128]{1,0:T(8,128)(2,1)} %get-tuple-element.38), channel_id=1, source_target_pairs={{0,32},{32,64},{64,96},{96,0},{1,33},{33,65},{65,97},{97,1},{2,34}... | collective-permute-start | bytes 1585160 | tf_op jit(solution)/shard_map/ppermute | solution.py:514
  6.2 24.7 %collective-permute-start.1 = (bf16[2064,128]{1,0:T(8,128)(2,1)}, bf16[2064,128]{1,0:T(8,128)(2,1)}, u32[]{:S(2)}, u32[]{:S(2)}) collective-permute-start(bf16[2064,128]{1,0:T(8,128)(2,1)} %get-tuple-element.39), channel_id=1, source_target_pairs={{0,96},{32,0},{64,32},{96,64},{1,97},{33,1},{65,33},{97,65},{2,98}... | collective-permute-start | bytes 1585160 | tf_op jit(solution)/shard_map/ppermute | solution.py:514
  7.7 25.5 %collective-permute-start.2 = (bf16[2064,128]{1,0:T(8,128)(2,1)}, bf16[2064,128]{1,0:T(8,128)(2,1)}, u32[]{:S(2)}, u32[]{:S(2)}) collective-permute-start(bf16[2064,128]{1,0:T(8,128)(2,1)} %get-tuple-element.40), channel_id=1, source_target_pairs={{0,64},{32,96},{64,0},{96,32},{1,65},{33,97},{65,1},{97,33},{2,66}... | collective-permute-start | bytes 1585160 | tf_op jit(solution)/shard_map/ppermute | solution.py:514
  11.8 27.5 %all-to-all-start = ((bf16[32,32,512]{2,1,0:T(8,128)(2,1)}), bf16[32,32,512]{2,1,0:T(8,128)(2,1)}, u32[]{:S(2)}, u32[]{:S(2)}) async-start(bf16[32,32,512]{2,1,0:T(8,128)(2,1)} %bitcast.21), calls=%async_computation | async-start | bytes 2097152 | tf_op jit(solution)/shard_map/all_to_all | solution.py:545
  30.4 2.8 %copy-start.8 = (bf16[2064,128]{1,0:T(8,128)(2,1)}, bf16[2064,128]{1,0:T(8,128)(2,1)S(1)}, u32[]{:S(2)}) copy-start(bf16[2064,128]{1,0:T(8,128)(2,1)S(1)} %collective-permute-done.refs_2_.refs_5_) | copy-start | bytes 1585156
  30.4 26.4 %collective-permute-start.3 = (bf16[2048,128]{1,0:T(8,128)(2,1)}, bf16[2048,128]{1,0:T(8,128)(2,1)}, u32[]{:S(2)}, u32[]{:S(2)}) collective-permute-start(bf16[2048,128]{1,0:T(8,128)(2,1)} %get-tuple-element.44), channel_id=1, source_target_pairs={{0,32},{32,64},{64,96},{96,0},{1,33},{33,65},{65,97},{97,1},{2,34}... | collective-permute-start | bytes 1572872 | tf_op jit(solution)/shard_map/ppermute | solution.py:514
  30.9 25.9 %collective-permute-start.4 = (bf16[2048,128]{1,0:T(8,128)(2,1)}, bf16[2048,128]{1,0:T(8,128)(2,1)}, u32[]{:S(2)}, u32[]{:S(2)}) collective-permute-start(bf16[2048,128]{1,0:T(8,128)(2,1)} %get-tuple-element.46), channel_id=1, source_target_pairs={{0,96},{32,0},{64,32},{96,64},{1,97},{33,1},{65,33},{97,65},{2,98}... | collective-permute-start | bytes 1572872 | tf_op jit(solution)/shard_map/ppermute | solution.py:514
  33.2 23.7 %collective-permute-start.5 = (bf16[2048,128]{1,0:T(8,128)(2,1)}, bf16[2048,128]{1,0:T(8,128)(2,1)}, u32[]{:S(2)}, u32[]{:S(2)}) collective-permute-start(bf16[2048,128]{1,0:T(8,128)(2,1)} %get-tuple-element.48), channel_id=1, source_target_pairs={{0,64},{32,96},{64,0},{96,32},{1,65},{33,97},{65,1},{97,33},{2,66}... | collective-permute-start | bytes 1572872 | tf_op jit(solution)/shard_map/ppermute | solution.py:514
  39.3 28.1 %all-to-all-start.2 = ((bf16[32,32,512]{2,1,0:T(8,128)(2,1)}), bf16[32,32,512]{2,1,0:T(8,128)(2,1)}, u32[]{:S(2)}, u32[]{:S(2)}) async-start(bf16[32,32,512]{2,1,0:T(8,128)(2,1)} %bitcast.22), calls=%async_computation.2 | async-start | bytes 2097152 | tf_op jit(solution)/shard_map/all_to_all | solution.py:545
  67.4 22.5 %all-to-all-start.1 = ((bf16[32,144,128]{2,1,0:T(8,128)(2,1)}), bf16[32,144,128]{2,1,0:T(8,128)(2,1)}, u32[]{:S(2)}, u32[]{:S(2)}) async-start(bf16[32,144,128]{2,1,0:T(8,128)(2,1)} %get-tuple-element.55), calls=%async_computation.1 | async-start | bytes 2359296 | tf_op jit(solution)/shard_map/all_to_all | solution.py:545
  89.9 15.8 %copy-start = (bf16[256,1024]{1,0:T(8,128)(2,1)S(1)}, bf16[256,1024]{1,0:T(8,128)(2,1)}, u32[]{:S(2)}) copy-start(bf16[256,1024]{1,0:T(8,128)(2,1)} %cand_ref.4) | copy-start | bytes 1572868
  89.9 15.8 %copy-start.1 = (bf16[1024,192]{0,1:T(8,128)(2,1)S(1)}, bf16[1024,192]{0,1:T(8,128)(2,1)}, u32[]{:S(2)}) copy-start(bf16[1024,192]{0,1:T(8,128)(2,1)} %param.21) | copy-start | bytes 1179652
  89.9 15.8 %copy-start.5 = (s32[256,2]{0,1:T(2,128)S(1)}, s32[256,2]{0,1:T(2,128)}, u32[]{:S(2)}) copy-start(s32[256,2]{0,1:T(2,128)} %param.22) | copy-start | bytes 6148
  89.9 23.1 %copy-start.6 = (s32[8,512]{1,0:T(8,128)S(1)}, s32[8,512]{1,0:T(8,128)}, u32[]{:S(2)}) copy-start(s32[8,512]{1,0:T(8,128)} %get-tuple-element.34.refs_11_.spot_ref) | copy-start | bytes 49156
  100.7 12.4 %all-to-all-start.3 = ((f32[32,2,128]{2,1,0:T(2,128)}), f32[32,2,128]{2,1,0:T(2,128)S(1)}, u32[]{:S(2)}, u32[]{:S(2)}) async-start(f32[32,2,128]{2,1,0:T(2,128)} %expert.1), calls=%async_computation.3 | async-start | bytes 65536 | tf_op jit(solution)/shard_map/all_to_all | solution.py:545
  105.7 1.0 copy-start.2
  106.7 0.9 copy-start.3
  107.6 0.9 copy-start.4

commit v6 on v5

--- a/solution.py
+++ b/solution.py
@@ -111,6 +111,10 @@
 
 def tower_kernel(down_at, tower_ref, out_ref, down, sems):
     count, tile, _ = down.shape
+    feature = tower_ref.shape[1]
+    weight = tower_ref[...].astype(F32)
+    weight = jnp.concatenate([weight, jnp.zeros((16 - weight.shape[0], feature), F32)], axis=0)
+    weight = weight.astype(BF16)
     loads = []
     for i in range(count):
         here = pl.ds(i * tile, tile)
@@ -121,7 +125,7 @@
         if i + 2 < count:
             loads[i + 2].start()
         loads[i].wait()
-        product = lax.dot_general(tower_ref[...], down[i], NT, preferred_element_type=F32)
+        product = lax.dot_general(weight, down[i], NT, preferred_element_type=F32)
         high = product.astype(BF16)
         low = (product - high.astype(F32)).astype(BF16)
         out_ref[:, pl.ds(i * tile, tile)] = jnp.concatenate([high[0:8], low[0:8]], axis=0)
@@ -613,8 +617,7 @@
     )
     stuff_in = exchange(stuff_out.reshape(experts, capacity, early))
 
-    tower_rows = jnp.pad(w_tower.T, ((0, 16 - tasks), (0, 0)))
-    tower_rows, _ = lax.optimization_barrier((tower_rows, cand_in))
+    tower_rows, _ = lax.optimization_barrier((w_tower.T, cand_in))
     towers = pl.pallas_call(
         tower_kernel,
         in_specs=[pl.BlockSpec(memory_space=pl.ANY), pl.BlockSpec(memory_space=pltpu.VMEM)],

time: 115 us -> 115 us (level)
    unnamed x18 -> x16, local copies, waits for them, and re-layouts: 2.82 us -> 2.82 us
  transfers between devices with their start and end apart: 10 -> 10, of which waited for: 3 -> 3; matrix products, arithmetic and copies ran while one was open for 1% -> 0% of each run, Pallas kernels for 38% -> 39%
where the time goes in v6:
time: 115 us; the launch traced here: 114 us
  Pallas kernels  59.5 us (52%)
  starting transfers between devices  38.9 us (34%)
  waiting for transfers between devices  12.5 us (11%)
  local copies, waits for them, and re-layouts  2.82 us (2%)
    all_to_all x4, starting transfers between devices, exchange(): return lax.all_to_all(item, 'exp', split_axis=0, concat_axis=0, tiled=True)  30.9 us
    pallas_call x1, Pallas kernels, local(): pl.pallas_call(early_kernel, in_specs=[anywhere] * 3, out_specs=[anywhere...  13.5 us
    all_to_all x4, waiting for transfers between devices, exchange(): return lax.all_to_all(item, 'exp', split_axis=0, concat_axis=0, tiled=True)  12.5 us
    pallas_call x2, Pallas kernels, attend(): pl.pallas_call(functools.partial(attend_kernel, chunk), in_specs=[smem] *...  12.4 us
    pallas_call x1, Pallas kernels, local(): pl.pallas_call(expert_kernel, in_specs=[anywhere] * 5, out_shape=jax.Shap...  10.7 us
    ppermute x6, starting transfers between devices, send(): return lax.ppermute(item, 'req', pairs)  8.09 us
    pallas_call x2, Pallas kernels, pack(): pl.pallas_call(functools.partial(pack_kernel, chunk), in_specs=[smem, sme...  7.07 us
    pallas_call x1, Pallas kernels, local(): pl.pallas_call(tower_kernel, in_specs=[pl.BlockSpec(memory_space=pl.ANY),...  6.6 us
  transfers between devices with their start and end apart: 10, of which 3 were waited for; matrix products, arithmetic and copies ran while one was open for 0% of the time, Pallas kernels for 39%

profile of v6, /device:TPU:1, one launch (start us, length us, event | category | flops | bytes accessed | tf_op | source)
XLA Modules:
  0.0 114.0 jit_solution(2124749064985225309)
XLA Ops:
  0.0 3.8 %pack.2 = (bf16[2064,128]{1,0:T(8,128)(2,1)}, bf16[2064,128]{1,0:T(8,128)(2,1)}, bf16[2064,128]{1,0:T(8,128)(2,1)}, bf16[16,128]{1,0:T(8,128)(2,1)}) custom-call(s32[1]{0:T(128)} %bitcast.1.me_ref, s32[8]{0:T(128)} %ids_ref.3, bf16[4,256,2048]{2,1,0:T(8,128)(2,1)} %bitcast.17), custom_call_target="tpu_custom_call" | custom-call | bytes 1000000 | tf_op jit(solution)/shard_map/pack/pallas_call | solution.py:502
  3.8 2.2 %collective-permute-start = (bf16[2064,128]{1,0:T(8,128)(2,1)}, bf16[2064,128]{1,0:T(8,128)(2,1)S(1)}, u32[]{:S(2)}, u32[]{:S(2)}) collective-permute-start(bf16[2064,128]{1,0:T(8,128)(2,1)} %get-tuple-element.38), channel_id=1, source_target_pairs={{0,32},{32,64},{64,96},{96,0},{1,33},{33,65},{65,97},{97,1},{2,34}... | collective-permute-start | bytes 1585160 | tf_op jit(solution)/shard_map/ppermute | solution.py:518
  6.0 1.5 %collective-permute-start.1 = (bf16[2064,128]{1,0:T(8,128)(2,1)}, bf16[2064,128]{1,0:T(8,128)(2,1)}, u32[]{:S(2)}, u32[]{:S(2)}) collective-permute-start(bf16[2064,128]{1,0:T(8,128)(2,1)} %get-tuple-element.39), channel_id=1, source_target_pairs={{0,96},{32,0},{64,32},{96,64},{1,97},{33,1},{65,33},{97,65},{2,98}... | collective-permute-start | bytes 1585160 | tf_op jit(solution)/shard_map/ppermute | solution.py:518
  7.6 1.6 %collective-permute-start.2 = (bf16[2064,128]{1,0:T(8,128)(2,1)}, bf16[2064,128]{1,0:T(8,128)(2,1)}, u32[]{:S(2)}, u32[]{:S(2)}) collective-permute-start(bf16[2064,128]{1,0:T(8,128)(2,1)} %get-tuple-element.40), channel_id=1, source_target_pairs={{0,64},{32,96},{64,0},{96,32},{1,65},{33,97},{65,1},{97,33},{2,66}... | collective-permute-start | bytes 1585160 | tf_op jit(solution)/shard_map/ppermute | solution.py:518
  9.1 2.6 %route.1 = (s32[8,512]{1,0:T(8,128)}, bf16[256,128]{1,0:T(8,128)(2,1)}, bf16[1024,512]{1,0:T(8,128)(2,1)}) custom-call(s32[2,256]{1,0:T(2,128)} %bitcast.14, s32[1,256]{1,0:T(1,128)} %bitcast.27, bf16[256,1024]{1,0:T(8,128)(2,1)} %cand_ref.4), custom_call_target="tpu_custom_call" | custom-call | flops 500000000 | bytes 3000000 | tf_op jit(solution)/shard_map/route/pallas_call | solution.py:529
  11.7 9.5 %all-to-all-start = ((bf16[32,32,512]{2,1,0:T(8,128)(2,1)}), bf16[32,32,512]{2,1,0:T(8,128)(2,1)}, u32[]{:S(2)}, u32[]{:S(2)}) async-start(bf16[32,32,512]{2,1,0:T(8,128)(2,1)} %bitcast.21), calls=%async_computation | async-start | bytes 2097152 | tf_op jit(solution)/shard_map/all_to_all | solution.py:549
  21.2 3.2 %pack.3 = (bf16[2048,128]{1,0:T(8,128)(2,1)}, bf16[2048,128]{1,0:T(8,128)(2,1)}, bf16[2048,128]{1,0:T(8,128)(2,1)}) custom-call(s32[1]{0:T(128)} %bitcast.1.me_ref, s32[8]{0:T(128)} %ids_ref.3, bf16[4,256,2048]{2,1,0:T(8,128)(2,1)} %bitcast.18), custom_call_target="tpu_custom_call" | custom-call | bytes 1000000 | tf_op jit(solution)/shard_map/pack/pallas_call | solution.py:502
  24.5 5.2 %project.1 = (bf16[256,1024]{1,0:T(8,128)(2,1)}, f32[256,1024]{1,0:T(8,128)}) custom-call(bf16[256,1024]{1,0:T(8,128)(2,1)} %cand_ref.4, bf16[1024,2048]{1,0:T(8,128)(2,1)} %weight_at.1, f32[1,1024]{1,0:T(1,128)} %bitcast.24), custom_call_target="tpu_custom_call" | custom-call | flops 1100000000 | bytes 6000000 | tf_op jit(solution)/shard_map/project/pallas_call | solution.py:556
  29.6 0.0 collective-permute-done.refs_2_.refs_5_
  29.7 0.0 copy-start.7
  29.7 0.5 collective-permute-start.3
  30.1 0.0 collective-permute-done.1.refs_3_.refs_6_
  30.1 2.3 %collective-permute-start.4 = (bf16[2048,128]{1,0:T(8,128)(2,1)}, bf16[2048,128]{1,0:T(8,128)(2,1)}, u32[]{:S(2)}, u32[]{:S(2)}) collective-permute-start(bf16[2048,128]{1,0:T(8,128)(2,1)} %get-tuple-element.46), channel_id=1, source_target_pairs={{0,96},{32,0},{64,32},{96,64},{1,97},{33,1},{65,33},{97,65},{2,98}... | collective-permute-start | bytes 1572872 | tf_op jit(solution)/shard_map/ppermute | solution.py:518
  32.4 0.0 collective-permute-done.2.refs_4_.refs_7_
  32.4 0.1 collective-permute-start.5
  32.5 0.0 copy-done.7
  32.5 6.1 %attend_first.1 = (bf16[1024,512]{1,0:T(8,128)(2,1)}, bf16[256,512]{1,0:T(8,128)(2,1)}, f32[256,128]{1,0:T(8,128)}) custom-call(s32[1]{0:T(128)} %bitcast.1.me_ref, s32[2]{0:T(128)} %hist_ref.3, f32[4,8]{1,0:T(4,128)} %bitcast.25, bf16[256,1024]{1,0:T(8,128)(2,1)} %get-tuple-element.37.refs_0_, bf16[4,256,2048]{2,1,0:T(8,128)(2,1)} %bitcast.19, ...), custom_call_target="tpu_custom_call" | custom-call | flops 30000001024 | bytes 1000000 | tf_op jit(solution)/shard_map/attend_first/pallas_call | solution.py:580
  38.6 0.0 all-to-all-done.cand_at
  38.6 11.5 %all-to-all-start.2 = ((bf16[32,32,512]{2,1,0:T(8,128)(2,1)}), bf16[32,32,512]{2,1,0:T(8,128)(2,1)}, u32[]{:S(2)}, u32[]{:S(2)}) async-start(bf16[32,32,512]{2,1,0:T(8,128)(2,1)} %bitcast.22), calls=%async_computation.2 | async-start | bytes 2097152 | tf_op jit(solution)/shard_map/all_to_all | solution.py:549
  50.0 6.6 %tower.1.tower_at = bf16[16,4096]{1,0:T(8,128)(2,1)} custom-call(bf16[1,4096,1024]{2,1,0:T(8,128)(2,1)} %down_at.1, bf16[6,1024]{1,0:T(8,128)(2,1)} %bitcast.23), custom_call_target="tpu_custom_call" | custom-call | flops 100000000 | bytes 9000000 | tf_op jit(solution)/shard_map/tower/pallas_call | solution.py:621
  56.7 0.0 collective-permute-done.3.refs_2_
  56.7 0.0 collective-permute-done.4.refs_3_
  56.7 0.0 collective-permute-done.5.refs_4_
  56.7 6.3 %attend_last.1 = (bf16[32,144,128]{2,1,0:T(8,128)(2,1)}, bf16[256,512]{1,0:T(8,128)(2,1)}, f32[256,128]{1,0:T(8,128)}) custom-call(s32[1]{0:T(128)} %bitcast.1.me_ref, s32[2]{0:T(128)} %hist_ref.3, f32[4,8]{1,0:T(4,128)} %bitcast.26, bf16[256,1024]{1,0:T(8,128)(2,1)} %get-tuple-element.37.refs_0_, bf16[4,256,2048]{2,1,0:T(8,128)(2,1)} %bitcast.20, ...), custom_call_target="tpu_custom_call" | custom-call | flops 99999997952 | bytes 1000000 | tf_op jit(solution)/shard_map/attend_last/pallas_call | solution.py:580
  63.0 4.3 %all-to-all-done.2.stuff_at = bf16[32,32,512]{2,1,0:T(8,128)(2,1)} async-done(((bf16[32,32,512]{2,1,0:T(8,128)(2,1)}), bf16[32,32,512]{2,1,0:T(8,128)(2,1)}, u32[]{:S(2)}, u32[]{:S(2)}) %all-to-all-start.2) | async-done | bytes 1048608 | tf_op jit(solution)/shard_map/all_to_all | solution.py:549
  67.3 4.8 %all-to-all-start.1 = ((bf16[32,144,128]{2,1,0:T(8,128)(2,1)}), bf16[32,144,128]{2,1,0:T(8,128)(2,1)}, u32[]{:S(2)}, u32[]{:S(2)}) async-start(bf16[32,144,128]{2,1,0:T(8,128)(2,1)} %get-tuple-element.55), calls=%async_computation.1 | async-start | bytes 2359296 | tf_op jit(solution)/shard_map/all_to_all | solution.py:549
  72.1 13.5 %early.1 = (bf16[4096,1024]{1,0:T(8,128)(2,1)}, bf16[4096,1024]{1,0:T(8,128)(2,1)}) custom-call(bf16[32,32,512]{2,1,0:T(8,128)(2,1)} %all-to-all-done.cand_at, bf16[32,32,512]{2,1,0:T(8,128)(2,1)} %all-to-all-done.2.stuff_at, bf16[1,1024,4096]{2,1,0:T(8,128)(2,1)} %up_at.3), custom_call_target="tpu_custom_call" | custom-call | flops 5000000000 | bytes 1000000 | tf_op jit(solution)/shard_map/early/pallas_call | solution.py:654
  85.6 4.2 %all-to-all-done.1.last_at = bf16[32,144,128]{2,1,0:T(8,128)(2,1)} async-done(((bf16[32,144,128]{2,1,0:T(8,128)(2,1)}), bf16[32,144,128]{2,1,0:T(8,128)(2,1)}, u32[]{:S(2)}, u32[]{:S(2)}) %all-to-all-start.1) | async-done | bytes 1179680 | tf_op jit(solution)/shard_map/all_to_all | solution.py:549
  89.8 0.0 copy-start
  89.8 0.0 copy-start.1
  89.8 0.0 copy-start.5
  89.8 0.0 copy-start.6
  89.8 10.7 %expert.1 = f32[32,2,128]{2,1,0:T(2,128)} custom-call(bf16[32,144,128]{2,1,0:T(8,128)(2,1)} %all-to-all-done.1.last_at, bf16[4096,1024]{1,0:T(8,128)(2,1)} %get-tuple-element.57.cand_product_at, bf16[4096,1024]{1,0:T(8,128)(2,1)} %get-tuple-element.58.stuff_product_at, bf16[1,1024,4096]{2,1,0:T(8,128)(2,1)} %up_at.3, bf16[16,4096]{1,0:T(8,128)(2,1)} %tower.1.tower_at), custom_call_target="tpu_custom_call" | custom-call | flops 6000000000 | bytes 25000000 | tf_op jit(solution)/shard_map/expert/pallas_call | solution.py:681
  100.5 5.1 %all-to-all-start.3 = ((f32[32,2,128]{2,1,0:T(2,128)}), f32[32,2,128]{2,1,0:T(2,128)S(1)}, u32[]{:S(2)}, u32[]{:S(2)}) async-start(f32[32,2,128]{2,1,0:T(2,128)} %expert.1), calls=%async_computation.3 | async-start | bytes 65536 | tf_op jit(solution)/shard_map/all_to_all | solution.py:549
  105.6 0.0 copy-done
  105.6 0.0 copy-done.1
  105.6 0.0 copy-done.5
  105.7 0.0 copy-start.2
  105.7 0.9 copy-done.2
  106.6 0.0 copy-start.3
  106.6 0.9 copy-done.3
  107.6 0.0 copy-start.4
  107.6 0.9 copy-done.4
  108.5 0.4 gate.1.gate_ref
  108.9 4.1 %all-to-all-done.3 = f32[32,2,128]{2,1,0:T(2,128)S(1)} async-done(((f32[32,2,128]{2,1,0:T(2,128)}), f32[32,2,128]{2,1,0:T(2,128)S(1)}, u32[]{:S(2)}, u32[]{:S(2)}) %all-to-all-start.3) | async-done | bytes 32800 | tf_op jit(solution)/shard_map/all_to_all | solution.py:549
  113.0 0.0 copy-done.6
  113.0 1.0 combine.1
Async XLA Ops:
  3.8 25.8 %collective-permute-start = (bf16[2064,128]{1,0:T(8,128)(2,1)}, bf16[2064,128]{1,0:T(8,128)(2,1)S(1)}, u32[]{:S(2)}, u32[]{:S(2)}) collective-permute-start(bf16[2064,128]{1,0:T(8,128)(2,1)} %get-tuple-element.38), channel_id=1, source_target_pairs={{0,32},{32,64},{64,96},{96,0},{1,33},{33,65},{65,97},{97,1},{2,34}... | collective-permute-start | bytes 1585160 | tf_op jit(solution)/shard_map/ppermute | solution.py:518
  6.0 24.1 %collective-permute-start.1 = (bf16[2064,128]{1,0:T(8,128)(2,1)}, bf16[2064,128]{1,0:T(8,128)(2,1)}, u32[]{:S(2)}, u32[]{:S(2)}) collective-permute-start(bf16[2064,128]{1,0:T(8,128)(2,1)} %get-tuple-element.39), channel_id=1, source_target_pairs={{0,96},{32,0},{64,32},{96,64},{1,97},{33,1},{65,33},{97,65},{2,98}... | collective-permute-start | bytes 1585160 | tf_op jit(solution)/shard_map/ppermute | solution.py:518
  7.6 24.8 %collective-permute-start.2 = (bf16[2064,128]{1,0:T(8,128)(2,1)}, bf16[2064,128]{1,0:T(8,128)(2,1)}, u32[]{:S(2)}, u32[]{:S(2)}) collective-permute-start(bf16[2064,128]{1,0:T(8,128)(2,1)} %get-tuple-element.40), channel_id=1, source_target_pairs={{0,64},{32,96},{64,0},{96,32},{1,65},{33,97},{65,1},{97,33},{2,66}... | collective-permute-start | bytes 1585160 | tf_op jit(solution)/shard_map/ppermute | solution.py:518
  11.7 26.9 %all-to-all-start = ((bf16[32,32,512]{2,1,0:T(8,128)(2,1)}), bf16[32,32,512]{2,1,0:T(8,128)(2,1)}, u32[]{:S(2)}, u32[]{:S(2)}) async-start(bf16[32,32,512]{2,1,0:T(8,128)(2,1)} %bitcast.21), calls=%async_computation | async-start | bytes 2097152 | tf_op jit(solution)/shard_map/all_to_all | solution.py:549
  29.7 2.8 %copy-start.7 = (bf16[2064,128]{1,0:T(8,128)(2,1)}, bf16[2064,128]{1,0:T(8,128)(2,1)S(1)}, u32[]{:S(2)}) copy-start(bf16[2064,128]{1,0:T(8,128)(2,1)S(1)} %collective-permute-done.refs_2_.refs_5_) | copy-start | bytes 1585156
  29.7 27.0 %collective-permute-start.3 = (bf16[2048,128]{1,0:T(8,128)(2,1)}, bf16[2048,128]{1,0:T(8,128)(2,1)}, u32[]{:S(2)}, u32[]{:S(2)}) collective-permute-start(bf16[2048,128]{1,0:T(8,128)(2,1)} %get-tuple-element.44), channel_id=1, source_target_pairs={{0,32},{32,64},{64,96},{96,0},{1,33},{33,65},{65,97},{97,1},{2,34}... | collective-permute-start | bytes 1572872 | tf_op jit(solution)/shard_map/ppermute | solution.py:518
  30.1 26.5 %collective-permute-start.4 = (bf16[2048,128]{1,0:T(8,128)(2,1)}, bf16[2048,128]{1,0:T(8,128)(2,1)}, u32[]{:S(2)}, u32[]{:S(2)}) collective-permute-start(bf16[2048,128]{1,0:T(8,128)(2,1)} %get-tuple-element.46), channel_id=1, source_target_pairs={{0,96},{32,0},{64,32},{96,64},{1,97},{33,1},{65,33},{97,65},{2,98}... | collective-permute-start | bytes 1572872 | tf_op jit(solution)/shard_map/ppermute | solution.py:518
  32.4 24.3 %collective-permute-start.5 = (bf16[2048,128]{1,0:T(8,128)(2,1)}, bf16[2048,128]{1,0:T(8,128)(2,1)}, u32[]{:S(2)}, u32[]{:S(2)}) collective-permute-start(bf16[2048,128]{1,0:T(8,128)(2,1)} %get-tuple-element.48), channel_id=1, source_target_pairs={{0,64},{32,96},{64,0},{96,32},{1,65},{33,97},{65,1},{97,33},{2,66}... | collective-permute-start | bytes 1572872 | tf_op jit(solution)/shard_map/ppermute | solution.py:518
  38.6 28.7 %all-to-all-start.2 = ((bf16[32,32,512]{2,1,0:T(8,128)(2,1)}), bf16[32,32,512]{2,1,0:T(8,128)(2,1)}, u32[]{:S(2)}, u32[]{:S(2)}) async-start(bf16[32,32,512]{2,1,0:T(8,128)(2,1)} %bitcast.22), calls=%async_computation.2 | async-start | bytes 2097152 | tf_op jit(solution)/shard_map/all_to_all | solution.py:549
  67.3 22.5 %all-to-all-start.1 = ((bf16[32,144,128]{2,1,0:T(8,128)(2,1)}), bf16[32,144,128]{2,1,0:T(8,128)(2,1)}, u32[]{:S(2)}, u32[]{:S(2)}) async-start(bf16[32,144,128]{2,1,0:T(8,128)(2,1)} %get-tuple-element.55), calls=%async_computation.1 | async-start | bytes 2359296 | tf_op jit(solution)/shard_map/all_to_all | solution.py:549
  89.8 15.8 %copy-start = (bf16[256,1024]{1,0:T(8,128)(2,1)S(1)}, bf16[256,1024]{1,0:T(8,128)(2,1)}, u32[]{:S(2)}) copy-start(bf16[256,1024]{1,0:T(8,128)(2,1)} %cand_ref.4) | copy-start | bytes 1572868
  89.8 15.8 %copy-start.1 = (bf16[1024,192]{0,1:T(8,128)(2,1)S(1)}, bf16[1024,192]{0,1:T(8,128)(2,1)}, u32[]{:S(2)}) copy-start(bf16[1024,192]{0,1:T(8,128)(2,1)} %param.21) | copy-start | bytes 1179652
  89.8 15.9 %copy-start.5 = (s32[256,2]{0,1:T(2,128)S(1)}, s32[256,2]{0,1:T(2,128)}, u32[]{:S(2)}) copy-start(s32[256,2]{0,1:T(2,128)} %param.22) | copy-start | bytes 6148
  89.8 23.2 %copy-start.6 = (s32[8,512]{1,0:T(8,128)S(1)}, s32[8,512]{1,0:T(8,128)}, u32[]{:S(2)}) copy-start(s32[8,512]{1,0:T(8,128)} %get-tuple-element.34.refs_11_.spot_ref) | copy-start | bytes 49156
  100.5 12.4 %all-to-all-start.3 = ((f32[32,2,128]{2,1,0:T(2,128)}), f32[32,2,128]{2,1,0:T(2,128)S(1)}, u32[]{:S(2)}, u32[]{:S(2)}) async-start(f32[32,2,128]{2,1,0:T(2,128)} %expert.1), calls=%async_computation.3 | async-start | bytes 65536 | tf_op jit(solution)/shard_map/all_to_all | solution.py:549
  105.7 1.0 copy-start.2
  106.6 0.9 copy-start.3
  107.6 0.9 copy-start.4
